TPU v7x, 256 devices: a whole 4x4x8 slice. The times are simulated.
256 devices in a mesh: pair: 8 (over x, core), sec: 32 (over z, y).
Axes of the slice: x: 4, y: 4, z: 8, core: 2. Of those that a mesh axis runs over, the one named last changes fastest.
Arguments:
- psi_blocks: bfloat16 [384, 128, 128], P('sec'), may hold values from -1 to 1
- sector_rows: int32 [384], P('sec'), may hold values from 16 to 128, as said below
- left_ops: bfloat16 [384, 128, 128], P('pair'), may hold values from -0.5 to 0.5
- connect: int32 [384, 384], P('pair', 'sec'), may hold values from 0 to 383
- tile_order: int32 [96], replicated, may hold values from 0 to 95, each once
Outputs:
- rdm_tiles: float32 [768, 64, 128], P(('pair', 'sec'))
Inputs may be any that keep to these rules, and one draw needn't show every extreme that they name: `sector_rows`: every value from 16 to 128; some sector has all 128 states live. `tile_order`: A permutation of the tiles of one group.
All inputs are finite; a program needn't handle non-finite values.
Results may differ from a plain program's by a relative error of at most 0.0029.
Values may be sent and summed in bfloat16 or wider, within the bound.
No kernel may reach another device: no remote copies, remote signals or barrier semaphores. Data moves between devices by JAX's collectives and lax.ppermute only.
A program may use at most 128 MiB of HBM per device.

v0:
```python
import jax
import jax.numpy as jnp
from jax import lax
from jax.sharding import PartitionSpec as P


def shifted(block, axis, distance):
    devices = range(lax.axis_size(axis))
    route = [((i - distance) % len(devices), i) for i in devices]
    return lax.ppermute(block, axis, route)


def per_device(psi_blocks, sector_rows, left_ops, connect, tile_order):
    block_dim = psi_blocks.shape[1]
    pair_ops = left_ops.shape[0]
    tile_count = 2 * pair_ops
    tile_height = block_dim // 2
    live_rows = jnp.arange(block_dim)[None, :, None] < sector_rows[:, None, None]
    psi_live = jnp.where(live_rows, psi_blocks, jnp.zeros_like(psi_blocks))
    gathered = lax.all_gather(psi_live, "sec", axis=0, tiled=True)
    halves = jnp.einsum(
        "sba,pbc->psac", psi_live, left_ops, preferred_element_type=jnp.float32
    ).astype(jnp.bfloat16)
    chosen = gathered[connect]
    density = jnp.einsum("psac,pscd->pad", halves, chosen, preferred_element_type=jnp.float32)
    density = density + shifted(density, "pair", 1)
    tile_rows = density.reshape(tile_count, tile_height, block_dim)[tile_order]
    return lax.psum_scatter(tile_rows, "sec", scatter_dimension=0, tiled=True)


def solution(mesh):
    in_specs = (P("sec", None, None), P("sec"), P("pair", None, None), P("pair", "sec"), P())
    out_specs = P(("pair", "sec"), None, None)
    return jax.shard_map(
        per_device, mesh=mesh, in_specs=in_specs, out_specs=out_specs, check_vma=False
    )
```

profile of v0, /device:TPU:32, one launch (start us, length us, event | category | flops | bytes accessed | tf_op | source)
XLA Modules:
  0.0 435.9 jit_solution(12258068648244348540)
XLA Ops:
  6.5 0.0 copy-start
  6.5 0.0 all-gather.2.cloned.1.call-start
  6.5 0.8 iota_compare_fusion
  7.4 2.0 broadcast_select_fusion
  9.4 0.0 all-gather.2.cloned.1.call-update
  9.4 0.0 reduce-scatter.2.cloned.1.call-start
  9.5 0.7 compare_select_fusion
  10.2 0.1 copy.8
  10.3 0.1 reshape.31
  10.4 0.0 copy-start.1
  10.4 120.1 %all-gather.2.cloned.1.call-done = bf16[384,128,128]{2,1,0:T(8,128)(2,1)} async-done(((bf16[12,128,128]{2,1,0:T(8,128)(2,1)}), bf16[384,128,128]{2,1,0:T(8,128)(2,1)}) %all-gather.2.cloned.1.call-update) | async-done | bytes 12582928 | tf_op jit(solution)/shard_map/all_gather | solution.py:20
  130.5 20.5 %gather_fusion = bf16[576,128,128]{2,1,0:T(8,128)(2,1)} fusion(bf16[384,128,128]{2,1,0:T(8,128)(2,1)} %all-gather.2.cloned.1.call-done, s32[1024]{0:T(1024)S(1)} %pad_clamp_fusion.1), kind=kCustom, calls=%fused_computation | custom fusion | bytes 37751040 | tf_op jit(solution)/shard_map/gather | solution.py:24
  151.0 0.0 copy-done
  151.0 0.0 copy-done.1
  151.0 0.0 copy-start.2
  151.0 15.2 %fusion.5 = f32[48,128,128]{2,1,0:T(8,128)} fusion(bf16[48,12,128,128]{3,2,1,0:T(8,128)(2,1)} %bitcast.21, bf16[48,128,128]{2,1,0:T(8,128)(2,1)S(1)} %copy-done, bf16[12,128,128]{2,1,0:T(8,128)(2,1)S(1)} %copy-done.1), kind=kOutput, calls=%fused_computation.6 | convolution fusion | flops 4841275392 | bytes 23986176 | tf_op jit(solution)/shard_map/psac,pscd->pad/dot_general | solution.py:25
  166.2 0.0 collective-permute-start
  166.2 0.0 copy-done.2
  166.3 38.1 %collective-permute-done = f32[48,128,128]{2,1,0:T(8,128)S(1)} collective-permute-done((f32[48,128,128]{2,1,0:T(8,128)}, f32[48,128,128]{2,1,0:T(8,128)S(1)}, u32[]{:S(2)}, u32[]{:S(2)}) %collective-permute-start) | collective-permute-done | bytes 3145760 | tf_op jit(solution)/shard_map/ppermute | solution.py:10
  204.4 4.2 add.19
  208.6 4.3 gather_fusion.1
  212.9 0.0 reduce-scatter.2.cloned.1.call-update
  212.9 216.2 %reduce-scatter.2.cloned.1.call-done = f32[3,64,128]{2,1,0:T(8,128)} async-done(((f32[96,64,128]{2,1,0:T(8,128)}), f32[3,64,128]{2,1,0:T(8,128)}) %reduce-scatter.2.cloned.1.call-update) | async-done | bytes 98320 | tf_op jit(solution)/shard_map/reduce_scatter | solution.py:28
  (3 shorter events, 0.0 us)
Async XLA Ops:
  6.5 144.5 %copy-start = (bf16[48,128,128]{2,1,0:T(8,128)(2,1)S(1)}, bf16[48,128,128]{2,1,0:T(8,128)(2,1)}, u32[]{:S(2)}) copy-start(bf16[48,128,128]{2,1,0:T(8,128)(2,1)} %param.7) | copy-start | bytes 4718596
  6.5 124.0 %all-gather.2.cloned.1.call-start = ((), (), s32[]{:S(2)}) async-start(), calls=%async_computation.1 | async-start | bytes 12976128 | tf_op jit(solution)/shard_map/all_gather | solution.py:20
  9.4 419.6 %reduce-scatter.2.cloned.1.call-start = ((), (), s32[]{:S(2)}) async-start(), calls=%async_computation.2 | async-start | bytes 3244032 | tf_op jit(solution)/shard_map/reduce_scatter | solution.py:28
  10.4 140.6 %copy-start.1 = (bf16[12,128,128]{2,1,0:T(8,128)(2,1)S(1)}, bf16[12,128,128]{2,1,0:T(8,128)(2,1)}, u32[]{:S(2)}) copy-start(bf16[12,128,128]{2,1,0:T(8,128)(2,1)} %broadcast_select_fusion) | copy-start | bytes 1179652
  151.0 15.2 %copy-start.2 = (s32[96]{0:T(128)S(1)}, s32[96]{0:T(128)}, u32[]{:S(2)}) copy-start(s32[96]{0:T(128)} %param.9) | copy-start | bytes 1156
  166.2 38.1 %collective-permute-start = (f32[48,128,128]{2,1,0:T(8,128)}, f32[48,128,128]{2,1,0:T(8,128)S(1)}, u32[]{:S(2)}, u32[]{:S(2)}) collective-permute-start(f32[48,128,128]{2,1,0:T(8,128)} %fusion.5), channel_id=1, source_target_pairs={{224,0},{0,32},{32,64},{64,96},{96,128},{128,160},{160,192},{192,2... | collective-permute-start | bytes 9437192 | tf_op jit(solution)/shard_map/ppermute | solution.py:10
Sparse Core Ops, SparseCore 0:
  9.9 120.5 all-gather.1
  213.0 216.0 reduce-scatter.1
where the time goes:
time: 437 us; the launch traced here: 436 us
  waiting for transfers between devices  374 us (86%)
  local copies, waits for them, and re-layouts  25 us (6%)
  matrix products  15.2 us (3%)
  between operations  13.4 us (3%)
  other arithmetic  7.83 us (2%)
    reduce_scatter x1, waiting for transfers between devices, per_device(): return lax.psum_scatter(tile_rows, 'sec', scatter_dimension=0, tiled=True)  216 us
    all_gather x1, waiting for transfers between devices, per_device(): gathered = lax.all_gather(psi_live, 'sec', axis=0, tiled=True)  120 us
    ppermute x1, waiting for transfers between devices, shifted(): return lax.ppermute(block, axis, route)  38.1 us
    gather x1, local copies, waits for them, and re-layouts, per_device(): chosen = gathered[connect]  20.5 us
    dot_general x1, matrix products, per_device(): jnp.einsum('psac,pscd->pad', halves, chosen, preferred_element_type=jnp.f...  15.2 us
  transfers between devices with their start and end apart: 3, of which 3 were waited for; matrix products, arithmetic and copies ran while one was open for 0% of the time, Pallas kernels for 0%

commit v1 on v0

v1 whole, which is shorter than its diff:
```python
import functools

import jax
import jax.numpy as jnp
import numpy as np
from jax import lax
from jax.experimental import pallas as pl
from jax.experimental.pallas import tpu as pltpu
from jax.sharding import PartitionSpec as P

NZ, NY = 8, 4
SLOTS = NZ * NY
SEC = 12
B = 128
ROWS = SEC * B
S1 = 4
N1, N2 = S1 * B, (SEC - S1) * B
NC = 32
TILES = 3
VMEM_LIMIT = 60 * 2**20
F32, BF16 = jnp.float32, jnp.bfloat16


def hop(v, dz, dy):
    route = []
    for pair in range(8):
        s = -1 if pair % 2 else 1
        for z in range(NZ):
            for y in range(NY):
                to = (z + s * dz) % NZ * NY + (y + s * dy) % NY
                route.append((pair * SLOTS + z * NY + y, pair * SLOTS + to))
    return lax.ppermute(v, ("pair", "sec"), route)


def zhop(v):
    return hop(v, 1, 0)


def yhop(v):
    return hop(v, 0, 1)


def swap(v):
    return lax.ppermute(v, "pair", [(i, i ^ 1) for i in range(lax.axis_size("pair"))])


def part(v, core, axis=0):
    n = v.shape[axis] // 2
    return lax.dynamic_slice_in_dim(v, core * n, n, axis)


YS = (0, 1, 2, -1)


def sync(*arrays):
    return lax.optimization_barrier(arrays)


def gather_pieces(first, second, core, *others):
    n, h2 = first.shape[0], N2 // 2
    w1, near, far = zhop(second), yhop(first), hop(part(first, core), 0, 2)
    w1, near, far, *others = sync(w1, near, far, *others)

    w2, other, w1s = zhop(w1), swap(jnp.concatenate([near, far])), swap(w1)
    w2, other, w1s = sync(w2, other, w1s)

    near_s, far_s = other[:n], other[n:]
    far = jnp.where(core == 0, jnp.concatenate([far, far_s]), jnp.concatenate([far_s, far]))
    bundle = jnp.stack([first, near, far, near_s])
    own = jnp.where(core == 0, second, jnp.concatenate([second[h2:], second[:h2]]))
    a = jnp.concatenate([w1, own, w1s])
    bundle, a, w2 = sync(bundle, a, w2)
    w3, w4, z1, a1, w2s = zhop(w2), hop(part(w2, core), 2, 0), zhop(bundle), yhop(a), swap(w2)
    w3, w4, z1, a1, w2s = sync(w3, w4, z1, a1, w2s)

    ha = a.shape[0] // 2
    b = jnp.concatenate([w2, w2s])
    wc = jnp.concatenate([w3, w4])
    z2, a2, b1, wcs, a1s = zhop(z1), yhop(a1[:ha]), yhop(b), swap(wc), swap(a1)
    z2, a2, b1, wcs, a1s, wc = sync(z2, a2, b1, wcs, a1s, wc)

    c = jnp.concatenate([wc, wcs])
    hb, hc = b.shape[0] // 2, c.shape[0] // 2
    z3, c1, b2, z1s, a2s = zhop(z2), yhop(c), yhop(b1[:hb]), swap(z1), swap(a2)
    z3, c1, b2, z1s, a2s = sync(z3, c1, b2, z1s, a2s)

    z4, c2 = zhop(lax.dynamic_slice_in_dim(z3, core, 2, 0)), yhop(c1[:hc])
    z2s, b1s, c1s = swap(z2), swap(b1), swap(c1)
    z4, c2, z2s, b1s, c1s = sync(z4, c2, z2s, b1s, c1s)
    z3s, b2s, z4s, c2s = swap(z3), swap(b2), swap(z4), swap(c2)

    def step(dz):
        return [(i, dz, dy, 0) for i, dy in enumerate(YS)]

    def shift(seg, dy, stop):
        return [(r, m, dz, dy, o, e) for r, m, dz, _, o, e in seg if r < stop]

    a_seg = [(0, N2, 1, 0, 0, 0), (N2, h2, 0, 0, 0, h2), (N2 + h2, h2, 0, 0, h2, -h2),
             (2 * N2, N2, -1, 0, 0, 0)]
    b_seg = [(0, N2, 2, 0, 0, 0), (N2, N2, -2, 0, 0, 0)]
    c_seg = [(0, N2, 3, 0, 0, 0), (N2, h2, 4, 0, 0, h2), (hc, N2, -3, 0, 0, 0),
             (hc + N2, h2, 4, 0, h2, -h2)]
    corner = [(0, 4, 0, 1), (1, 4, 1, 1)]
    couples = [
        (2, c1, c1s, shift(c_seg, 1, 2 * hc)), (1, z3, z3s, step(3)), (2, b2, b2s, shift(b_seg, 2, hb)),
        (2, c2, c2s, shift(c_seg, 2, hc)), (1, z4, z4s, corner),
        (1, bundle, None, step(0)), (2, a, None, a_seg), (2, a1, a1s, shift(a_seg, 1, 2 * ha)),
        (1, z1, z1s, step(1)), (2, b, None, b_seg), (2, c, None, c_seg),
        (2, a2, a2s, shift(a_seg, 2, ha)), (2, b1, b1s, shift(b_seg, 1, 2 * hb)), (1, z2, z2s, step(2)),
    ]
    return couples, others


def place(seg, stream, core, swapped):
    who = 1 - core if swapped else core
    sign = 2 * who - 1
    if stream == 1:
        i, dz, dy, special = seg
        return dz * sign, (1 + i if who else -i) if special else dy * sign, 0, N1
    r, rows, dz, dy, o, more = seg
    return dz * sign, dy * sign, N1 + o + more * who, rows


def sectors(seg, stream, core, swapped):
    dz, dy, row, rows = place(seg, stream, core, swapped)
    return [(dz % NZ, dy % NY, row // B + q) for q in range(rows // B)]


def couple_order(couple, core):
    stream, _, v, segments = couple
    left = [t for seg in segments for t in sectors(seg, stream, core, False)]
    if v is None:
        half = len(left) // 2
        return list(zip(left[:half], left[half:]))
    return list(zip(left, [t for seg in segments for t in sectors(seg, stream, core, True)]))


def arrays_of(couples):
    return [(w, seg, st, swapped) for st, u, v, seg in couples
            for w, swapped in ((u, False), (v, True)) if w is not None]


def orders(couples):
    slots, pairs = [], []
    for core in (0, 1):
        rows = [place(t, 1, core, swapped)[:2] for _, seg, st, swapped in arrays_of(couples) if st == 1
                for t in seg]
        slots.append([(dz % NZ, dy % NY) for dz, dy in rows])
        pairs.append([p for couple in couples for p in couple_order(couple, core)])
    return slots, pairs


def couple_spec(couple):
    stream, u, v, _ = couple
    rows = u.shape[0] * N1 if stream == 1 else u.shape[0]
    count = rows // B // (2 if v is None else 1)
    return count, next(n for n in (12, 16, 8) if count % n == 0)


def prepare_kernel(rows, psi, here, there, first, second):
    core = lax.rem(lax.axis_index("pair"), 2)
    row = lax.broadcasted_iota(jnp.int32, (B, B), 0)
    for s in range(SEC):
        live = jnp.where(row < rows[s], psi[s], jnp.zeros((B, B), BF16))
        if s < S1:
            first[pl.ds(s * B, B), :] = live
        else:
            second[pl.ds((s - S1) * B, B), :] = live
    pairs = here.shape[0]
    lane = lax.broadcasted_iota(jnp.int32, (pairs, B), 1)
    pair = lax.broadcasted_iota(jnp.int32, (pairs, B), 0)
    high = jnp.where(lane == pair, 1.0, 0.0).astype(BF16)
    low = jnp.where(lane == pair + B // 2, 1.0, 0.0).astype(BF16)

    def words(ref):
        v = ref[...]
        contract = (((0,), (0,)), ((), ()))
        up = (v // 16).astype(F32).astype(BF16)
        down = (v % 16).astype(F32).astype(BF16)
        return (lax.dot_general(up, high, contract, preferred_element_type=F32)
                + lax.dot_general(down, low, contract, preferred_element_type=F32)).astype(BF16)

    mine, other = words(here), words(there)
    zero = jnp.zeros((16 - SEC, B), BF16)
    even = jnp.where(core == 0, mine, other)
    odd = jnp.where(core == 0, other, mine)
    first[pl.ds(N1, NC), :] = jnp.concatenate([even, zero, odd, zero], axis=0)


def tiles_kernel(specs, plan, meta, *refs):
    n = len(plan)
    pieces, ops, pick, out = refs[:n], *refs[n:n + 3]
    psi, halves, turned, words, table, conn, weights, sems, csem, osem = refs[n + 3:]
    core, zpos, ypos = meta[TILES], meta[TILES + 1], meta[TILES + 2]
    pairs = SLOTS * SEC // 2
    targets, places = TILES + 3, TILES + 3 + 2 * pairs

    for k in range(TILES):
        pltpu.make_async_copy(ops.at[meta[k] // 2], weights.at[k], osem).start()
    start = 0
    for ref, (segments, stream, swapped, couple) in zip(pieces, plan):
        if stream == 1:
            at = pl.ds(pl.multiple_of(N1 + core * 16, 16), 16)
            size = len(segments)
            pltpu.make_async_copy(ref.at[:, at], words.at[pl.ds(start, size)], csem).start()
            start += size
    for ref, (segments, stream, swapped, couple) in zip(pieces, plan):
        at_core = [[place(seg, stream, c, swapped) for seg in segments] for c in (0, 1)]
        for seg, (dz0, dy0, row0, rows), (dz1, dy1, row1, _) in zip(segments, *at_core):
            dz, dy = jnp.where(core == 0, dz0, dz1), jnp.where(core == 0, dy0, dy1)
            slot = lax.rem(zpos + dz + NZ, NZ) * NY + lax.rem(ypos + dy + NY, NY)
            row = slot * ROWS + jnp.where(core == 0, row0, row1)
            src = ref.at[seg[0], pl.ds(0, N1)] if stream == 1 else ref.at[pl.ds(seg[0], rows)]
            dst = psi.at[pl.ds(pl.multiple_of(row, B), rows)]
            pltpu.make_async_copy(src, dst, sems.at[couple]).start()
    pltpu.make_async_copy(ops.at[pl.ds(0, TILES)], weights, osem).wait()

    def sector(s):
        return psi[pl.ds(pl.multiple_of(s * B, B), B), :]

    base = 0
    for couple, (count, batch) in enumerate(specs):
        rows = psi.at[pl.ds(0, 2 * count * B)]
        pltpu.make_async_copy(rows, rows, sems.at[couple]).wait()

        def some(j, carry, batch=batch, base=base):
            for q in range(batch):
                for e in range(2):
                    t = sector(meta[places + 2 * (base + j * batch + q) + e]).T
                    for k in range(TILES):
                        low = lax.rem(meta[k], 2) == 0
                        turned[k, q, :, pl.ds(e * B, B)] = jnp.where(low, t[:64], t[64:])
            for k in range(TILES):
                for e in range(2):
                    rows = turned[k, pl.ds(0, batch), :, pl.ds(e * B, B)].reshape(batch * 64, B)
                    r = jnp.dot(rows, weights[k], preferred_element_type=F32).astype(BF16)
                    to = pl.ds(base + j * batch, batch)
                    halves[k, to, :, pl.ds(e * B, B)] = r.reshape(batch, 64, B)
            return carry

        lax.fori_loop(0, count // batch, some, 0)
        base += count
        if couple == 4:
            pltpu.make_async_copy(words, words, csem).wait()
            values = lax.dot_general(pick[...], words[...].reshape(SLOTS * 16, B), (((1,), (1,)), ((), ())),
            preferred_element_type=F32)
            table[...] = values.astype(jnp.int32)
            pltpu.make_async_copy(table, conn, csem).start()
    pltpu.make_async_copy(table, conn, csem).wait()

    unroll = 12

    def second_stage(j, sums):
        sums = list(sums)
        for u in range(unroll):
            at = j * unroll + u
            for k in range(TILES):
                left, right = (conn[k, meta[targets + 2 * at + e]] for e in (0, 1))
                rhs = jnp.concatenate([sector(left), sector(right)], axis=0)
                sums[k] = sums[k] + jnp.dot(halves[k, at], rhs, preferred_element_type=F32)
        return tuple(sums)

    sums = lax.fori_loop(0, pairs // unroll, second_stage, (jnp.zeros((64, B), F32),) * TILES)
    for k in range(TILES):
        out[k] = sums[k]


def tables():
    shapes = []

    def trace(first, second):
        couples, _ = gather_pieces(first, second, jnp.int32(0))
        shapes.extend(couples)
        return first

    jax.eval_shape(
        trace, jax.ShapeDtypeStruct((N1 + NC, B), BF16), jax.ShapeDtypeStruct((N2, B), BF16))
    slots, pairs = orders(shapes)
    index, places = [], []
    for c in (0, 1):
        number = {at: o for o, at in enumerate(slots[c])}
        flat = [t for p in pairs[c] for t in p]
        index.append([number[t[:2]] * 16 + t[2] for t in flat])
        places.append(flat)
    return np.array(index, np.int32), np.array(places, np.int32)


def per_device(psi_blocks, sector_rows, left_ops, connect, tile_order):
    sec, pair = lax.axis_index("sec"), lax.axis_index("pair")
    zpos, ypos, core = sec // NY, sec % NY, pair % 2
    vmem = pl.BlockSpec(memory_space=pltpu.VMEM)
    first, second = pl.pallas_call(
        prepare_kernel,
        out_shape=(jax.ShapeDtypeStruct((N1 + NC, B), BF16), jax.ShapeDtypeStruct((N2, B), BF16)),
        grid_spec=pltpu.PrefetchScalarGridSpec(
            num_scalar_prefetch=1, grid=(), in_specs=[vmem] * 3, out_specs=[vmem] * 2,
        ),
    )(sector_rows, psi_blocks, connect, swap(connect))

    mytiles = lax.dynamic_slice_in_dim(tile_order, sec * TILES, TILES)
    lane = jnp.arange(B)[None, :]
    mypairs = jnp.pad(mytiles // 2, (0, 16 - TILES))[:, None]
    pick = jnp.where(lane == mypairs, 16.0, 0.0) + jnp.where(lane == B // 2 + mypairs, 1.0, 0.0)
    pick = pick.astype(BF16)

    index, places = tables()
    index = jnp.asarray(index)[core]
    places = jnp.asarray(places)[core]
    places = ((zpos + places[:, 0]) % NZ * NY + (ypos + places[:, 1]) % NY) * SEC + places[:, 2]
    meta = jnp.concatenate([mytiles, jnp.stack([core, zpos, ypos]), index, places]).astype(jnp.int32)
    couples, (meta, pick) = gather_pieces(first, second, core, meta, pick)

    arrays = arrays_of(couples)
    plan = [(seg, st, swapped, number) for number, couple in enumerate(couples)
            for _, seg, st, swapped in arrays_of([couple])]
    hbm = pl.BlockSpec(memory_space=pl.ANY)
    tiles = pl.pallas_call(
        functools.partial(tiles_kernel, [couple_spec(couple) for couple in couples], plan),
        out_shape=jax.ShapeDtypeStruct((TILES, 64, B), F32),
        grid_spec=pltpu.PrefetchScalarGridSpec(
            num_scalar_prefetch=1,
            grid=(),
            in_specs=[hbm] * (len(plan) + 1) + [vmem],
            out_specs=vmem,
            scratch_shapes=[
                pltpu.VMEM((SLOTS * ROWS, B), BF16),
                pltpu.VMEM((TILES, SLOTS * SEC // 2, 64, 2 * B), BF16),
                pltpu.VMEM((TILES, 16, 64, 2 * B), BF16),
                pltpu.VMEM((SLOTS, 16, B), BF16),
                pltpu.VMEM((16, SLOTS * 16), jnp.int32),
                pltpu.SMEM((16, SLOTS * 16), jnp.int32),
                pltpu.VMEM((TILES, B, B), BF16),
                pltpu.SemaphoreType.DMA((len(couples),)),
                pltpu.SemaphoreType.DMA,
                pltpu.SemaphoreType.DMA,
            ],
        ),
        compiler_params=pltpu.CompilerParams(vmem_limit_bytes=VMEM_LIMIT),
    )(meta, *[w for w, _, _, _ in arrays], left_ops, pick)
    ring = [((i - 1) % 8, i) for i in range(8)]
    return tiles + lax.ppermute(tiles, "pair", ring)


def solution(mesh):
    in_specs = (P("sec", None, None), P("sec"), P("pair", None, None), P("pair", "sec"), P())
    out_specs = P(("pair", "sec"), None, None)
    return jax.shard_map(
        per_device, mesh=mesh, in_specs=in_specs, out_specs=out_specs, check_vma=False
    )
```

time: 437 us -> 128 us (0.29)
  waiting for transfers between devices: 374 us -> 56.8 us
  Pallas kernels: 0 us -> 28.9 us
  starting transfers between devices: 0.05 us -> 25.9 us
  matrix products: 15.2 us -> 0 us
  local copies, waits for them, and re-layouts: 25 us -> 11 us
  between operations: 13.4 us -> 0.52 us
    reduce_scatter x1 -> x0, waiting for transfers between devices: 216 us -> none  [per_device(): return lax.psum_scatter(tile_rows, 'sec', scatter_dimension=0, tiled=True)]
    all_gather x1 -> x0, waiting for transfers between devices: 120 us -> none  [per_device(): gathered = lax.all_gather(psi_live, 'sec', axis=0, tiled=True)]
    pallas_call x0 -> x2, Pallas kernels: none -> 28.9 us  [the longest x1 26.3 us: per_device(): pl.pallas_call(functools.partial(tiles_kernel, [couple_spec(couple) for c...]
    ppermute x1 -> x32, starting transfers between devices: 0.01 us -> 25.9 us  [the longest x16 18.4 us: hop(): return lax.ppermute(v, ('pair', 'sec'), route)]
    gather x2 -> x0, local copies, waits for them, and re-layouts: 24.8 us -> none  [the longest x1 20.5 us: per_device(): chosen = gathered[connect]]
    ppermute x1 -> x32, waiting for transfers between devices: 38.1 us -> 56.8 us  [the longest x16 44.9 us: hop(): return lax.ppermute(v, ('pair', 'sec'), route)]
    dot_general x1 -> x0, matrix products: 15.2 us -> none  [per_device(): jnp.einsum('psac,pscd->pad', halves, chosen, preferred_element_type=jnp.f...]
    unnamed x6 -> x56, local copies, waits for them, and re-layouts: 0.01 us -> 5.67 us
  transfers between devices with their start and end apart: 3 -> 32, of which waited for: 3 -> 13; matrix products, arithmetic and copies ran while one was open for 0% -> 7% of each run, Pallas kernels for 0% -> 0%
where the time goes in v1:
time: 128 us; the launch traced here: 127 us
  waiting for transfers between devices  56.8 us (44%)
  Pallas kernels  28.9 us (23%)
  starting transfers between devices  25.9 us (20%)
  local copies, waits for them, and re-layouts  11 us (9%)
  other arithmetic  4.21 us (3%)
    ppermute x16, waiting for transfers between devices, hop(): return lax.ppermute(v, ('pair', 'sec'), route)  44.9 us
    pallas_call x1, Pallas kernels, per_device(): pl.pallas_call(functools.partial(tiles_kernel, [couple_spec(couple) for c...  26.3 us
    ppermute x16, starting transfers between devices, hop(): return lax.ppermute(v, ('pair', 'sec'), route)  18.4 us
    ppermute x15, starting transfers between devices, swap(): lax.ppermute(v, 'pair', [(i, i ^ 1) for i in range(lax.axis_size('pair'))])  7.35 us
    ppermute x15, waiting for transfers between devices, swap(): lax.ppermute(v, 'pair', [(i, i ^ 1) for i in range(lax.axis_size('pair'))])  6.51 us
    unnamed x56, local copies, waits for them, and re-layouts  5.67 us
    ppermute x1, waiting for transfers between devices, per_device(): return tiles + lax.ppermute(tiles, 'pair', ring)  5.32 us
    pallas_call x1, Pallas kernels, per_device(): pl.pallas_call(prepare_kernel, out_shape=(jax.ShapeDtypeStruct((N1 + NC,...  2.61 us
  transfers between devices with their start and end apart: 32, of which 13 were waited for; matrix products, arithmetic and copies ran while one was open for 7% of the time, Pallas kernels for 0%

profile of v1, /device:TPU:32, one launch (start us, length us, event | category | flops | bytes accessed | tf_op | source)
XLA Modules:
  0.0 127.3 jit_solution(14329173462500695868)
XLA Ops:
  0.0 0.8 copy.11.here
  0.9 0.7 and_select_fusion
  1.7 0.7 dynamic-slice_bitcast_fusion
  2.4 0.7 add_convert_fusion.refs_25_
  3.1 0.7 dynamic-slice_reduce_fusion
  3.8 0.7 concatenate.45.meta
  4.5 0.6 copy-done.25
  5.1 2.6 %shard_map.73 = (bf16[544,128]{1,0:T(8,128)(2,1)}, bf16[1024,128]{1,0:T(8,128)(2,1)}) custom-call(s32[12]{0:T(128)} %rows.1, bf16[12,128,128]{2,1,0:T(8,128)(2,1)} %psi.1, s32[48,12]{1,0:T(8,128)} %copy-done.24, s32[48,12]{1,0:T(8,128)} %copy-done.25), custom_call_target="tpu_custom_call" | custom-call | tf_op jit(solution)/shard_map/pallas_call | solution.py:292
  7.7 1.6 %collective-permute-start.2 = (bf16[544,128]{1,0:T(8,128)(2,1)}, bf16[544,128]{1,0:T(8,128)(2,1)S(1)}, u32[]{:S(2)}, u32[]{:S(2)}) collective-permute-start(bf16[544,128]{1,0:T(8,128)(2,1)} %get-tuple-element.40), channel_id=1, source_target_pairs={{0,1},{1,2},{2,3},{3,0},{4,5},{5,6},{6,7},{7,4},{8,9},{9,10},{10,1... | collective-permute-start | bytes 417800 | tf_op jit(solution)/shard_map/ppermute | solution.py:32
  9.3 1.9 %collective-permute-start.1 = (bf16[1024,128]{1,0:T(8,128)(2,1)}, bf16[1024,128]{1,0:T(8,128)(2,1)S(1)}, u32[]{:S(2)}, u32[]{:S(2)}) collective-permute-start(bf16[1024,128]{1,0:T(8,128)(2,1)} %get-tuple-element.39), channel_id=1, source_target_pairs={{0,4},{1,5},{2,6},{3,7},{4,8},{5,9},{6,10},{7,11},{8,12},{9,13},{1... | collective-permute-start | bytes 786440 | tf_op jit(solution)/shard_map/ppermute | solution.py:32
  11.2 0.9 constant_dynamic-slice_fusion.2
  12.1 2.9 %collective-permute-start.3 = (bf16[272,128]{1,0:T(8,128)(2,1)S(1)}, bf16[272,128]{1,0:T(8,128)(2,1)S(1)}, u32[]{:S(2)}, u32[]{:S(2)}) collective-permute-start(bf16[272,128]{1,0:T(8,128)(2,1)S(1)} %constant_dynamic-slice_fusion.2), channel_id=1, source_target_pairs={{0,2},{1,3},{2,0},{3,1},{4,6},{5,7},{6,4},{7,5},{8,10},{9,11},{10,... | collective-permute-start | bytes 208904 | tf_op jit(solution)/shard_map/ppermute | solution.py:32
  15.0 1.0 fusion.8
  15.9 1.9 %collective-permute-done.3 = bf16[272,128]{1,0:T(8,128)(2,1)S(1)} collective-permute-done((bf16[272,128]{1,0:T(8,128)(2,1)S(1)}, bf16[272,128]{1,0:T(8,128)(2,1)S(1)}, u32[]{:S(2)}, u32[]{:S(2)}) %collective-permute-start.3) | collective-permute-done | bytes 69664 | tf_op jit(solution)/shard_map/ppermute | solution.py:32
  17.9 2.0 %collective-permute-start.4 = (bf16[1024,128]{1,0:T(8,128)(2,1)S(1)}, bf16[1024,128]{1,0:T(8,128)(2,1)S(1)}, u32[]{:S(2)}, u32[]{:S(2)}) collective-permute-start(bf16[1024,128]{1,0:T(8,128)(2,1)S(1)} %collective-permute-done.1), channel_id=1, source_target_pairs={{0,4},{1,5},{2,6},{3,7},{4,8},{5,9},{6,10},{7,11},{8,12},{9,13},{1... | collective-permute-start | bytes 786440 | tf_op jit(solution)/shard_map/ppermute | solution.py:32
  19.9 2.1 %collective-permute-start.5 = (bf16[816,128]{1,0:T(8,128)(2,1)S(1)}, bf16[816,128]{1,0:T(8,128)(2,1)S(1)}, u32[]{:S(2)}, u32[]{:S(2)}) collective-permute-start(bf16[816,128]{1,0:T(8,128)(2,1)S(1)} %pad_maximum_fusion.2), channel_id=1, source_target_pairs={{0,32},{32,0},{64,96},{96,64},{128,160},{160,128},{192,224},{224,1... | collective-permute-start | bytes 626696 | tf_op jit(solution)/shard_map/ppermute | solution.py:44
  22.0 1.0 maximum_select_fusion
  23.1 3.3 %collective-permute-done.4 = bf16[1024,128]{1,0:T(8,128)(2,1)S(1)} collective-permute-done((bf16[1024,128]{1,0:T(8,128)(2,1)S(1)}, bf16[1024,128]{1,0:T(8,128)(2,1)S(1)}, u32[]{:S(2)}, u32[]{:S(2)}) %collective-permute-start.4) | collective-permute-done | bytes 262176 | tf_op jit(solution)/shard_map/ppermute | solution.py:32
  26.8 2.0 %collective-permute-start.9 = (bf16[4,544,128]{2,1,0:T(8,128)(2,1)S(1)}, bf16[4,544,128]{2,1,0:T(8,128)(2,1)S(1)}, u32[]{:S(2)}, u32[]{:S(2)}) collective-permute-start(bf16[4,544,128]{2,1,0:T(8,128)(2,1)S(1)} %pad_maximum_fusion.1.refs_10_), channel_id=1, source_target_pairs={{0,4},{1,5},{2,6},{3,7},{4,8},{5,9},{6,10},{7,11},{8,12},{9,13},{1... | collective-permute-start | bytes 1671176 | tf_op jit(solution)/shard_map/ppermute | solution.py:32
  28.8 2.5 %collective-permute-start.7 = (bf16[1024,128]{1,0:T(8,128)(2,1)S(1)}, bf16[1024,128]{1,0:T(8,128)(2,1)S(1)}, u32[]{:S(2)}, u32[]{:S(2)}) collective-permute-start(bf16[1024,128]{1,0:T(8,128)(2,1)S(1)} %collective-permute-done.4), channel_id=1, source_target_pairs={{0,4},{1,5},{2,6},{3,7},{4,8},{5,9},{6,10},{7,11},{8,12},{9,13},{1... | collective-permute-start | bytes 786440 | tf_op jit(solution)/shard_map/ppermute | solution.py:32
  31.3 2.8 %collective-permute-start.8 = (bf16[512,128]{1,0:T(8,128)(2,1)S(1)}, bf16[512,128]{1,0:T(8,128)(2,1)S(1)}, u32[]{:S(2)}, u32[]{:S(2)}) collective-permute-start(bf16[512,128]{1,0:T(8,128)(2,1)S(1)} %constant_dynamic-slice_fusion.1), channel_id=1, source_target_pairs={{0,8},{1,9},{2,10},{3,11},{4,12},{5,13},{6,14},{7,15},{8,16},{9,17... | collective-permute-start | bytes 393224 | tf_op jit(solution)/shard_map/ppermute | solution.py:32
  34.0 11.9 %collective-permute-done.8 = bf16[512,128]{1,0:T(8,128)(2,1)S(1)} collective-permute-done((bf16[512,128]{1,0:T(8,128)(2,1)S(1)}, bf16[512,128]{1,0:T(8,128)(2,1)S(1)}, u32[]{:S(2)}, u32[]{:S(2)}) %collective-permute-start.8) | collective-permute-done | bytes 131104 | tf_op jit(solution)/shard_map/ppermute | solution.py:32
  46.0 0.8 copy-done.10
  46.8 1.2 constant_dynamic-update-slice_fusion.refs_16_
  48.0 0.6 collective-permute-start.14
  48.7 1.0 constant_dynamic-update-slice_fusion.3
  49.7 1.6 %collective-permute-start.13 = (bf16[1536,128]{1,0:T(8,128)(2,1)S(1)}, bf16[1536,128]{1,0:T(8,128)(2,1)S(1)}, u32[]{:S(2)}, u32[]{:S(2)}) collective-permute-start(bf16[1536,128]{1,0:T(8,128)(2,1)S(1)} %slice.37), channel_id=1, source_target_pairs={{0,1},{1,2},{2,3},{3,0},{4,5},{5,6},{6,7},{7,4},{8,9},{9,10},{10,1... | collective-permute-start | bytes 1179656 | tf_op jit(solution)/shard_map/ppermute | solution.py:32
  51.3 1.6 %collective-permute-start.15 = (bf16[1536,128]{1,0:T(8,128)(2,1)S(1)}, bf16[1536,128]{1,0:T(8,128)(2,1)S(1)}, u32[]{:S(2)}, u32[]{:S(2)}) collective-permute-start(bf16[1536,128]{1,0:T(8,128)(2,1)S(1)} %constant_dynamic-update-slice_fusion.2), channel_id=1, source_target_pairs={{0,32},{32,0},{64,96},{96,64},{128,160},{160,128},{192,224},{224,1... | collective-permute-start | bytes 1179656 | tf_op jit(solution)/shard_map/ppermute | solution.py:44
  52.9 9.8 %collective-permute-done.13.refs_18_ = bf16[1536,128]{1,0:T(8,128)(2,1)S(1)} collective-permute-done((bf16[1536,128]{1,0:T(8,128)(2,1)S(1)}, bf16[1536,128]{1,0:T(8,128)(2,1)S(1)}, u32[]{:S(2)}, u32[]{:S(2)}) %collective-permute-start.13) | collective-permute-done | bytes 393248 | tf_op jit(solution)/shard_map/ppermute | solution.py:32
  63.0 2.0 %collective-permute-start.20 = (bf16[4,544,128]{2,1,0:T(8,128)(2,1)S(1)}, bf16[4,544,128]{2,1,0:T(8,128)(2,1)S(1)}, u32[]{:S(2)}, u32[]{:S(2)}) collective-permute-start(bf16[4,544,128]{2,1,0:T(8,128)(2,1)S(1)} %copy-done.11), channel_id=1, source_target_pairs={{0,32},{32,0},{64,96},{96,64},{128,160},{160,128},{192,224},{224,1... | collective-permute-start | bytes 1671176 | tf_op jit(solution)/shard_map/ppermute | solution.py:44
  65.2 1.4 %collective-permute-done.20.refs_15_ = bf16[4,544,128]{2,1,0:T(8,128)(2,1)S(1)} collective-permute-done((bf16[4,544,128]{2,1,0:T(8,128)(2,1)S(1)}, bf16[4,544,128]{2,1,0:T(8,128)(2,1)S(1)}, u32[]{:S(2)}, u32[]{:S(2)}) %collective-permute-start.20) | collective-permute-done | bytes 557088 | tf_op jit(solution)/shard_map/ppermute | solution.py:44
  66.6 12.4 %collective-permute-done.19.refs_4_ = bf16[1024,128]{1,0:T(8,128)(2,1)S(1)} collective-permute-done((bf16[1024,128]{1,0:T(8,128)(2,1)S(1)}, bf16[1024,128]{1,0:T(8,128)(2,1)S(1)}, u32[]{:S(2)}, u32[]{:S(2)}) %collective-permute-start.19) | collective-permute-done | bytes 262176 | tf_op jit(solution)/shard_map/ppermute | solution.py:32
  79.1 0.5 collective-permute-start.25
  80.0 0.2 collective-permute-start.22
  80.2 2.8 %collective-permute-done.25.refs_21_ = bf16[2048,128]{1,0:T(8,128)(2,1)} collective-permute-done((bf16[2048,128]{1,0:T(8,128)(2,1)S(1)}, bf16[2048,128]{1,0:T(8,128)(2,1)}, u32[]{:S(2)}, u32[]{:S(2)}) %collective-permute-start.25) | collective-permute-done | bytes 524320 | tf_op jit(solution)/shard_map/ppermute | solution.py:44
  83.0 0.1 collective-permute-start.27
  83.2 0.1 collective-permute-done.24.refs_23_
  83.3 3.3 %collective-permute-done.22.refs_8_ = bf16[2,544,128]{2,1,0:T(8,128)(2,1)S(1)} collective-permute-done((bf16[2,544,128]{2,1,0:T(8,128)(2,1)S(1)}, bf16[2,544,128]{2,1,0:T(8,128)(2,1)S(1)}, u32[]{:S(2)}, u32[]{:S(2)}) %collective-permute-start.22) | collective-permute-done | bytes 278560 | tf_op jit(solution)/shard_map/ppermute | solution.py:32
  86.6 2.3 %collective-permute-done.23.refs_6_ = bf16[1536,128]{1,0:T(8,128)(2,1)S(1)} collective-permute-done((bf16[1536,128]{1,0:T(8,128)(2,1)S(1)}, bf16[1536,128]{1,0:T(8,128)(2,1)S(1)}, u32[]{:S(2)}, u32[]{:S(2)}) %collective-permute-start.23) | collective-permute-done | bytes 393248 | tf_op jit(solution)/shard_map/ppermute | solution.py:32
  89.0 0.5 collective-permute-start.30
  89.6 2.1 %collective-permute-done.28.refs_5_ = bf16[1024,128]{1,0:T(8,128)(2,1)S(1)} collective-permute-done((bf16[1024,128]{1,0:T(8,128)(2,1)}, bf16[1024,128]{1,0:T(8,128)(2,1)S(1)}, u32[]{:S(2)}, u32[]{:S(2)}) %collective-permute-start.28) | collective-permute-done | bytes 262176 | tf_op jit(solution)/shard_map/ppermute | solution.py:44
  91.7 0.7 copy-done.22
  92.4 0.7 copy-done.20
  93.2 0.8 copy-done.17
  94.0 26.3 %shard_map.74 = f32[3,64,128]{2,1,0:T(8,128)} custom-call(s32[774]{0:T(1024)} %concatenate.45.meta, bf16[3072,128]{1,0:T(8,128)(2,1)} %copy-done.3, bf16[3072,128]{1,0:T(8,128)(2,1)} %copy-done.9, bf16[4,544,128]{2,1,0:T(8,128)(2,1)} %copy-done.5, bf16[4,544,128]{2,1,0:T(8,128)(2,1)} %copy-done.13, bf16[1024,128]{1,0:T(8,128)(2,1)} %copy-done.21, ...), custom_call_target="tpu_custom_call" | custom-call | tf_op jit(solution)/shard_map/pallas_call | solution.py:317
  120.3 0.1 collective-permute-start.31
  120.4 5.3 %collective-permute-done.31 = f32[3,64,128]{2,1,0:T(8,128)S(1)} collective-permute-done((f32[3,64,128]{2,1,0:T(8,128)}, f32[3,64,128]{2,1,0:T(8,128)S(1)}, u32[]{:S(2)}, u32[]{:S(2)}) %collective-permute-start.31) | collective-permute-done | bytes 98336 | tf_op jit(solution)/shard_map/ppermute | solution.py:341
  125.8 1.5 %add.90 = f32[3,64,128]{2,1,0:T(8,128)} add(f32[3,64,128]{2,1,0:T(8,128)} %shard_map.74, f32[3,64,128]{2,1,0:T(8,128)S(1)} %collective-permute-done.31) | non-fusion elementwise | flops 24576 | bytes 294912 | tf_op jit(solution)/shard_map/add | solution.py:341
  (100 shorter events, 1.7 us)
Async XLA Ops:
  0.8 3.7 %copy-start.24 = (s32[48,12]{1,0:T(8,128)}, s32[48,12]{1,0:T(8,128)S(1)}, u32[]{:S(2)}) copy-start(s32[48,12]{1,0:T(8,128)S(1)} %copy.11.here) | copy-start | bytes 6916
  0.8 3.7 %collective-permute-start = (s32[48,12]{1,0:T(8,128)S(1)}, s32[48,12]{1,0:T(8,128)S(1)}, u32[]{:S(2)}, u32[]{:S(2)}) collective-permute-start(s32[48,12]{1,0:T(8,128)S(1)} %copy.11.here), channel_id=1, source_target_pairs={{0,32},{32,0},{64,96},{96,64},{128,160},{160,128},{192,224},{224,1... | collective-permute-start | bytes 6920 | tf_op jit(solution)/shard_map/ppermute | solution.py:44
  7.7 10.2 %collective-permute-start.2 = (bf16[544,128]{1,0:T(8,128)(2,1)}, bf16[544,128]{1,0:T(8,128)(2,1)S(1)}, u32[]{:S(2)}, u32[]{:S(2)}) collective-permute-start(bf16[544,128]{1,0:T(8,128)(2,1)} %get-tuple-element.40), channel_id=1, source_target_pairs={{0,1},{1,2},{2,3},{3,0},{4,5},{5,6},{6,7},{7,4},{8,9},{9,10},{10,1... | collective-permute-start | bytes 417800 | tf_op jit(solution)/shard_map/ppermute | solution.py:32
  9.3 8.6 %collective-permute-start.1 = (bf16[1024,128]{1,0:T(8,128)(2,1)}, bf16[1024,128]{1,0:T(8,128)(2,1)S(1)}, u32[]{:S(2)}, u32[]{:S(2)}) collective-permute-start(bf16[1024,128]{1,0:T(8,128)(2,1)} %get-tuple-element.39), channel_id=1, source_target_pairs={{0,4},{1,5},{2,6},{3,7},{4,8},{5,9},{6,10},{7,11},{8,12},{9,13},{1... | collective-permute-start | bytes 786440 | tf_op jit(solution)/shard_map/ppermute | solution.py:32
  12.1 5.8 %collective-permute-start.3 = (bf16[272,128]{1,0:T(8,128)(2,1)S(1)}, bf16[272,128]{1,0:T(8,128)(2,1)S(1)}, u32[]{:S(2)}, u32[]{:S(2)}) collective-permute-start(bf16[272,128]{1,0:T(8,128)(2,1)S(1)} %constant_dynamic-slice_fusion.2), channel_id=1, source_target_pairs={{0,2},{1,3},{2,0},{3,1},{4,6},{5,7},{6,4},{7,5},{8,10},{9,11},{10,... | collective-permute-start | bytes 208904 | tf_op jit(solution)/shard_map/ppermute | solution.py:32
  17.9 5.3 %collective-permute-start.6 = (bf16[1024,128]{1,0:T(8,128)(2,1)S(1)}, bf16[1024,128]{1,0:T(8,128)(2,1)S(1)}, u32[]{:S(2)}, u32[]{:S(2)}) collective-permute-start(bf16[1024,128]{1,0:T(8,128)(2,1)S(1)} %collective-permute-done.1), channel_id=1, source_target_pairs={{0,32},{32,0},{64,96},{96,64},{128,160},{160,128},{192,224},{224,1... | collective-permute-start | bytes 786440 | tf_op jit(solution)/shard_map/ppermute | solution.py:44
  17.9 8.6 %collective-permute-start.4 = (bf16[1024,128]{1,0:T(8,128)(2,1)S(1)}, bf16[1024,128]{1,0:T(8,128)(2,1)S(1)}, u32[]{:S(2)}, u32[]{:S(2)}) collective-permute-start(bf16[1024,128]{1,0:T(8,128)(2,1)S(1)} %collective-permute-done.1), channel_id=1, source_target_pairs={{0,4},{1,5},{2,6},{3,7},{4,8},{5,9},{6,10},{7,11},{8,12},{9,13},{1... | collective-permute-start | bytes 786440 | tf_op jit(solution)/shard_map/ppermute | solution.py:32
  19.9 6.7 %copy-start.18 = (bf16[544,128]{1,0:T(8,128)(2,1)S(1)}, bf16[544,128]{1,0:T(8,128)(2,1)}, u32[]{:S(2)}) copy-start(bf16[544,128]{1,0:T(8,128)(2,1)} %get-tuple-element.40) | copy-start | bytes 417796
  19.9 3.2 %collective-permute-start.5 = (bf16[816,128]{1,0:T(8,128)(2,1)S(1)}, bf16[816,128]{1,0:T(8,128)(2,1)S(1)}, u32[]{:S(2)}, u32[]{:S(2)}) collective-permute-start(bf16[816,128]{1,0:T(8,128)(2,1)S(1)} %pad_maximum_fusion.2), channel_id=1, source_target_pairs={{0,32},{32,0},{64,96},{96,64},{128,160},{160,128},{192,224},{224,1... | collective-permute-start | bytes 626696 | tf_op jit(solution)/shard_map/ppermute | solution.py:44
  26.6 23.1 %copy-start = (bf16[3072,128]{1,0:T(8,128)(2,1)}, bf16[3072,128]{1,0:T(8,128)(2,1)S(1)}, u32[]{:S(2)}) copy-start(bf16[3072,128]{1,0:T(8,128)(2,1)S(1)} %pad_maximum_fusion.refs_11_) | copy-start | bytes 2359300
  26.7 36.1 %copy-start.1 = (bf16[4,544,128]{2,1,0:T(8,128)(2,1)}, bf16[4,544,128]{2,1,0:T(8,128)(2,1)S(1)}, u32[]{:S(2)}) copy-start(bf16[4,544,128]{2,1,0:T(8,128)(2,1)S(1)} %pad_maximum_fusion.1.refs_10_) | copy-start | bytes 1671172
  26.7 19.2 %collective-permute-start.10 = (bf16[3072,128]{1,0:T(8,128)(2,1)S(1)}, bf16[3072,128]{1,0:T(8,128)(2,1)S(1)}, u32[]{:S(2)}, u32[]{:S(2)}) collective-permute-start(bf16[3072,128]{1,0:T(8,128)(2,1)S(1)} %pad_maximum_fusion.refs_11_), channel_id=1, source_target_pairs={{0,1},{1,2},{2,3},{3,0},{4,5},{5,6},{6,7},{7,4},{8,9},{9,10},{10,1... | collective-permute-start | bytes 2359304 | tf_op jit(solution)/shard_map/ppermute | solution.py:32
  26.8 19.1 %collective-permute-start.9 = (bf16[4,544,128]{2,1,0:T(8,128)(2,1)S(1)}, bf16[4,544,128]{2,1,0:T(8,128)(2,1)S(1)}, u32[]{:S(2)}, u32[]{:S(2)}) collective-permute-start(bf16[4,544,128]{2,1,0:T(8,128)(2,1)S(1)} %pad_maximum_fusion.1.refs_10_), channel_id=1, source_target_pairs={{0,4},{1,5},{2,6},{3,7},{4,8},{5,9},{6,10},{7,11},{8,12},{9,13},{1... | collective-permute-start | bytes 1671176 | tf_op jit(solution)/shard_map/ppermute | solution.py:32
  28.8 17.1 %collective-permute-start.11 = (bf16[1024,128]{1,0:T(8,128)(2,1)S(1)}, bf16[1024,128]{1,0:T(8,128)(2,1)}, u32[]{:S(2)}, u32[]{:S(2)}) collective-permute-start(bf16[1024,128]{1,0:T(8,128)(2,1)S(1)} %collective-permute-done.4), channel_id=1, source_target_pairs={{0,32},{32,0},{64,96},{96,64},{128,160},{160,128},{192,224},{224,1... | collective-permute-start | bytes 786440 | tf_op jit(solution)/shard_map/ppermute | solution.py:44
  28.8 17.1 %collective-permute-start.7 = (bf16[1024,128]{1,0:T(8,128)(2,1)S(1)}, bf16[1024,128]{1,0:T(8,128)(2,1)S(1)}, u32[]{:S(2)}, u32[]{:S(2)}) collective-permute-start(bf16[1024,128]{1,0:T(8,128)(2,1)S(1)} %collective-permute-done.4), channel_id=1, source_target_pairs={{0,4},{1,5},{2,6},{3,7},{4,8},{5,9},{6,10},{7,11},{8,12},{9,13},{1... | collective-permute-start | bytes 786440 | tf_op jit(solution)/shard_map/ppermute | solution.py:32
  31.3 14.6 %collective-permute-start.8 = (bf16[512,128]{1,0:T(8,128)(2,1)S(1)}, bf16[512,128]{1,0:T(8,128)(2,1)S(1)}, u32[]{:S(2)}, u32[]{:S(2)}) collective-permute-start(bf16[512,128]{1,0:T(8,128)(2,1)S(1)} %constant_dynamic-slice_fusion.1), channel_id=1, source_target_pairs={{0,8},{1,9},{2,10},{3,11},{4,12},{5,13},{6,14},{7,15},{8,16},{9,17... | collective-permute-start | bytes 393224 | tf_op jit(solution)/shard_map/ppermute | solution.py:32
  46.8 16.0 %copy-start.2 = (bf16[3072,128]{1,0:T(8,128)(2,1)}, bf16[3072,128]{1,0:T(8,128)(2,1)S(1)}, u32[]{:S(2)}) copy-start(bf16[3072,128]{1,0:T(8,128)(2,1)S(1)} %collective-permute-done.10.refs_12_) | copy-start | bytes 2359300
  46.8 16.0 %collective-permute-start.16 = (bf16[3072,128]{1,0:T(8,128)(2,1)S(1)}, bf16[3072,128]{1,0:T(8,128)(2,1)S(1)}, u32[]{:S(2)}, u32[]{:S(2)}) collective-permute-start(bf16[3072,128]{1,0:T(8,128)(2,1)S(1)} %collective-permute-done.10.refs_12_), channel_id=1, source_target_pairs={{0,32},{32,0},{64,96},{96,64},{128,160},{160,128},{192,224},{224,1... | collective-permute-start | bytes 2359304 | tf_op jit(solution)/shard_map/ppermute | solution.py:44
  48.0 14.7 %copy-start.7 = (bf16[2048,128]{1,0:T(8,128)(2,1)}, bf16[2048,128]{1,0:T(8,128)(2,1)S(1)}, u32[]{:S(2)}) copy-start(bf16[2048,128]{1,0:T(8,128)(2,1)S(1)} %constant_dynamic-update-slice_fusion.refs_16_) | copy-start | bytes 1572868
  48.0 15.0 %copy-start.11 = (bf16[4,544,128]{2,1,0:T(8,128)(2,1)S(1)}, bf16[4,544,128]{2,1,0:T(8,128)(2,1)}, u32[]{:S(2)}) copy-start(bf16[4,544,128]{2,1,0:T(8,128)(2,1)} %copy-done.10) | copy-start | bytes 1671172
  48.0 14.7 %collective-permute-start.14 = (bf16[2048,128]{1,0:T(8,128)(2,1)S(1)}, bf16[2048,128]{1,0:T(8,128)(2,1)S(1)}, u32[]{:S(2)}, u32[]{:S(2)}) collective-permute-start(bf16[2048,128]{1,0:T(8,128)(2,1)S(1)} %constant_dynamic-update-slice_fusion.refs_16_), channel_id=1, source_target_pairs={{0,1},{1,2},{2,3},{3,0},{4,5},{5,6},{6,7},{7,4},{8,9},{9,10},{10,1... | collective-permute-start | bytes 1572872 | tf_op jit(solution)/shard_map/ppermute | solution.py:32
  48.7 14.1 %collective-permute-start.12 = (bf16[4,544,128]{2,1,0:T(8,128)(2,1)}, bf16[4,544,128]{2,1,0:T(8,128)(2,1)}, u32[]{:S(2)}, u32[]{:S(2)}) collective-permute-start(bf16[4,544,128]{2,1,0:T(8,128)(2,1)} %copy-done.10), channel_id=1, source_target_pairs={{0,4},{1,5},{2,6},{3,7},{4,8},{5,9},{6,10},{7,11},{8,12},{9,13},{1... | collective-permute-start | bytes 1671176 | tf_op jit(solution)/shard_map/ppermute | solution.py:32
  49.7 13.0 %collective-permute-start.13 = (bf16[1536,128]{1,0:T(8,128)(2,1)S(1)}, bf16[1536,128]{1,0:T(8,128)(2,1)S(1)}, u32[]{:S(2)}, u32[]{:S(2)}) collective-permute-start(bf16[1536,128]{1,0:T(8,128)(2,1)S(1)} %slice.37), channel_id=1, source_target_pairs={{0,1},{1,2},{2,3},{3,0},{4,5},{5,6},{6,7},{7,4},{8,9},{9,10},{10,1... | collective-permute-start | bytes 1179656 | tf_op jit(solution)/shard_map/ppermute | solution.py:32
  51.3 11.4 %collective-permute-start.15 = (bf16[1536,128]{1,0:T(8,128)(2,1)S(1)}, bf16[1536,128]{1,0:T(8,128)(2,1)S(1)}, u32[]{:S(2)}, u32[]{:S(2)}) collective-permute-start(bf16[1536,128]{1,0:T(8,128)(2,1)S(1)} %constant_dynamic-update-slice_fusion.2), channel_id=1, source_target_pairs={{0,32},{32,0},{64,96},{96,64},{128,160},{160,128},{192,224},{224,1... | collective-permute-start | bytes 1179656 | tf_op jit(solution)/shard_map/ppermute | solution.py:44
  62.7 16.9 %copy-start.14 = (bf16[1536,128]{1,0:T(8,128)(2,1)}, bf16[1536,128]{1,0:T(8,128)(2,1)S(1)}, u32[]{:S(2)}) copy-start(bf16[1536,128]{1,0:T(8,128)(2,1)S(1)} %collective-permute-done.13.refs_18_) | copy-start | bytes 1179652
  62.7 17.3 %copy-start.6 = (bf16[2048,128]{1,0:T(8,128)(2,1)}, bf16[2048,128]{1,0:T(8,128)(2,1)S(1)}, u32[]{:S(2)}) copy-start(bf16[2048,128]{1,0:T(8,128)(2,1)S(1)} %collective-permute-done.14.refs_20_) | copy-start | bytes 1572868
  62.8 16.3 %copy-start.8 = (bf16[3072,128]{1,0:T(8,128)(2,1)}, bf16[3072,128]{1,0:T(8,128)(2,1)S(1)}, u32[]{:S(2)}) copy-start(bf16[3072,128]{1,0:T(8,128)(2,1)S(1)} %collective-permute-done.16.refs_13_) | copy-start | bytes 2359300
  62.9 30.3 %copy-start.4 = (bf16[3072,128]{1,0:T(8,128)(2,1)}, bf16[3072,128]{1,0:T(8,128)(2,1)S(1)}, u32[]{:S(2)}) copy-start(bf16[3072,128]{1,0:T(8,128)(2,1)S(1)} %constant_dynamic-update-slice_fusion.4.refs_17_) | copy-start | bytes 2359300
  62.9 16.1 %collective-permute-start.18 = (bf16[3072,128]{1,0:T(8,128)(2,1)S(1)}, bf16[3072,128]{1,0:T(8,128)(2,1)S(1)}, u32[]{:S(2)}, u32[]{:S(2)}) collective-permute-start(bf16[3072,128]{1,0:T(8,128)(2,1)S(1)} %constant_dynamic-update-slice_fusion.4.refs_17_), channel_id=1, source_target_pairs={{0,1},{1,2},{2,3},{3,0},{4,5},{5,6},{6,7},{7,4},{8,9},{9,10},{10,1... | collective-permute-start | bytes 2359304 | tf_op jit(solution)/shard_map/ppermute | solution.py:32
  63.0 3.6 %collective-permute-start.20 = (bf16[4,544,128]{2,1,0:T(8,128)(2,1)S(1)}, bf16[4,544,128]{2,1,0:T(8,128)(2,1)S(1)}, u32[]{:S(2)}, u32[]{:S(2)}) collective-permute-start(bf16[4,544,128]{2,1,0:T(8,128)(2,1)S(1)} %copy-done.11), channel_id=1, source_target_pairs={{0,32},{32,0},{64,96},{96,64},{128,160},{160,128},{192,224},{224,1... | collective-permute-start | bytes 1671176 | tf_op jit(solution)/shard_map/ppermute | solution.py:44
  65.0 14.0 %collective-permute-start.17 = (bf16[4,544,128]{2,1,0:T(8,128)(2,1)}, bf16[4,544,128]{2,1,0:T(8,128)(2,1)S(1)}, u32[]{:S(2)}, u32[]{:S(2)}) collective-permute-start(bf16[4,544,128]{2,1,0:T(8,128)(2,1)} %collective-permute-done.12.refs_22_), channel_id=1, source_target_pairs={{0,4},{1,5},{2,6},{3,7},{4,8},{5,9},{6,10},{7,11},{8,12},{9,13},{1... | collective-permute-start | bytes 1671176 | tf_op jit(solution)/shard_map/ppermute | solution.py:32
  65.0 14.0 %collective-permute-start.21 = (bf16[1536,128]{1,0:T(8,128)(2,1)S(1)}, bf16[1536,128]{1,0:T(8,128)(2,1)S(1)}, u32[]{:S(2)}, u32[]{:S(2)}) collective-permute-start(bf16[1536,128]{1,0:T(8,128)(2,1)S(1)} %collective-permute-done.13.refs_18_), channel_id=1, source_target_pairs={{0,32},{32,0},{64,96},{96,64},{128,160},{160,128},{192,224},{224,1... | collective-permute-start | bytes 1179656 | tf_op jit(solution)/shard_map/ppermute | solution.py:44
  65.1 13.9 %collective-permute-start.19 = (bf16[1024,128]{1,0:T(8,128)(2,1)S(1)}, bf16[1024,128]{1,0:T(8,128)(2,1)S(1)}, u32[]{:S(2)}, u32[]{:S(2)}) collective-permute-start(bf16[1024,128]{1,0:T(8,128)(2,1)S(1)} %slice.38), channel_id=1, source_target_pairs={{0,1},{1,2},{2,3},{3,0},{4,5},{5,6},{6,7},{7,4},{8,9},{9,10},{10,1... | collective-permute-start | bytes 786440 | tf_op jit(solution)/shard_map/ppermute | solution.py:32
  66.6 12.6 %copy-start.12 = (bf16[4,544,128]{2,1,0:T(8,128)(2,1)}, bf16[4,544,128]{2,1,0:T(8,128)(2,1)S(1)}, u32[]{:S(2)}) copy-start(bf16[4,544,128]{2,1,0:T(8,128)(2,1)S(1)} %collective-permute-done.20.refs_15_) | copy-start | bytes 1671172
  79.0 14.2 %copy-start.5 = (bf16[4,544,128]{2,1,0:T(8,128)(2,1)}, bf16[4,544,128]{2,1,0:T(8,128)(2,1)S(1)}, u32[]{:S(2)}) copy-start(bf16[4,544,128]{2,1,0:T(8,128)(2,1)S(1)} %collective-permute-done.17.refs_2_) | copy-start | bytes 1671172
  79.0 14.1 %copy-start.3 = (bf16[3072,128]{1,0:T(8,128)(2,1)}, bf16[3072,128]{1,0:T(8,128)(2,1)S(1)}, u32[]{:S(2)}) copy-start(bf16[3072,128]{1,0:T(8,128)(2,1)S(1)} %collective-permute-done.18.refs_0_) | copy-start | bytes 2359300
  79.0 9.9 %collective-permute-start.26 = (bf16[3072,128]{1,0:T(8,128)(2,1)S(1)}, bf16[3072,128]{1,0:T(8,128)(2,1)S(1)}, u32[]{:S(2)}, u32[]{:S(2)}) collective-permute-start(bf16[3072,128]{1,0:T(8,128)(2,1)S(1)} %collective-permute-done.18.refs_0_), channel_id=1, source_target_pairs={{0,32},{32,0},{64,96},{96,64},{128,160},{160,128},{192,224},{224,1... | collective-permute-start | bytes 2359304 | tf_op jit(solution)/shard_map/ppermute | solution.py:44
  79.1 3.9 %collective-permute-start.25 = (bf16[2048,128]{1,0:T(8,128)(2,1)S(1)}, bf16[2048,128]{1,0:T(8,128)(2,1)}, u32[]{:S(2)}, u32[]{:S(2)}) collective-permute-start(bf16[2048,128]{1,0:T(8,128)(2,1)S(1)} %collective-permute-done.14.refs_20_), channel_id=1, source_target_pairs={{0,32},{32,0},{64,96},{96,64},{128,160},{160,128},{192,224},{224,1... | collective-permute-start | bytes 1572872 | tf_op jit(solution)/shard_map/ppermute | solution.py:44
  79.8 3.5 %collective-permute-start.24 = (bf16[4,544,128]{2,1,0:T(8,128)(2,1)}, bf16[4,544,128]{2,1,0:T(8,128)(2,1)}, u32[]{:S(2)}, u32[]{:S(2)}) collective-permute-start(bf16[4,544,128]{2,1,0:T(8,128)(2,1)} %collective-permute-done.12.refs_22_), channel_id=1, source_target_pairs={{0,32},{32,0},{64,96},{96,64},{128,160},{160,128},{192,224},{224,1... | collective-permute-start | bytes 1671176 | tf_op jit(solution)/shard_map/ppermute | solution.py:44
  79.9 9.1 %collective-permute-start.23 = (bf16[1536,128]{1,0:T(8,128)(2,1)S(1)}, bf16[1536,128]{1,0:T(8,128)(2,1)S(1)}, u32[]{:S(2)}, u32[]{:S(2)}) collective-permute-start(bf16[1536,128]{1,0:T(8,128)(2,1)S(1)} %slice.39), channel_id=1, source_target_pairs={{0,1},{1,2},{2,3},{3,0},{4,5},{5,6},{6,7},{7,4},{8,9},{9,10},{10,1... | collective-permute-start | bytes 1179656 | tf_op jit(solution)/shard_map/ppermute | solution.py:32
  80.0 6.6 %collective-permute-start.22 = (bf16[2,544,128]{2,1,0:T(8,128)(2,1)S(1)}, bf16[2,544,128]{2,1,0:T(8,128)(2,1)S(1)}, u32[]{:S(2)}, u32[]{:S(2)}) collective-permute-start(bf16[2,544,128]{2,1,0:T(8,128)(2,1)S(1)} %constant_dynamic-slice_fusion), channel_id=1, source_target_pairs={{0,4},{1,5},{2,6},{3,7},{4,8},{5,9},{6,10},{7,11},{8,12},{9,13},{1... | collective-permute-start | bytes 835592 | tf_op jit(solution)/shard_map/ppermute | solution.py:32
  83.0 8.7 %collective-permute-start.27 = (bf16[4,544,128]{2,1,0:T(8,128)(2,1)S(1)}, bf16[4,544,128]{2,1,0:T(8,128)(2,1)S(1)}, u32[]{:S(2)}, u32[]{:S(2)}) collective-permute-start(bf16[4,544,128]{2,1,0:T(8,128)(2,1)S(1)} %collective-permute-done.17.refs_2_), channel_id=1, source_target_pairs={{0,32},{32,0},{64,96},{96,64},{128,160},{160,128},{192,224},{224,1... | collective-permute-start | bytes 1671176 | tf_op jit(solution)/shard_map/ppermute | solution.py:44
  86.6 5.1 %copy-start.19 = (bf16[2,544,128]{2,1,0:T(8,128)(2,1)}, bf16[2,544,128]{2,1,0:T(8,128)(2,1)S(1)}, u32[]{:S(2)}) copy-start(bf16[2,544,128]{2,1,0:T(8,128)(2,1)S(1)} %collective-permute-done.22.refs_8_) | copy-start | bytes 835588
  88.9 4.2 %copy-start.9 = (bf16[3072,128]{1,0:T(8,128)(2,1)}, bf16[3072,128]{1,0:T(8,128)(2,1)S(1)}, u32[]{:S(2)}) copy-start(bf16[3072,128]{1,0:T(8,128)(2,1)S(1)} %collective-permute-done.26.refs_1_) | copy-start | bytes 2359300
  88.9 4.2 %collective-permute-start.29 = (bf16[1536,128]{1,0:T(8,128)(2,1)S(1)}, bf16[1536,128]{1,0:T(8,128)(2,1)S(1)}, u32[]{:S(2)}, u32[]{:S(2)}) collective-permute-start(bf16[1536,128]{1,0:T(8,128)(2,1)S(1)} %collective-permute-done.23.refs_6_), channel_id=1, source_target_pairs={{0,32},{32,0},{64,96},{96,64},{128,160},{160,128},{192,224},{224,1... | collective-permute-start | bytes 1179656 | tf_op jit(solution)/shard_map/ppermute | solution.py:44
  89.0 2.7 %collective-permute-start.30 = (bf16[2,544,128]{2,1,0:T(8,128)(2,1)S(1)}, bf16[2,544,128]{2,1,0:T(8,128)(2,1)S(1)}, u32[]{:S(2)}, u32[]{:S(2)}) collective-permute-start(bf16[2,544,128]{2,1,0:T(8,128)(2,1)S(1)} %collective-permute-done.22.refs_8_), channel_id=1, source_target_pairs={{0,32},{32,0},{64,96},{96,64},{128,160},{160,128},{192,224},{224,1... | collective-permute-start | bytes 835592 | tf_op jit(solution)/shard_map/ppermute | solution.py:44
  89.5 2.2 %collective-permute-start.28 = (bf16[1024,128]{1,0:T(8,128)(2,1)}, bf16[1024,128]{1,0:T(8,128)(2,1)S(1)}, u32[]{:S(2)}, u32[]{:S(2)}) collective-permute-start(bf16[1024,128]{1,0:T(8,128)(2,1)} %copy-done.21), channel_id=1, source_target_pairs={{0,32},{32,0},{64,96},{96,64},{128,160},{160,128},{192,224},{224,1... | collective-permute-start | bytes 786440 | tf_op jit(solution)/shard_map/ppermute | solution.py:44
  120.3 5.5 %collective-permute-start.31 = (f32[3,64,128]{2,1,0:T(8,128)}, f32[3,64,128]{2,1,0:T(8,128)S(1)}, u32[]{:S(2)}, u32[]{:S(2)}) collective-permute-start(f32[3,64,128]{2,1,0:T(8,128)} %shard_map.74), channel_id=1, source_target_pairs={{224,0},{0,32},{32,64},{64,96},{96,128},{128,160},{160,192},{192,2... | collective-permute-start | bytes 294920 | tf_op jit(solution)/shard_map/ppermute | solution.py:341
  (10 other events, 10.4 us)

commit v2 on v1

v2 whole, which is shorter than its diff:
```python
import functools

import jax
import jax.numpy as jnp
import numpy as np
from jax import lax
from jax.experimental import pallas as pl
from jax.experimental.pallas import tpu as pltpu
from jax.sharding import PartitionSpec as P

NZ, NY = 8, 4
SLOTS = NZ * NY
SEC = 12
B = 128
ROWS = SEC * B
S1 = 4
N1, N2 = S1 * B, (SEC - S1) * B
NC = 32
TILES = 3
VMEM_LIMIT = 60 * 2**20
AHEAD = 2
F32, BF16 = jnp.float32, jnp.bfloat16


def hop(v, dz, dy):
    route = []
    for pair in range(8):
        s = -1 if pair % 2 else 1
        for z in range(NZ):
            for y in range(NY):
                to = (z + s * dz) % NZ * NY + (y + s * dy) % NY
                route.append((pair * SLOTS + z * NY + y, pair * SLOTS + to))
    return lax.ppermute(v, ("pair", "sec"), route)


def zhop(v):
    return hop(v, 1, 0)


def yhop(v):
    return hop(v, 0, 1)


def swap(v):
    return lax.ppermute(v, "pair", [(i, i ^ 1) for i in range(lax.axis_size("pair"))])


def part(v, core, axis=0):
    n = v.shape[axis] // 2
    return lax.dynamic_slice_in_dim(v, core * n, n, axis)


YS = (0, 1, 2, -1)


def sync(*arrays):
    return lax.optimization_barrier(arrays)


def gather_pieces(first, second, core, *others):
    n, h2 = first.shape[0], N2 // 2
    w1, near, far = zhop(second), yhop(first), hop(part(first, core), 0, 2)
    w1, near, far, *others = sync(w1, near, far, *others)

    w2, other = zhop(w1), swap(jnp.concatenate([near, far, w1]))
    w2, other = sync(w2, other)

    near_s, far_s, w1s = other[:n], other[n:n + n // 2], other[n + n // 2:]
    far = jnp.where(core == 0, jnp.concatenate([far, far_s]), jnp.concatenate([far_s, far]))
    bundle = jnp.concatenate([first, near, far, near_s])
    own = jnp.where(core == 0, second, jnp.concatenate([second[h2:], second[:h2]]))
    a = jnp.concatenate([w1, own, w1s])
    w3, z1, a1 = zhop(w2), zhop(bundle), yhop(a)
    w4, w2s = hop(part(w2, core), 2, 0), swap(w2)
    w3, z1, a1, w4, w2s = sync(w3, z1, a1, w4, w2s)

    ha = a.shape[0] // 2
    b = jnp.concatenate([w2, w2s])
    wc = jnp.concatenate([w3, w4])
    z2, ab, wcs, a1s = zhop(z1), yhop(jnp.concatenate([a1[:ha], b])), swap(wc), swap(a1)
    z2, ab, wcs, a1s = sync(z2, ab, wcs, a1s)

    c = jnp.concatenate([wc, wcs])
    hb, hc = b.shape[0] // 2, c.shape[0] // 2
    z3, cb, z1s, abs_ = zhop(z2), yhop(jnp.concatenate([c, ab[ha:ha + hb]])), swap(z1), swap(ab)
    z3, cb, z1s, abs_ = sync(z3, cb, z1s, abs_)

    z4, c2 = zhop(lax.dynamic_slice_in_dim(z3, core * n, 2 * n, 0)), yhop(cb[:hc])
    z2s, z3s, cbs = swap(z2), swap(z3), swap(cb)
    z4, c2, z2s, z3s, cbs = sync(z4, c2, z2s, z3s, cbs)
    z4s, c2s = swap(z4), swap(c2)

    def step(dz):
        return [(i * n, N1, dz, dy, 0, 0, False) for i, dy in enumerate(YS)]

    def shift(seg, dy, stop, by=0):
        return [(r + by, m, dz, dy, o, e, x) for r, m, dz, _, o, e, x in seg if r < stop]

    def rest(parts):
        segs, r = [], 0
        for rows, dz, o, more in parts:
            segs.append((r, rows, dz, 0, N1 + o, more, False))
            r += rows
        return segs

    a_seg = rest([(N2, 1, 0, 0), (h2, 0, 0, h2), (h2, 0, h2, -h2), (N2, -1, 0, 0)])
    b_seg = rest([(N2, 2, 0, 0), (N2, -2, 0, 0)])
    c_seg = rest([(N2, 3, 0, 0), (h2, 4, 0, h2), (N2, -3, 0, 0), (h2, 4, h2, -h2)])
    couples = [
        (bundle, None, step(0)), (a, None, a_seg), (a1, a1s, shift(a_seg, 1, 2 * ha)),
        (z1, z1s, step(1)), (b, None, b_seg), (c, None, c_seg),
        (ab, abs_, shift(a_seg, 2, ha) + shift(b_seg, 1, 2 * hb, ha)), (z2, z2s, step(2)),
        (cb, cbs, shift(c_seg, 1, 2 * hc) + shift(b_seg, 2, hb, 2 * hc)), (z3, z3s, step(3)),
        (c2, c2s, shift(c_seg, 2, hc)),
        (z4, z4s, [(i * n, N1, 4, i, 0, 0, True) for i in range(2)]),
    ]
    return couples, others


def place(seg, core, swapped):
    who = 1 - core if swapped else core
    sign = 2 * who - 1
    _, _, dz, dy, row, more, last = seg
    return dz * sign, (1 + dy if who else -dy) if last else dy * sign, row + more * who


def sectors(segments, core, swapped):
    found = []
    for seg in segments:
        dz, dy, row = place(seg, core, swapped)
        found += [(dz % NZ, dy % NY, row // B + q) for q in range(seg[1] // B)]
    return found


def arrays_of(couples):
    return [(w, seg, swapped, number) for number, (u, v, seg) in enumerate(couples)
            for w, swapped in ((u, False), (v, True)) if w is not None]


def couple_spec(couple):
    _, v, segments = couple
    count = sum(seg[1] for seg in segments) // B // (2 if v is None else 1)
    return count, next(n for n in (12, 16, 14, 8) if count % n == 0)


def tables():
    shapes = []

    def trace(first, second):
        couples, _ = gather_pieces(first, second, jnp.int32(0))
        shapes.extend(couples)
        return first

    jax.eval_shape(
        trace, jax.ShapeDtypeStruct((N1 + NC, B), BF16), jax.ShapeDtypeStruct((N2, B), BF16))
    index, places, segs = [], [], []
    for core in (0, 1):
        at = [(place(seg, core, swapped), seg[1]) for _, segments, swapped, _ in arrays_of(shapes)
              for seg in segments]
        number = {}
        for (dz, dy, row), rows in at:
            if row < N1:
                number[dz % NZ, dy % NY] = len(number)
        flat = []
        for _, v, segments in shapes:
            left = sectors(segments, core, False)
            half = len(left) // 2
            left, right = (left[:half], left[half:]) if v is None else (left, sectors(segments, core, True))
            flat += [t for p in zip(left, right) for t in p]
        index.append([number[t[:2]] * 16 + t[2] for t in flat])
        places.append(flat)
        segs.append([p for p, _ in at])
    return (np.array(t, np.int32) for t in (index, places, segs))


def prepare_kernel(rows, psi, here, there, first, second):
    core = lax.rem(lax.axis_index("pair"), 2)
    row = lax.broadcasted_iota(jnp.int32, (B, B), 0)
    for s in range(SEC):
        live = jnp.where(row < rows[s], psi[s], jnp.zeros((B, B), BF16))
        if s < S1:
            first[pl.ds(s * B, B), :] = live
        else:
            second[pl.ds((s - S1) * B, B), :] = live
    pairs = here.shape[0]
    lane = lax.broadcasted_iota(jnp.int32, (pairs, B), 1)
    pair = lax.broadcasted_iota(jnp.int32, (pairs, B), 0)
    high = jnp.where(lane == pair, 1.0, 0.0).astype(BF16)
    low = jnp.where(lane == pair + B // 2, 1.0, 0.0).astype(BF16)

    def words(ref):
        v = ref[...]
        contract = (((0,), (0,)), ((), ()))
        up = (v // 16).astype(F32).astype(BF16)
        down = (v % 16).astype(F32).astype(BF16)
        return (lax.dot_general(up, high, contract, preferred_element_type=F32)
                + lax.dot_general(down, low, contract, preferred_element_type=F32)).astype(BF16)

    mine, other = words(here), words(there)
    zero = jnp.zeros((16 - SEC, B), BF16)
    even = jnp.where(core == 0, mine, other)
    odd = jnp.where(core == 0, other, mine)
    first[pl.ds(N1, NC), :] = jnp.concatenate([even, zero, odd, zero], axis=0)


def tiles_kernel(specs, plan, meta, *refs):
    n = len(plan)
    pieces, ops, pick, out = refs[:n], *refs[n:n + 3]
    psi, halves, turned, words, table, conn, sems, csem = refs[n + 3:]
    core = meta[TILES]
    pairs = SLOTS * SEC // 2
    targets, places, rows_to = TILES + 1, TILES + 1 + 2 * pairs, TILES + 1 + 4 * pairs

    def fetch(wanted):
        number = 0
        for ref, (segments, couple) in zip(pieces, plan):
            for r, rows, _, _, row, _, _ in segments:
                if couple == wanted:
                    to = pl.ds(pl.multiple_of(meta[rows_to + number], B), rows)
                    pltpu.make_async_copy(ref.at[pl.ds(r, rows)], psi.at[to], sems.at[couple]).start()
                number += 1

    for couple in range(AHEAD):
        fetch(couple)
    slot = 0
    for ref, (segments, couple) in zip(pieces, plan):
        for r, rows, _, _, row, _, _ in segments:
            if row < N1:
                at = pl.ds(pl.multiple_of(r + N1 + core * 16, 16), 16)
                pltpu.make_async_copy(ref.at[at], words.at[slot], csem).start()
                slot += 1

    def sector(s):
        return psi[pl.ds(pl.multiple_of(s * B, B), B), :]

    base = 0
    for couple, (count, batch) in enumerate(specs):
        fetch(couple + AHEAD)
        rows = psi.at[pl.ds(0, 2 * count * B)]
        pltpu.make_async_copy(rows, rows, sems.at[couple]).wait()

        def some(j, carry, batch=batch, base=base):
            for q in range(batch):
                for e in range(2):
                    t = sector(meta[places + 2 * (base + j * batch + q) + e]).T
                    for k in range(TILES):
                        low = lax.rem(meta[k], 2) == 0
                        turned[k, q, :, pl.ds(e * B, B)] = jnp.where(low, t[:64], t[64:])
            for k in range(TILES):
                for e in range(2):
                    rows = turned[k, pl.ds(0, batch), :, pl.ds(e * B, B)].reshape(batch * 64, B)
                    r = jnp.dot(rows, ops[k], preferred_element_type=F32).astype(BF16)
                    to = pl.ds(base + j * batch, batch)
                    halves[k, to, :, pl.ds(e * B, B)] = r.reshape(batch, 64, B)
            return carry

        lax.fori_loop(0, count // batch, some, 0)
        base += count
        if couple == 6:
            pltpu.make_async_copy(words, words, csem).wait()
            values = lax.dot_general(pick[...], words[...].reshape(SLOTS * 16, B), (((1,), (1,)), ((), ())),
            preferred_element_type=F32)
            table[...] = values.astype(jnp.int32)
            pltpu.make_async_copy(table, conn, csem).start()
    pltpu.make_async_copy(table, conn, csem).wait()

    unroll = 48

    def second_stage(j, sums):
        sums = list(sums)
        for u in range(unroll):
            at = j * unroll + u
            for k in range(TILES):
                left, right = (conn[k, meta[targets + 2 * at + e]] for e in (0, 1))
                rhs = jnp.concatenate([sector(left), sector(right)], axis=0)
                sums[k] = sums[k] + jnp.dot(halves[k, at], rhs, preferred_element_type=F32)
        return tuple(sums)

    sums = lax.fori_loop(0, pairs // unroll, second_stage, (jnp.zeros((64, B), F32),) * TILES)
    for k in range(TILES):
        out[k] = sums[k]


def per_device(psi_blocks, sector_rows, left_ops, connect, tile_order):
    sec, pair = lax.axis_index("sec"), lax.axis_index("pair")
    zpos, ypos, core = sec // NY, sec % NY, pair % 2
    vmem = pl.BlockSpec(memory_space=pltpu.VMEM)
    first, second = pl.pallas_call(
        prepare_kernel,
        out_shape=(jax.ShapeDtypeStruct((N1 + NC, B), BF16), jax.ShapeDtypeStruct((N2, B), BF16)),
        grid_spec=pltpu.PrefetchScalarGridSpec(
            num_scalar_prefetch=1, grid=(), in_specs=[vmem] * 3, out_specs=[vmem] * 2,
        ),
    )(sector_rows, psi_blocks, connect, swap(connect))

    mytiles = lax.dynamic_slice_in_dim(tile_order, sec * TILES, TILES)
    lane = jnp.arange(B)[None, :]
    mypairs = jnp.pad(mytiles // 2, (0, 16 - TILES))[:, None]
    pick = jnp.where(lane == mypairs, 16.0, 0.0) + jnp.where(lane == B // 2 + mypairs, 1.0, 0.0)
    pick = pick.astype(BF16)

    index, places, segs = (jnp.asarray(t)[core] for t in tables())

    def slot_of(t):
        return (zpos + t[:, 0]) % NZ * NY + (ypos + t[:, 1]) % NY

    places = slot_of(places) * SEC + places[:, 2]
    rows_to = slot_of(segs) * ROWS + segs[:, 2]
    meta = jnp.concatenate([mytiles, core[None], index, places, rows_to]).astype(jnp.int32)
    couples, (meta, pick, ops) = gather_pieces(first, second, core, meta, pick, left_ops[mytiles // 2])

    arrays = arrays_of(couples)
    plan = [(segments, number) for _, segments, _, number in arrays]
    hbm = pl.BlockSpec(memory_space=pltpu.HBM)
    tiles = pl.pallas_call(
        functools.partial(tiles_kernel, [couple_spec(couple) for couple in couples], plan),
        out_shape=jax.ShapeDtypeStruct((TILES, 64, B), F32),
        grid_spec=pltpu.PrefetchScalarGridSpec(
            num_scalar_prefetch=1,
            grid=(),
            in_specs=[hbm] * len(plan) + [vmem, vmem],
            out_specs=vmem,
            scratch_shapes=[
                pltpu.VMEM((SLOTS * ROWS, B), BF16),
                pltpu.VMEM((TILES, SLOTS * SEC // 2, 64, 2 * B), BF16),
                pltpu.VMEM((TILES, 16, 64, 2 * B), BF16),
                pltpu.VMEM((SLOTS, 16, B), BF16),
                pltpu.VMEM((16, SLOTS * 16), jnp.int32),
                pltpu.SMEM((16, SLOTS * 16), jnp.int32),
                pltpu.SemaphoreType.DMA((len(couples),)),
                pltpu.SemaphoreType.DMA,
            ],
        ),
        compiler_params=pltpu.CompilerParams(vmem_limit_bytes=VMEM_LIMIT),
    )(meta, *[w for w, _, _, _ in arrays], ops, pick)
    ring = [((i - 1) % 8, i) for i in range(8)]
    return tiles + lax.ppermute(tiles, "pair", ring)


def solution(mesh):
    in_specs = (P("sec", None, None), P("sec"), P("pair", None, None), P("pair", "sec"), P())
    out_specs = P(("pair", "sec"), None, None)
    return jax.shard_map(
        per_device, mesh=mesh, in_specs=in_specs, out_specs=out_specs, check_vma=False
    )
```

time: 128 us -> 121 us (0.945)
  Pallas kernels: 28.9 us -> 24.1 us
  starting transfers between devices: 25.9 us -> 21.9 us
  other arithmetic: 4.21 us -> 7.09 us
    pallas_call x1, Pallas kernels: 26.3 us -> 21.5 us  [per_device(): pl.pallas_call(functools.partial(tiles_kernel, [couple_spec(couple) for c...]
    concatenate x1 -> x7, other arithmetic: 0.01 us -> 3.9 us  [the longest x1 1.8 us: gather_pieces(): b = jnp.concatenate([w2, w2s])]
    ppermute x15 -> x12, starting transfers between devices: 7.35 us -> 3.56 us  [swap(): lax.ppermute(v, 'pair', [(i, i ^ 1) for i in range(lax.axis_size('pair'))])]
    unnamed x56 -> x39, local copies, waits for them, and re-layouts: 5.67 us -> 2.97 us
    ppermute x16 -> x14, waiting for transfers between devices: 44.9 us -> 43 us  [hop(): return lax.ppermute(v, ('pair', 'sec'), route)]
    ppermute x15 -> x12, waiting for transfers between devices: 6.51 us -> 7.83 us  [swap(): lax.ppermute(v, 'pair', [(i, i ^ 1) for i in range(lax.axis_size('pair'))])]
    ppermute x16 -> x14, starting transfers between devices: 18.4 us -> 18 us  [hop(): return lax.ppermute(v, ('pair', 'sec'), route)]
  transfers between devices with their start and end apart: 32 -> 27, of which waited for: 13 -> 14; matrix products, arithmetic and copies ran while one was open for 7% -> 9% of each run, Pallas kernels for 0% -> 0%
where the time goes in v2:
time: 121 us; the launch traced here: 120 us
  waiting for transfers between devices  55.9 us (46%)
  Pallas kernels  24.1 us (20%)
  starting transfers between devices  21.9 us (18%)
  local copies, waits for them, and re-layouts  11 us (9%)
  other arithmetic  7.09 us (6%)
    ppermute x14, waiting for transfers between devices, hop(): return lax.ppermute(v, ('pair', 'sec'), route)  43 us
    pallas_call x1, Pallas kernels, per_device(): pl.pallas_call(functools.partial(tiles_kernel, [couple_spec(couple) for c...  21.5 us
    ppermute x14, starting transfers between devices, hop(): return lax.ppermute(v, ('pair', 'sec'), route)  18 us
    ppermute x12, waiting for transfers between devices, swap(): lax.ppermute(v, 'pair', [(i, i ^ 1) for i in range(lax.axis_size('pair'))])  7.83 us
    ppermute x1, waiting for transfers between devices, per_device(): return tiles + lax.ppermute(tiles, 'pair', ring)  5.1 us
    ppermute x12, starting transfers between devices, swap(): lax.ppermute(v, 'pair', [(i, i ^ 1) for i in range(lax.axis_size('pair'))])  3.56 us
    unnamed x39, local copies, waits for them, and re-layouts  2.97 us
    pallas_call x1, Pallas kernels, per_device(): pl.pallas_call(prepare_kernel, out_shape=(jax.ShapeDtypeStruct((N1 + NC,...  2.61 us
  transfers between devices with their start and end apart: 27, of which 14 were waited for; matrix products, arithmetic and copies ran while one was open for 9% of the time, Pallas kernels for 0%

profile of v2, /device:TPU:32, one launch (start us, length us, event | category | flops | bytes accessed | tf_op | source)
XLA Modules:
  0.0 120.3 jit_solution(16672033288565479563)
XLA Ops:
  0.0 0.9 copy.12.here
  1.0 0.7 compare_select_fusion
  1.8 0.7 add_convert_fusion.refs_21_
  2.4 0.7 dynamic-slice_bitcast_fusion
  3.2 0.7 dynamic-slice_bitcast_fusion.1
  3.9 0.6 copy-done.18
  4.5 2.6 %shard_map.82 = (bf16[544,128]{1,0:T(8,128)(2,1)}, bf16[1024,128]{1,0:T(8,128)(2,1)}) custom-call(s32[12]{0:T(128)} %rows.1, bf16[12,128,128]{2,1,0:T(8,128)(2,1)} %psi.1, s32[48,12]{1,0:T(8,128)} %copy-done.17, s32[48,12]{1,0:T(8,128)} %copy-done.18), custom_call_target="tpu_custom_call" | custom-call | tf_op jit(solution)/shard_map/pallas_call | solution.py:288
  7.1 1.9 %collective-permute-start.1 = (bf16[1024,128]{1,0:T(8,128)(2,1)}, bf16[1024,128]{1,0:T(8,128)(2,1)S(1)}, u32[]{:S(2)}, u32[]{:S(2)}) collective-permute-start(bf16[1024,128]{1,0:T(8,128)(2,1)} %get-tuple-element.33), channel_id=1, source_target_pairs={{0,4},{1,5},{2,6},{3,7},{4,8},{5,9},{6,10},{7,11},{8,12},{9,13},{1... | collective-permute-start | bytes 786440 | tf_op jit(solution)/shard_map/ppermute | solution.py:33
  9.0 1.7 %collective-permute-start.2 = (bf16[544,128]{1,0:T(8,128)(2,1)}, bf16[544,128]{1,0:T(8,128)(2,1)S(1)}, u32[]{:S(2)}, u32[]{:S(2)}) collective-permute-start(bf16[544,128]{1,0:T(8,128)(2,1)} %get-tuple-element.34), channel_id=1, source_target_pairs={{0,1},{1,2},{2,3},{3,0},{4,5},{5,6},{6,7},{7,4},{8,9},{9,10},{10,1... | collective-permute-start | bytes 417800 | tf_op jit(solution)/shard_map/ppermute | solution.py:33
  10.7 0.9 constant_dynamic-slice_fusion.2
  11.6 2.9 %collective-permute-start.3 = (bf16[272,128]{1,0:T(8,128)(2,1)S(1)}, bf16[272,128]{1,0:T(8,128)(2,1)S(1)}, u32[]{:S(2)}, u32[]{:S(2)}) collective-permute-start(bf16[272,128]{1,0:T(8,128)(2,1)S(1)} %constant_dynamic-slice_fusion.2), channel_id=1, source_target_pairs={{0,2},{1,3},{2,0},{3,1},{4,6},{5,7},{6,4},{7,5},{8,10},{9,11},{10,... | collective-permute-start | bytes 208904 | tf_op jit(solution)/shard_map/ppermute | solution.py:33
  14.5 1.2 gather_fusion
  15.7 0.7 dynamic-slice_reduce_fusion
  16.4 0.7 concatenate.39.meta
  17.1 1.2 %collective-permute-done.3 = bf16[272,128]{1,0:T(8,128)(2,1)S(1)} collective-permute-done((bf16[272,128]{1,0:T(8,128)(2,1)S(1)}, bf16[272,128]{1,0:T(8,128)(2,1)S(1)}, u32[]{:S(2)}, u32[]{:S(2)}) %collective-permute-start.3) | collective-permute-done | bytes 69664 | tf_op jit(solution)/shard_map/ppermute | solution.py:33
  18.3 2.0 %collective-permute-start.4 = (bf16[1024,128]{1,0:T(8,128)(2,1)S(1)}, bf16[1024,128]{1,0:T(8,128)(2,1)S(1)}, u32[]{:S(2)}, u32[]{:S(2)}) collective-permute-start(bf16[1024,128]{1,0:T(8,128)(2,1)S(1)} %collective-permute-done.1), channel_id=1, source_target_pairs={{0,4},{1,5},{2,6},{3,7},{4,8},{5,9},{6,10},{7,11},{8,12},{9,13},{1... | collective-permute-start | bytes 786440 | tf_op jit(solution)/shard_map/ppermute | solution.py:33
  20.4 1.2 %collective-permute-start.5 = (bf16[1840,128]{1,0:T(8,128)(2,1)S(1)}, bf16[1840,128]{1,0:T(8,128)(2,1)S(1)}, u32[]{:S(2)}, u32[]{:S(2)}) collective-permute-start(bf16[1840,128]{1,0:T(8,128)(2,1)S(1)} %pad_maximum_fusion.6), channel_id=1, source_target_pairs={{0,32},{32,0},{64,96},{96,64},{128,160},{160,128},{192,224},{224,1... | collective-permute-start | bytes 1413128 | tf_op jit(solution)/shard_map/ppermute | solution.py:45
  21.6 1.0 fusion.12
  22.7 2.1 %collective-permute-done.4 = bf16[1024,128]{1,0:T(8,128)(2,1)S(1)} collective-permute-done((bf16[1024,128]{1,0:T(8,128)(2,1)S(1)}, bf16[1024,128]{1,0:T(8,128)(2,1)S(1)}, u32[]{:S(2)}, u32[]{:S(2)}) %collective-permute-start.4) | collective-permute-done | bytes 262176 | tf_op jit(solution)/shard_map/ppermute | solution.py:33
  25.0 0.8 collective-permute-start.8
  25.8 2.6 %collective-permute-start.7 = (bf16[2176,128]{1,0:T(8,128)(2,1)S(1)}, bf16[2176,128]{1,0:T(8,128)(2,1)}, u32[]{:S(2)}, u32[]{:S(2)}) collective-permute-start(bf16[2176,128]{1,0:T(8,128)(2,1)S(1)} %pad_maximum_fusion.4.refs_0_), channel_id=1, source_target_pairs={{0,4},{1,5},{2,6},{3,7},{4,8},{5,9},{6,10},{7,11},{8,12},{9,13},{1... | collective-permute-start | bytes 1671176 | tf_op jit(solution)/shard_map/ppermute | solution.py:33
  28.4 2.5 %collective-permute-start.6 = (bf16[1024,128]{1,0:T(8,128)(2,1)S(1)}, bf16[1024,128]{1,0:T(8,128)(2,1)S(1)}, u32[]{:S(2)}, u32[]{:S(2)}) collective-permute-start(bf16[1024,128]{1,0:T(8,128)(2,1)S(1)} %collective-permute-done.4), channel_id=1, source_target_pairs={{0,4},{1,5},{2,6},{3,7},{4,8},{5,9},{6,10},{7,11},{8,12},{9,13},{1... | collective-permute-start | bytes 786440 | tf_op jit(solution)/shard_map/ppermute | solution.py:33
  30.9 1.9 %collective-permute-start.9 = (bf16[512,128]{1,0:T(8,128)(2,1)S(1)}, bf16[512,128]{1,0:T(8,128)(2,1)S(1)}, u32[]{:S(2)}, u32[]{:S(2)}) collective-permute-start(bf16[512,128]{1,0:T(8,128)(2,1)S(1)} %constant_dynamic-slice_fusion.1), channel_id=1, source_target_pairs={{0,8},{1,9},{2,10},{3,11},{4,12},{5,13},{6,14},{7,15},{8,16},{9,17... | collective-permute-start | bytes 393224 | tf_op jit(solution)/shard_map/ppermute | solution.py:33
  32.9 10.8 %collective-permute-done.9 = bf16[512,128]{1,0:T(8,128)(2,1)S(1)} collective-permute-done((bf16[512,128]{1,0:T(8,128)(2,1)S(1)}, bf16[512,128]{1,0:T(8,128)(2,1)S(1)}, u32[]{:S(2)}, u32[]{:S(2)}) %collective-permute-start.9) | collective-permute-done | bytes 131104 | tf_op jit(solution)/shard_map/ppermute | solution.py:33
  43.7 1.1 slice.53
  44.8 1.0 pad_maximum_fusion.1
  45.8 1.4 %collective-permute-start.12 = (bf16[3584,128]{1,0:T(8,128)(2,1)S(1)}, bf16[3584,128]{1,0:T(8,128)(2,1)S(1)}, u32[]{:S(2)}, u32[]{:S(2)}) collective-permute-start(bf16[3584,128]{1,0:T(8,128)(2,1)S(1)} %pad_maximum_fusion.1), channel_id=1, source_target_pairs={{0,1},{1,2},{2,3},{3,0},{4,5},{5,6},{6,7},{7,4},{8,9},{9,10},{10,1... | collective-permute-start | bytes 2752520 | tf_op jit(solution)/shard_map/ppermute | solution.py:33
  47.2 0.6 collective-permute-start.13
  47.8 2.2 %collective-permute-done.13 = bf16[1536,128]{1,0:T(8,128)(2,1)S(1)} collective-permute-done((bf16[1536,128]{1,0:T(8,128)(2,1)S(1)}, bf16[1536,128]{1,0:T(8,128)(2,1)S(1)}, u32[]{:S(2)}, u32[]{:S(2)}) %collective-permute-start.13) | collective-permute-done | bytes 393248 | tf_op jit(solution)/shard_map/ppermute | solution.py:45
  50.0 7.0 %collective-permute-done.11.refs_10_ = bf16[2176,128]{1,0:T(8,128)(2,1)} collective-permute-done((bf16[2176,128]{1,0:T(8,128)(2,1)}, bf16[2176,128]{1,0:T(8,128)(2,1)}, u32[]{:S(2)}, u32[]{:S(2)}) %collective-permute-start.11) | collective-permute-done | bytes 557088 | tf_op jit(solution)/shard_map/ppermute | solution.py:33
  57.0 3.5 %collective-permute-done.12.refs_8_ = bf16[3584,128]{1,0:T(8,128)(2,1)S(1)} collective-permute-done((bf16[3584,128]{1,0:T(8,128)(2,1)S(1)}, bf16[3584,128]{1,0:T(8,128)(2,1)S(1)}, u32[]{:S(2)}, u32[]{:S(2)}) %collective-permute-start.12) | collective-permute-done | bytes 917536 | tf_op jit(solution)/shard_map/ppermute | solution.py:33
  60.8 0.7 copy-done.3
  61.4 0.5 collective-permute-start.17
  61.9 2.6 %collective-permute-done.17.refs_5_ = bf16[2176,128]{1,0:T(8,128)(2,1)S(1)} collective-permute-done((bf16[2176,128]{1,0:T(8,128)(2,1)}, bf16[2176,128]{1,0:T(8,128)(2,1)S(1)}, u32[]{:S(2)}, u32[]{:S(2)}) %collective-permute-start.17) | collective-permute-done | bytes 557088 | tf_op jit(solution)/shard_map/ppermute | solution.py:45
  64.5 7.1 %collective-permute-done.15.refs_14_ = bf16[2176,128]{1,0:T(8,128)(2,1)S(1)} collective-permute-done((bf16[2176,128]{1,0:T(8,128)(2,1)}, bf16[2176,128]{1,0:T(8,128)(2,1)S(1)}, u32[]{:S(2)}, u32[]{:S(2)}) %collective-permute-start.15) | collective-permute-done | bytes 557088 | tf_op jit(solution)/shard_map/ppermute | solution.py:33
  71.7 5.1 %collective-permute-done.16.refs_12_ = bf16[4096,128]{1,0:T(8,128)(2,1)} collective-permute-done((bf16[4096,128]{1,0:T(8,128)(2,1)S(1)}, bf16[4096,128]{1,0:T(8,128)(2,1)}, u32[]{:S(2)}, u32[]{:S(2)}) %collective-permute-start.16) | collective-permute-done | bytes 1048608 | tf_op jit(solution)/shard_map/ppermute | solution.py:33
  76.8 0.5 collective-permute-start.21
  77.4 1.0 slice.55
  78.7 2.7 %collective-permute-done.21.refs_11_ = bf16[2176,128]{1,0:T(8,128)(2,1)} collective-permute-done((bf16[2176,128]{1,0:T(8,128)(2,1)}, bf16[2176,128]{1,0:T(8,128)(2,1)}, u32[]{:S(2)}, u32[]{:S(2)}) %collective-permute-start.21) | collective-permute-done | bytes 557088 | tf_op jit(solution)/shard_map/ppermute | solution.py:45
  81.4 3.8 %collective-permute-done.19.refs_18_ = bf16[1088,128]{1,0:T(8,128)(2,1)S(1)} collective-permute-done((bf16[1088,128]{1,0:T(8,128)(2,1)S(1)}, bf16[1088,128]{1,0:T(8,128)(2,1)S(1)}, u32[]{:S(2)}, u32[]{:S(2)}) %collective-permute-start.19) | collective-permute-done | bytes 278560 | tf_op jit(solution)/shard_map/ppermute | solution.py:33
  85.2 2.3 %collective-permute-done.20.refs_16_ = bf16[1536,128]{1,0:T(8,128)(2,1)S(1)} collective-permute-done((bf16[1536,128]{1,0:T(8,128)(2,1)S(1)}, bf16[1536,128]{1,0:T(8,128)(2,1)S(1)}, u32[]{:S(2)}, u32[]{:S(2)}) %collective-permute-start.20) | collective-permute-done | bytes 393248 | tf_op jit(solution)/shard_map/ppermute | solution.py:33
  87.6 1.8 %pad_maximum_fusion.5.refs_6_ = bf16[2048,128]{1,0:T(8,128)(2,1)} fusion(bf16[1024,128]{1,0:T(8,128)(2,1)} %collective-permute-done.10, bf16[1024,128]{1,0:T(8,128)(2,1)S(1)} %collective-permute-done.4), kind=kLoop, calls=%fused_computation.6 | loop fusion | flops 1048576 | bytes 1048576 | tf_op jit(solution)/shard_map/concatenate | solution.py:78
  89.4 0.5 collective-permute-start.25
  89.9 0.9 pad_maximum_fusion.3.refs_7_
  91.1 0.7 copy-done.16
  91.8 21.5 %shard_map.83 = f32[3,64,128]{2,1,0:T(8,128)} custom-call(s32[844]{0:T(1024)} %concatenate.39.meta, bf16[2176,128]{1,0:T(8,128)(2,1)} %copy-done.2, bf16[3072,128]{1,0:T(8,128)(2,1)} %copy-done.1, bf16[3072,128]{1,0:T(8,128)(2,1)} %collective-permute-done.8.refs_2_, bf16[3072,128]{1,0:T(8,128)(2,1)} %copy-done.9, ...), custom_call_target="tpu_custom_call" | custom-call | tf_op jit(solution)/shard_map/pallas_call | solution.py:315
  113.7 5.1 %collective-permute-done.26 = f32[3,64,128]{2,1,0:T(8,128)S(1)} collective-permute-done((f32[3,64,128]{2,1,0:T(8,128)}, f32[3,64,128]{2,1,0:T(8,128)S(1)}, u32[]{:S(2)}, u32[]{:S(2)}) %collective-permute-start.26) | collective-permute-done | bytes 98336 | tf_op jit(solution)/shard_map/ppermute | solution.py:337
  118.8 1.5 %add.139 = f32[3,64,128]{2,1,0:T(8,128)} add(f32[3,64,128]{2,1,0:T(8,128)} %shard_map.83, f32[3,64,128]{2,1,0:T(8,128)S(1)} %collective-permute-done.26) | non-fusion elementwise | flops 24576 | bytes 294912 | tf_op jit(solution)/shard_map/add | solution.py:337
  (80 shorter events, 1.8 us)
Async XLA Ops:
  0.0 14.5 %copy-start = (bf16[48,128,128]{2,1,0:T(8,128)(2,1)S(1)}, bf16[48,128,128]{2,1,0:T(8,128)(2,1)}, u32[]{:S(2)}) copy-start(bf16[48,128,128]{2,1,0:T(8,128)(2,1)} %param.10) | copy-start | bytes 4718596
  0.9 3.0 %copy-start.17 = (s32[48,12]{1,0:T(8,128)}, s32[48,12]{1,0:T(8,128)S(1)}, u32[]{:S(2)}) copy-start(s32[48,12]{1,0:T(8,128)S(1)} %copy.12.here) | copy-start | bytes 6916
  0.9 3.0 %collective-permute-start = (s32[48,12]{1,0:T(8,128)S(1)}, s32[48,12]{1,0:T(8,128)S(1)}, u32[]{:S(2)}, u32[]{:S(2)}) collective-permute-start(s32[48,12]{1,0:T(8,128)S(1)} %copy.12.here), channel_id=1, source_target_pairs={{0,32},{32,0},{64,96},{96,64},{128,160},{160,128},{192,224},{224,1... | collective-permute-start | bytes 6920 | tf_op jit(solution)/shard_map/ppermute | solution.py:45
  3.9 0.6 copy-start.18
  7.1 15.5 %copy-start.7 = (bf16[1024,128]{1,0:T(8,128)(2,1)S(1)}, bf16[1024,128]{1,0:T(8,128)(2,1)}, u32[]{:S(2)}) copy-start(bf16[1024,128]{1,0:T(8,128)(2,1)} %get-tuple-element.33) | copy-start | bytes 786436
  7.1 11.2 %collective-permute-start.1 = (bf16[1024,128]{1,0:T(8,128)(2,1)}, bf16[1024,128]{1,0:T(8,128)(2,1)S(1)}, u32[]{:S(2)}, u32[]{:S(2)}) collective-permute-start(bf16[1024,128]{1,0:T(8,128)(2,1)} %get-tuple-element.33), channel_id=1, source_target_pairs={{0,4},{1,5},{2,6},{3,7},{4,8},{5,9},{6,10},{7,11},{8,12},{9,13},{1... | collective-permute-start | bytes 786440 | tf_op jit(solution)/shard_map/ppermute | solution.py:33
  9.0 9.3 %collective-permute-start.2 = (bf16[544,128]{1,0:T(8,128)(2,1)}, bf16[544,128]{1,0:T(8,128)(2,1)S(1)}, u32[]{:S(2)}, u32[]{:S(2)}) collective-permute-start(bf16[544,128]{1,0:T(8,128)(2,1)} %get-tuple-element.34), channel_id=1, source_target_pairs={{0,1},{1,2},{2,3},{3,0},{4,5},{5,6},{6,7},{7,4},{8,9},{9,10},{10,1... | collective-permute-start | bytes 417800 | tf_op jit(solution)/shard_map/ppermute | solution.py:33
  11.6 6.7 %collective-permute-start.3 = (bf16[272,128]{1,0:T(8,128)(2,1)S(1)}, bf16[272,128]{1,0:T(8,128)(2,1)S(1)}, u32[]{:S(2)}, u32[]{:S(2)}) collective-permute-start(bf16[272,128]{1,0:T(8,128)(2,1)S(1)} %constant_dynamic-slice_fusion.2), channel_id=1, source_target_pairs={{0,2},{1,3},{2,0},{3,1},{4,6},{5,7},{6,4},{7,5},{8,10},{9,11},{10,... | collective-permute-start | bytes 208904 | tf_op jit(solution)/shard_map/ppermute | solution.py:33
  18.3 4.3 %copy-start.11 = (bf16[544,128]{1,0:T(8,128)(2,1)}, bf16[544,128]{1,0:T(8,128)(2,1)S(1)}, u32[]{:S(2)}) copy-start(bf16[544,128]{1,0:T(8,128)(2,1)S(1)} %collective-permute-done.2) | copy-start | bytes 417796
  18.3 6.4 %collective-permute-start.4 = (bf16[1024,128]{1,0:T(8,128)(2,1)S(1)}, bf16[1024,128]{1,0:T(8,128)(2,1)S(1)}, u32[]{:S(2)}, u32[]{:S(2)}) collective-permute-start(bf16[1024,128]{1,0:T(8,128)(2,1)S(1)} %collective-permute-done.1), channel_id=1, source_target_pairs={{0,4},{1,5},{2,6},{3,7},{4,8},{5,9},{6,10},{7,11},{8,12},{9,13},{1... | collective-permute-start | bytes 786440 | tf_op jit(solution)/shard_map/ppermute | solution.py:33
  20.4 4.4 %collective-permute-start.5 = (bf16[1840,128]{1,0:T(8,128)(2,1)S(1)}, bf16[1840,128]{1,0:T(8,128)(2,1)S(1)}, u32[]{:S(2)}, u32[]{:S(2)}) collective-permute-start(bf16[1840,128]{1,0:T(8,128)(2,1)S(1)} %pad_maximum_fusion.6), channel_id=1, source_target_pairs={{0,32},{32,0},{64,96},{96,64},{128,160},{160,128},{192,224},{224,1... | collective-permute-start | bytes 1413128 | tf_op jit(solution)/shard_map/ppermute | solution.py:45
  22.7 3.0 %copy-start.12 = (bf16[544,128]{1,0:T(8,128)(2,1)S(1)}, bf16[544,128]{1,0:T(8,128)(2,1)}, u32[]{:S(2)}) copy-start(bf16[544,128]{1,0:T(8,128)(2,1)} %copy-done.11) | copy-start | bytes 417796
  22.7 3.0 %copy-start.14 = (bf16[544,128]{1,0:T(8,128)(2,1)S(1)}, bf16[544,128]{1,0:T(8,128)(2,1)}, u32[]{:S(2)}) copy-start(bf16[544,128]{1,0:T(8,128)(2,1)} %get-tuple-element.34) | copy-start | bytes 417796
  25.0 20.8 %copy-start.1 = (bf16[3072,128]{1,0:T(8,128)(2,1)}, bf16[3072,128]{1,0:T(8,128)(2,1)S(1)}, u32[]{:S(2)}) copy-start(bf16[3072,128]{1,0:T(8,128)(2,1)S(1)} %pad_maximum_fusion.2.refs_1_) | copy-start | bytes 2359300
  25.0 18.7 %collective-permute-start.8 = (bf16[3072,128]{1,0:T(8,128)(2,1)S(1)}, bf16[3072,128]{1,0:T(8,128)(2,1)}, u32[]{:S(2)}, u32[]{:S(2)}) collective-permute-start(bf16[3072,128]{1,0:T(8,128)(2,1)S(1)} %pad_maximum_fusion.2.refs_1_), channel_id=1, source_target_pairs={{0,1},{1,2},{2,3},{3,0},{4,5},{5,6},{6,7},{7,4},{8,9},{9,10},{10,1... | collective-permute-start | bytes 2359304 | tf_op jit(solution)/shard_map/ppermute | solution.py:33
  25.8 21.4 %copy-start.2 = (bf16[2176,128]{1,0:T(8,128)(2,1)}, bf16[2176,128]{1,0:T(8,128)(2,1)S(1)}, u32[]{:S(2)}) copy-start(bf16[2176,128]{1,0:T(8,128)(2,1)S(1)} %pad_maximum_fusion.4.refs_0_) | copy-start | bytes 1671172
  25.8 17.9 %collective-permute-start.7 = (bf16[2176,128]{1,0:T(8,128)(2,1)S(1)}, bf16[2176,128]{1,0:T(8,128)(2,1)}, u32[]{:S(2)}, u32[]{:S(2)}) collective-permute-start(bf16[2176,128]{1,0:T(8,128)(2,1)S(1)} %pad_maximum_fusion.4.refs_0_), channel_id=1, source_target_pairs={{0,4},{1,5},{2,6},{3,7},{4,8},{5,9},{6,10},{7,11},{8,12},{9,13},{1... | collective-permute-start | bytes 1671176 | tf_op jit(solution)/shard_map/ppermute | solution.py:33
  28.4 15.3 %collective-permute-start.10 = (bf16[1024,128]{1,0:T(8,128)(2,1)S(1)}, bf16[1024,128]{1,0:T(8,128)(2,1)}, u32[]{:S(2)}, u32[]{:S(2)}) collective-permute-start(bf16[1024,128]{1,0:T(8,128)(2,1)S(1)} %collective-permute-done.4), channel_id=1, source_target_pairs={{0,32},{32,0},{64,96},{96,64},{128,160},{160,128},{192,224},{224,1... | collective-permute-start | bytes 786440 | tf_op jit(solution)/shard_map/ppermute | solution.py:45
  28.4 15.3 %collective-permute-start.6 = (bf16[1024,128]{1,0:T(8,128)(2,1)S(1)}, bf16[1024,128]{1,0:T(8,128)(2,1)S(1)}, u32[]{:S(2)}, u32[]{:S(2)}) collective-permute-start(bf16[1024,128]{1,0:T(8,128)(2,1)S(1)} %collective-permute-done.4), channel_id=1, source_target_pairs={{0,4},{1,5},{2,6},{3,7},{4,8},{5,9},{6,10},{7,11},{8,12},{9,13},{1... | collective-permute-start | bytes 786440 | tf_op jit(solution)/shard_map/ppermute | solution.py:33
  30.9 12.8 %collective-permute-start.9 = (bf16[512,128]{1,0:T(8,128)(2,1)S(1)}, bf16[512,128]{1,0:T(8,128)(2,1)S(1)}, u32[]{:S(2)}, u32[]{:S(2)}) collective-permute-start(bf16[512,128]{1,0:T(8,128)(2,1)S(1)} %constant_dynamic-slice_fusion.1), channel_id=1, source_target_pairs={{0,8},{1,9},{2,10},{3,11},{4,12},{5,13},{6,14},{7,15},{8,16},{9,17... | collective-permute-start | bytes 393224 | tf_op jit(solution)/shard_map/ppermute | solution.py:33
  43.7 16.8 %copy-start.5 = (bf16[512,128]{1,0:T(8,128)(2,1)}, bf16[512,128]{1,0:T(8,128)(2,1)S(1)}, u32[]{:S(2)}) copy-start(bf16[512,128]{1,0:T(8,128)(2,1)S(1)} %collective-permute-done.9) | copy-start | bytes 393220
  45.8 14.7 %collective-permute-start.12 = (bf16[3584,128]{1,0:T(8,128)(2,1)S(1)}, bf16[3584,128]{1,0:T(8,128)(2,1)S(1)}, u32[]{:S(2)}, u32[]{:S(2)}) collective-permute-start(bf16[3584,128]{1,0:T(8,128)(2,1)S(1)} %pad_maximum_fusion.1), channel_id=1, source_target_pairs={{0,1},{1,2},{2,3},{3,0},{4,5},{5,6},{6,7},{7,4},{8,9},{9,10},{10,1... | collective-permute-start | bytes 2752520 | tf_op jit(solution)/shard_map/ppermute | solution.py:33
  47.2 9.9 %collective-permute-start.14 = (bf16[3072,128]{1,0:T(8,128)(2,1)}, bf16[3072,128]{1,0:T(8,128)(2,1)S(1)}, u32[]{:S(2)}, u32[]{:S(2)}) collective-permute-start(bf16[3072,128]{1,0:T(8,128)(2,1)} %collective-permute-done.8.refs_2_), channel_id=1, source_target_pairs={{0,32},{32,0},{64,96},{96,64},{128,160},{160,128},{192,224},{224,1... | collective-permute-start | bytes 2359304 | tf_op jit(solution)/shard_map/ppermute | solution.py:45
  47.2 9.8 %collective-permute-start.11 = (bf16[2176,128]{1,0:T(8,128)(2,1)}, bf16[2176,128]{1,0:T(8,128)(2,1)}, u32[]{:S(2)}, u32[]{:S(2)}) collective-permute-start(bf16[2176,128]{1,0:T(8,128)(2,1)} %collective-permute-done.7.refs_4_), channel_id=1, source_target_pairs={{0,4},{1,5},{2,6},{3,7},{4,8},{5,9},{6,10},{7,11},{8,12},{9,13},{1... | collective-permute-start | bytes 1671176 | tf_op jit(solution)/shard_map/ppermute | solution.py:33
  47.2 2.8 %collective-permute-start.13 = (bf16[1536,128]{1,0:T(8,128)(2,1)S(1)}, bf16[1536,128]{1,0:T(8,128)(2,1)S(1)}, u32[]{:S(2)}, u32[]{:S(2)}) collective-permute-start(bf16[1536,128]{1,0:T(8,128)(2,1)S(1)} %pad_maximum_fusion.7), channel_id=1, source_target_pairs={{0,32},{32,0},{64,96},{96,64},{128,160},{160,128},{192,224},{224,1... | collective-permute-start | bytes 1179656 | tf_op jit(solution)/shard_map/ppermute | solution.py:45
  57.0 3.5 %copy-start.9 = (bf16[3072,128]{1,0:T(8,128)(2,1)}, bf16[3072,128]{1,0:T(8,128)(2,1)S(1)}, u32[]{:S(2)}) copy-start(bf16[3072,128]{1,0:T(8,128)(2,1)S(1)} %collective-permute-done.14.refs_3_) | copy-start | bytes 2359300
  60.5 0.9 copy-start.3
  60.6 29.3 %copy-start.6 = (bf16[512,128]{1,0:T(8,128)(2,1)S(1)}, bf16[512,128]{1,0:T(8,128)(2,1)}, u32[]{:S(2)}) copy-start(bf16[512,128]{1,0:T(8,128)(2,1)} %copy-done.5) | copy-start | bytes 393220
  60.6 16.2 %collective-permute-start.16 = (bf16[4096,128]{1,0:T(8,128)(2,1)S(1)}, bf16[4096,128]{1,0:T(8,128)(2,1)}, u32[]{:S(2)}, u32[]{:S(2)}) collective-permute-start(bf16[4096,128]{1,0:T(8,128)(2,1)S(1)} %pad_maximum_fusion), channel_id=1, source_target_pairs={{0,1},{1,2},{2,3},{3,0},{4,5},{5,6},{6,7},{7,4},{8,9},{9,10},{10,1... | collective-permute-start | bytes 3145736 | tf_op jit(solution)/shard_map/ppermute | solution.py:33
  61.4 10.3 %collective-permute-start.18 = (bf16[3584,128]{1,0:T(8,128)(2,1)S(1)}, bf16[3584,128]{1,0:T(8,128)(2,1)S(1)}, u32[]{:S(2)}, u32[]{:S(2)}) collective-permute-start(bf16[3584,128]{1,0:T(8,128)(2,1)S(1)} %collective-permute-done.12.refs_8_), channel_id=1, source_target_pairs={{0,32},{32,0},{64,96},{96,64},{128,160},{160,128},{192,224},{224,1... | collective-permute-start | bytes 2752520 | tf_op jit(solution)/shard_map/ppermute | solution.py:45
  61.4 3.1 %collective-permute-start.17 = (bf16[2176,128]{1,0:T(8,128)(2,1)}, bf16[2176,128]{1,0:T(8,128)(2,1)S(1)}, u32[]{:S(2)}, u32[]{:S(2)}) collective-permute-start(bf16[2176,128]{1,0:T(8,128)(2,1)} %collective-permute-done.7.refs_4_), channel_id=1, source_target_pairs={{0,32},{32,0},{64,96},{96,64},{128,160},{160,128},{192,224},{224,1... | collective-permute-start | bytes 1671176 | tf_op jit(solution)/shard_map/ppermute | solution.py:45
  61.9 9.7 %collective-permute-start.15 = (bf16[2176,128]{1,0:T(8,128)(2,1)}, bf16[2176,128]{1,0:T(8,128)(2,1)S(1)}, u32[]{:S(2)}, u32[]{:S(2)}) collective-permute-start(bf16[2176,128]{1,0:T(8,128)(2,1)} %collective-permute-done.11.refs_10_), channel_id=1, source_target_pairs={{0,4},{1,5},{2,6},{3,7},{4,8},{5,9},{6,10},{7,11},{8,12},{9,13},{1... | collective-permute-start | bytes 1671176 | tf_op jit(solution)/shard_map/ppermute | solution.py:33
  64.5 12.8 %copy-start.10 = (bf16[2176,128]{1,0:T(8,128)(2,1)}, bf16[2176,128]{1,0:T(8,128)(2,1)S(1)}, u32[]{:S(2)}) copy-start(bf16[2176,128]{1,0:T(8,128)(2,1)S(1)} %collective-permute-done.17.refs_5_) | copy-start | bytes 1671172
  71.7 19.1 %copy-start.4 = (bf16[2176,128]{1,0:T(8,128)(2,1)}, bf16[2176,128]{1,0:T(8,128)(2,1)S(1)}, u32[]{:S(2)}) copy-start(bf16[2176,128]{1,0:T(8,128)(2,1)S(1)} %collective-permute-done.15.refs_14_) | copy-start | bytes 1671172
  71.7 5.1 %copy-start.8 = (bf16[3584,128]{1,0:T(8,128)(2,1)}, bf16[3584,128]{1,0:T(8,128)(2,1)S(1)}, u32[]{:S(2)}) copy-start(bf16[3584,128]{1,0:T(8,128)(2,1)S(1)} %collective-permute-done.18.refs_9_) | copy-start | bytes 2752516
  76.8 10.7 %collective-permute-start.23 = (bf16[4096,128]{1,0:T(8,128)(2,1)}, bf16[4096,128]{1,0:T(8,128)(2,1)}, u32[]{:S(2)}, u32[]{:S(2)}) collective-permute-start(bf16[4096,128]{1,0:T(8,128)(2,1)} %collective-permute-done.16.refs_12_), channel_id=1, source_target_pairs={{0,32},{32,0},{64,96},{96,64},{128,160},{160,128},{192,224},{224,1... | collective-permute-start | bytes 3145736 | tf_op jit(solution)/shard_map/ppermute | solution.py:45
  76.8 4.6 %collective-permute-start.21 = (bf16[2176,128]{1,0:T(8,128)(2,1)}, bf16[2176,128]{1,0:T(8,128)(2,1)}, u32[]{:S(2)}, u32[]{:S(2)}) collective-permute-start(bf16[2176,128]{1,0:T(8,128)(2,1)} %collective-permute-done.11.refs_10_), channel_id=1, source_target_pairs={{0,32},{32,0},{64,96},{96,64},{128,160},{160,128},{192,224},{224,1... | collective-permute-start | bytes 1671176 | tf_op jit(solution)/shard_map/ppermute | solution.py:45
  77.3 10.2 %collective-permute-start.22 = (bf16[2176,128]{1,0:T(8,128)(2,1)S(1)}, bf16[2176,128]{1,0:T(8,128)(2,1)}, u32[]{:S(2)}, u32[]{:S(2)}) collective-permute-start(bf16[2176,128]{1,0:T(8,128)(2,1)S(1)} %collective-permute-done.15.refs_14_), channel_id=1, source_target_pairs={{0,32},{32,0},{64,96},{96,64},{128,160},{160,128},{192,224},{224,1... | collective-permute-start | bytes 1671176 | tf_op jit(solution)/shard_map/ppermute | solution.py:45
  78.4 9.1 %collective-permute-start.20 = (bf16[1536,128]{1,0:T(8,128)(2,1)S(1)}, bf16[1536,128]{1,0:T(8,128)(2,1)S(1)}, u32[]{:S(2)}, u32[]{:S(2)}) collective-permute-start(bf16[1536,128]{1,0:T(8,128)(2,1)S(1)} %slice.55), channel_id=1, source_target_pairs={{0,1},{1,2},{2,3},{3,0},{4,5},{5,6},{6,7},{7,4},{8,9},{9,10},{10,1... | collective-permute-start | bytes 1179656 | tf_op jit(solution)/shard_map/ppermute | solution.py:33
  78.6 6.6 %collective-permute-start.19 = (bf16[1088,128]{1,0:T(8,128)(2,1)S(1)}, bf16[1088,128]{1,0:T(8,128)(2,1)S(1)}, u32[]{:S(2)}, u32[]{:S(2)}) collective-permute-start(bf16[1088,128]{1,0:T(8,128)(2,1)S(1)} %constant_dynamic-slice_fusion), channel_id=1, source_target_pairs={{0,4},{1,5},{2,6},{3,7},{4,8},{5,9},{6,10},{7,11},{8,12},{9,13},{1... | collective-permute-start | bytes 835592 | tf_op jit(solution)/shard_map/ppermute | solution.py:33
  85.2 5.9 %copy-start.15 = (bf16[1088,128]{1,0:T(8,128)(2,1)}, bf16[1088,128]{1,0:T(8,128)(2,1)S(1)}, u32[]{:S(2)}) copy-start(bf16[1088,128]{1,0:T(8,128)(2,1)S(1)} %collective-permute-done.19.refs_18_) | copy-start | bytes 835588
  87.5 3.6 %copy-start.13 = (bf16[1536,128]{1,0:T(8,128)(2,1)}, bf16[1536,128]{1,0:T(8,128)(2,1)S(1)}, u32[]{:S(2)}) copy-start(bf16[1536,128]{1,0:T(8,128)(2,1)S(1)} %collective-permute-done.20.refs_16_) | copy-start | bytes 1179652
  87.5 3.6 %collective-permute-start.24 = (bf16[1536,128]{1,0:T(8,128)(2,1)S(1)}, bf16[1536,128]{1,0:T(8,128)(2,1)}, u32[]{:S(2)}, u32[]{:S(2)}) collective-permute-start(bf16[1536,128]{1,0:T(8,128)(2,1)S(1)} %collective-permute-done.20.refs_16_), channel_id=1, source_target_pairs={{0,32},{32,0},{64,96},{96,64},{128,160},{160,128},{192,224},{224,1... | collective-permute-start | bytes 1179656 | tf_op jit(solution)/shard_map/ppermute | solution.py:45
  89.4 1.6 %collective-permute-start.25 = (bf16[1088,128]{1,0:T(8,128)(2,1)S(1)}, bf16[1088,128]{1,0:T(8,128)(2,1)S(1)}, u32[]{:S(2)}, u32[]{:S(2)}) collective-permute-start(bf16[1088,128]{1,0:T(8,128)(2,1)S(1)} %collective-permute-done.19.refs_18_), channel_id=1, source_target_pairs={{0,32},{32,0},{64,96},{96,64},{128,160},{160,128},{192,224},{224,1... | collective-permute-start | bytes 835592 | tf_op jit(solution)/shard_map/ppermute | solution.py:45
  91.1 0.7 copy-start.16
  113.3 5.5 %collective-permute-start.26 = (f32[3,64,128]{2,1,0:T(8,128)}, f32[3,64,128]{2,1,0:T(8,128)S(1)}, u32[]{:S(2)}, u32[]{:S(2)}) collective-permute-start(f32[3,64,128]{2,1,0:T(8,128)} %shard_map.83), channel_id=1, source_target_pairs={{224,0},{0,32},{32,64},{64,96},{96,128},{128,160},{160,192},{192,2... | collective-permute-start | bytes 294920 | tf_op jit(solution)/shard_map/ppermute | solution.py:337

commit v3 on v2

--- a/solution.py
+++ b/solution.py
@@ -78,12 +78,12 @@
     b = jnp.concatenate([w2, w2s])
     wc = jnp.concatenate([w3, w4])
     z2, ab, wcs, a1s = zhop(z1), yhop(jnp.concatenate([a1[:ha], b])), swap(wc), swap(a1)
-    z2, ab, wcs, a1s = sync(z2, ab, wcs, a1s)
+    z2, ab, wcs, a1s, b = sync(z2, ab, wcs, a1s, b)
 
     c = jnp.concatenate([wc, wcs])
     hb, hc = b.shape[0] // 2, c.shape[0] // 2
     z3, cb, z1s, abs_ = zhop(z2), yhop(jnp.concatenate([c, ab[ha:ha + hb]])), swap(z1), swap(ab)
-    z3, cb, z1s, abs_ = sync(z3, cb, z1s, abs_)
+    z3, cb, z1s, abs_, c = sync(z3, cb, z1s, abs_, c)
 
     z4, c2 = zhop(lax.dynamic_slice_in_dim(z3, core * n, 2 * n, 0)), yhop(cb[:hc])
     z2s, z3s, cbs = swap(z2), swap(z3), swap(cb)
@@ -107,12 +107,12 @@
     b_seg = rest([(N2, 2, 0, 0), (N2, -2, 0, 0)])
     c_seg = rest([(N2, 3, 0, 0), (h2, 4, 0, h2), (N2, -3, 0, 0), (h2, 4, h2, -h2)])
     couples = [
-        (bundle, None, step(0)), (a, None, a_seg), (a1, a1s, shift(a_seg, 1, 2 * ha)),
-        (z1, z1s, step(1)), (b, None, b_seg), (c, None, c_seg),
-        (ab, abs_, shift(a_seg, 2, ha) + shift(b_seg, 1, 2 * hb, ha)), (z2, z2s, step(2)),
-        (cb, cbs, shift(c_seg, 1, 2 * hc) + shift(b_seg, 2, hb, 2 * hc)), (z3, z3s, step(3)),
+        (bundle, None, step(0)), (a, None, a_seg), (z1, z1s, step(1)), (z2, z2s, step(2)),
+        (z3, z3s, step(3)), (z4, z4s, [(i * n, N1, 4, i, 0, 0, True) for i in range(2)]),
+        (a1, a1s, shift(a_seg, 1, 2 * ha)), (b, None, b_seg), (c, None, c_seg),
+        (ab, abs_, shift(a_seg, 2, ha) + shift(b_seg, 1, 2 * hb, ha)),
+        (cb, cbs, shift(c_seg, 1, 2 * hc) + shift(b_seg, 2, hb, 2 * hc)),
         (c2, c2s, shift(c_seg, 2, hc)),
-        (z4, z4s, [(i * n, N1, 4, i, 0, 0, True) for i in range(2)]),
     ]
     return couples, others
 
@@ -153,24 +153,32 @@
 
     jax.eval_shape(
         trace, jax.ShapeDtypeStruct((N1 + NC, B), BF16), jax.ShapeDtypeStruct((N2, B), BF16))
-    index, places, segs = [], [], []
+    index, names, rows = [], [], []
     for core in (0, 1):
-        at = [(place(seg, core, swapped), seg[1]) for _, segments, swapped, _ in arrays_of(shapes)
-              for seg in segments]
         number = {}
-        for (dz, dy, row), rows in at:
-            if row < N1:
-                number[dz % NZ, dy % NY] = len(number)
-        flat = []
-        for _, v, segments in shapes:
-            left = sectors(segments, core, False)
-            half = len(left) // 2
-            left, right = (left[:half], left[half:]) if v is None else (left, sectors(segments, core, True))
-            flat += [t for p in zip(left, right) for t in p]
+        for _, segments, swapped, _ in arrays_of(shapes):
+            for seg in segments:
+                dz, dy, row = place(seg, core, swapped)
+                if row < N1:
+                    number[dz % NZ, dy % NY] = len(number)
+        flat, held, base = [], [], 0
+        for u, v, segments in shapes:
+            sides = []
+            for w, swapped in ((u, False), (v, True)):
+                if w is not None:
+                    at = [base + seg[0] + q * B for seg in segments for q in range(seg[1] // B)]
+                    sides.append(list(zip(sectors(segments, core, swapped), at)))
+                    base += w.shape[0]
+            if v is None:
+                half = len(sides[0]) // 2
+                sides = [sides[0][:half], sides[0][half:]]
+            for p in zip(*sides):
+                flat += [t for t, _ in p]
+                held += [at for _, at in p]
         index.append([number[t[:2]] * 16 + t[2] for t in flat])
-        places.append(flat)
-        segs.append([p for p, _ in at])
-    return (np.array(t, np.int32) for t in (index, places, segs))
+        names.append(flat)
+        rows.append(held)
+    return (np.array(t, np.int32) for t in (index, names, rows))
 
 
 def prepare_kernel(rows, psi, here, there, first, second):
@@ -206,37 +214,42 @@
 def tiles_kernel(specs, plan, meta, *refs):
     n = len(plan)
     pieces, ops, pick, out = refs[:n], *refs[n:n + 3]
-    psi, halves, turned, words, table, conn, sems, csem = refs[n + 3:]
+    psi, halves, turned, table, conn, sems, csem = refs[n + 3:]
     core = meta[TILES]
     pairs = SLOTS * SEC // 2
-    targets, places, rows_to = TILES + 1, TILES + 1 + 2 * pairs, TILES + 1 + 4 * pairs
+    targets, places, row_of = TILES + 1, TILES + 1 + 2 * pairs, TILES + 1 + 4 * pairs
+    size = [sum(ref.shape[0] for ref, (_, c) in zip(pieces, plan) if c == couple) for couple in range(len(specs))]
 
     def fetch(wanted):
-        number = 0
-        for ref, (segments, couple) in zip(pieces, plan):
-            for r, rows, _, _, row, _, _ in segments:
-                if couple == wanted:
-                    to = pl.ds(pl.multiple_of(meta[rows_to + number], B), rows)
-                    pltpu.make_async_copy(ref.at[pl.ds(r, rows)], psi.at[to], sems.at[couple]).start()
-                number += 1
+        base = 0
+        for ref, (_, couple) in zip(pieces, plan):
+            if couple == wanted:
+                to = psi.at[pl.ds(base, ref.shape[0])]
+                pltpu.make_async_copy(ref, to, sems.at[couple]).start()
+            base += ref.shape[0]
 
     for couple in range(AHEAD):
         fetch(couple)
-    slot = 0
-    for ref, (segments, couple) in zip(pieces, plan):
-        for r, rows, _, _, row, _, _ in segments:
-            if row < N1:
-                at = pl.ds(pl.multiple_of(r + N1 + core * 16, 16), 16)
-                pltpu.make_async_copy(ref.at[at], words.at[slot], csem).start()
-                slot += 1
+
+    def read_connect():
+        words, base = [], 0
+        for ref, (segments, _) in zip(pieces, plan):
+            for r, _, _, _, row, _, _ in segments:
+                if row < N1:
+                    words.append(psi[pl.ds(pl.multiple_of(base + r + N1 + core * 16, 16), 16), :])
+            base += ref.shape[0]
+        values = lax.dot_general(pick[...], jnp.concatenate(words, axis=0), (((1,), (1,)), ((), ())),
+                                 preferred_element_type=F32)
+        table[...] = values.astype(jnp.int32)
+        pltpu.make_async_copy(table, conn, csem).start()
 
     def sector(s):
-        return psi[pl.ds(pl.multiple_of(s * B, B), B), :]
+        return psi[pl.ds(pl.multiple_of(s, 32), B), :]
 
     base = 0
     for couple, (count, batch) in enumerate(specs):
         fetch(couple + AHEAD)
-        rows = psi.at[pl.ds(0, 2 * count * B)]
+        rows = psi.at[pl.ds(0, size[couple])]
         pltpu.make_async_copy(rows, rows, sems.at[couple]).wait()
 
         def some(j, carry, batch=batch, base=base):
@@ -256,12 +269,8 @@
 
         lax.fori_loop(0, count // batch, some, 0)
         base += count
-        if couple == 6:
-            pltpu.make_async_copy(words, words, csem).wait()
-            values = lax.dot_general(pick[...], words[...].reshape(SLOTS * 16, B), (((1,), (1,)), ((), ())),
-            preferred_element_type=F32)
-            table[...] = values.astype(jnp.int32)
-            pltpu.make_async_copy(table, conn, csem).start()
+        if couple == 5:
+            read_connect()
     pltpu.make_async_copy(table, conn, csem).wait()
 
     unroll = 48
@@ -271,7 +280,7 @@
         for u in range(unroll):
             at = j * unroll + u
             for k in range(TILES):
-                left, right = (conn[k, meta[targets + 2 * at + e]] for e in (0, 1))
+                left, right = (meta[row_of + conn[k, meta[targets + 2 * at + e]]] for e in (0, 1))
                 rhs = jnp.concatenate([sector(left), sector(right)], axis=0)
                 sums[k] = sums[k] + jnp.dot(halves[k, at], rhs, preferred_element_type=F32)
         return tuple(sums)
@@ -299,14 +308,11 @@
     pick = jnp.where(lane == mypairs, 16.0, 0.0) + jnp.where(lane == B // 2 + mypairs, 1.0, 0.0)
     pick = pick.astype(BF16)
 
-    index, places, segs = (jnp.asarray(t)[core] for t in tables())
-
-    def slot_of(t):
-        return (zpos + t[:, 0]) % NZ * NY + (ypos + t[:, 1]) % NY
-
-    places = slot_of(places) * SEC + places[:, 2]
-    rows_to = slot_of(segs) * ROWS + segs[:, 2]
-    meta = jnp.concatenate([mytiles, core[None], index, places, rows_to]).astype(jnp.int32)
+    index, names, rows = (jnp.asarray(t)[core] for t in tables())
+    slot = (zpos + names[:, 0]) % NZ * NY + (ypos + names[:, 1]) % NY
+    here = (slot * SEC + names[:, 2])[None, :] == jnp.arange(SLOTS * SEC)[:, None]
+    row_of = jnp.sum(jnp.where(here, rows[None, :], 0), axis=1)
+    meta = jnp.concatenate([mytiles, core[None], index, rows, row_of]).astype(jnp.int32)
     couples, (meta, pick, ops) = gather_pieces(first, second, core, meta, pick, left_ops[mytiles // 2])
 
     arrays = arrays_of(couples)
@@ -321,10 +327,9 @@
             in_specs=[hbm] * len(plan) + [vmem, vmem],
             out_specs=vmem,
             scratch_shapes=[
-                pltpu.VMEM((SLOTS * ROWS, B), BF16),
+                pltpu.VMEM((SLOTS * (ROWS + NC), B), BF16),
                 pltpu.VMEM((TILES, SLOTS * SEC // 2, 64, 2 * B), BF16),
                 pltpu.VMEM((TILES, 16, 64, 2 * B), BF16),
-                pltpu.VMEM((SLOTS, 16, B), BF16),
                 pltpu.VMEM((16, SLOTS * 16), jnp.int32),
                 pltpu.SMEM((16, SLOTS * 16), jnp.int32),
                 pltpu.SemaphoreType.DMA((len(couples),)),

time: 121 us -> 120 us (level)
  local copies, waits for them, and re-layouts: 11 us -> 9.63 us
  waiting for transfers between devices: 55.9 us -> 57.2 us
    ppermute x14, waiting for transfers between devices: 43 us -> 45.4 us  [hop(): return lax.ppermute(v, ('pair', 'sec'), route)]
    ppermute x12, waiting for transfers between devices: 7.83 us -> 6.46 us  [swap(): lax.ppermute(v, 'pair', [(i, i ^ 1) for i in range(lax.axis_size('pair'))])]
    unnamed x39 -> x37, local copies, waits for them, and re-layouts: 2.97 us -> 2.28 us
where the time goes in v3:
time: 120 us; the launch traced here: 119 us
  waiting for transfers between devices  57.2 us (48%)
  Pallas kernels  23.2 us (19%)
  starting transfers between devices  21.9 us (18%)
  local copies, waits for them, and re-layouts  9.63 us (8%)
  other arithmetic  7.2 us (6%)
    ppermute x14, waiting for transfers between devices, hop(): return lax.ppermute(v, ('pair', 'sec'), route)  45.4 us
    pallas_call x1, Pallas kernels, per_device(): pl.pallas_call(functools.partial(tiles_kernel, [couple_spec(couple) for c...  20.6 us
    ppermute x14, starting transfers between devices, hop(): return lax.ppermute(v, ('pair', 'sec'), route)  18.1 us
    ppermute x12, waiting for transfers between devices, swap(): lax.ppermute(v, 'pair', [(i, i ^ 1) for i in range(lax.axis_size('pair'))])  6.46 us
    ppermute x1, waiting for transfers between devices, per_device(): return tiles + lax.ppermute(tiles, 'pair', ring)  5.33 us
    ppermute x12, starting transfers between devices, swap(): lax.ppermute(v, 'pair', [(i, i ^ 1) for i in range(lax.axis_size('pair'))])  3.62 us
    pallas_call x1, Pallas kernels, per_device(): pl.pallas_call(prepare_kernel, out_shape=(jax.ShapeDtypeStruct((N1 + NC,...  2.6 us
  transfers between devices with their start and end apart: 27, of which 14 were waited for; matrix products, arithmetic and copies ran while one was open for 9% of the time, Pallas kernels for 0%

profile of v3, /device:TPU:32, one launch (start us, length us, event | category | flops | bytes accessed | tf_op | source)
XLA Modules:
  0.0 119.5 jit_solution(6143808772238350436)
XLA Ops:
  0.0 0.9 copy.14.here
  1.0 0.7 compare_select_fusion
  1.8 0.7 dynamic-slice_bitcast_fusion
  2.5 0.7 add_convert_fusion.refs_21_
  3.2 0.6 copy-done.17
  3.8 2.6 %shard_map.82 = (bf16[544,128]{1,0:T(8,128)(2,1)}, bf16[1024,128]{1,0:T(8,128)(2,1)}) custom-call(s32[12]{0:T(128)} %rows.1, bf16[12,128,128]{2,1,0:T(8,128)(2,1)} %psi.1, s32[48,12]{1,0:T(8,128)} %copy-done.16, s32[48,12]{1,0:T(8,128)} %copy-done.17), custom_call_target="tpu_custom_call" | custom-call | tf_op jit(solution)/shard_map/pallas_call | solution.py:297
  6.4 1.9 %collective-permute-start.1 = (bf16[1024,128]{1,0:T(8,128)(2,1)}, bf16[1024,128]{1,0:T(8,128)(2,1)S(1)}, u32[]{:S(2)}, u32[]{:S(2)}) collective-permute-start(bf16[1024,128]{1,0:T(8,128)(2,1)} %get-tuple-element.35), channel_id=1, source_target_pairs={{0,4},{1,5},{2,6},{3,7},{4,8},{5,9},{6,10},{7,11},{8,12},{9,13},{1... | collective-permute-start | bytes 786440 | tf_op jit(solution)/shard_map/ppermute | solution.py:33
  8.3 1.2 %gather_fusion = bf16[3,128,128]{2,1,0:T(8,128)(2,1)} fusion(bf16[48,128,128]{2,1,0:T(8,128)(2,1)S(1)} %copy-done, s32[1024]{0:T(1024)S(1)} %pad_clamp_fusion), kind=kCustom, calls=%fused_computation | custom fusion | bytes 196620 | tf_op jit(solution)/shard_map/gather | solution.py:316
  9.5 0.7 dynamic-slice_reduce_fusion
  10.2 1.7 %collective-permute-start.2 = (bf16[544,128]{1,0:T(8,128)(2,1)}, bf16[544,128]{1,0:T(8,128)(2,1)S(1)}, u32[]{:S(2)}, u32[]{:S(2)}) collective-permute-start(bf16[544,128]{1,0:T(8,128)(2,1)} %get-tuple-element.36), channel_id=1, source_target_pairs={{0,1},{1,2},{2,3},{3,0},{4,5},{5,6},{6,7},{7,4},{8,9},{9,10},{10,1... | collective-permute-start | bytes 417800 | tf_op jit(solution)/shard_map/ppermute | solution.py:33
  11.9 0.9 constant_dynamic-slice_fusion.2
  12.8 2.9 %collective-permute-start.3 = (bf16[272,128]{1,0:T(8,128)(2,1)S(1)}, bf16[272,128]{1,0:T(8,128)(2,1)S(1)}, u32[]{:S(2)}, u32[]{:S(2)}) collective-permute-start(bf16[272,128]{1,0:T(8,128)(2,1)S(1)} %constant_dynamic-slice_fusion.2), channel_id=1, source_target_pairs={{0,2},{1,3},{2,0},{3,1},{4,6},{5,7},{6,4},{7,5},{8,10},{9,11},{10,... | collective-permute-start | bytes 208904 | tf_op jit(solution)/shard_map/ppermute | solution.py:33
  15.9 0.7 concatenate.39.meta
  16.5 3.0 %collective-permute-done.3 = bf16[272,128]{1,0:T(8,128)(2,1)S(1)} collective-permute-done((bf16[272,128]{1,0:T(8,128)(2,1)S(1)}, bf16[272,128]{1,0:T(8,128)(2,1)S(1)}, u32[]{:S(2)}, u32[]{:S(2)}) %collective-permute-start.3) | collective-permute-done | bytes 69664 | tf_op jit(solution)/shard_map/ppermute | solution.py:33
  19.5 2.0 %collective-permute-start.4 = (bf16[1024,128]{1,0:T(8,128)(2,1)S(1)}, bf16[1024,128]{1,0:T(8,128)(2,1)S(1)}, u32[]{:S(2)}, u32[]{:S(2)}) collective-permute-start(bf16[1024,128]{1,0:T(8,128)(2,1)S(1)} %collective-permute-done.1), channel_id=1, source_target_pairs={{0,4},{1,5},{2,6},{3,7},{4,8},{5,9},{6,10},{7,11},{8,12},{9,13},{1... | collective-permute-start | bytes 786440 | tf_op jit(solution)/shard_map/ppermute | solution.py:33
  21.6 1.2 %collective-permute-start.5 = (bf16[1840,128]{1,0:T(8,128)(2,1)S(1)}, bf16[1840,128]{1,0:T(8,128)(2,1)S(1)}, u32[]{:S(2)}, u32[]{:S(2)}) collective-permute-start(bf16[1840,128]{1,0:T(8,128)(2,1)S(1)} %pad_maximum_fusion.6), channel_id=1, source_target_pairs={{0,32},{32,0},{64,96},{96,64},{128,160},{160,128},{192,224},{224,1... | collective-permute-start | bytes 1413128 | tf_op jit(solution)/shard_map/ppermute | solution.py:45
  22.8 1.0 fusion.8
  23.9 2.1 %collective-permute-done.4 = bf16[1024,128]{1,0:T(8,128)(2,1)S(1)} collective-permute-done((bf16[1024,128]{1,0:T(8,128)(2,1)S(1)}, bf16[1024,128]{1,0:T(8,128)(2,1)S(1)}, u32[]{:S(2)}, u32[]{:S(2)}) %collective-permute-start.4) | collective-permute-done | bytes 262176 | tf_op jit(solution)/shard_map/ppermute | solution.py:33
  26.2 0.8 collective-permute-start.8
  27.0 2.6 %collective-permute-start.7 = (bf16[2176,128]{1,0:T(8,128)(2,1)S(1)}, bf16[2176,128]{1,0:T(8,128)(2,1)}, u32[]{:S(2)}, u32[]{:S(2)}) collective-permute-start(bf16[2176,128]{1,0:T(8,128)(2,1)S(1)} %pad_maximum_fusion.4.refs_0_), channel_id=1, source_target_pairs={{0,4},{1,5},{2,6},{3,7},{4,8},{5,9},{6,10},{7,11},{8,12},{9,13},{1... | collective-permute-start | bytes 1671176 | tf_op jit(solution)/shard_map/ppermute | solution.py:33
  29.6 2.5 %collective-permute-start.6 = (bf16[1024,128]{1,0:T(8,128)(2,1)S(1)}, bf16[1024,128]{1,0:T(8,128)(2,1)S(1)}, u32[]{:S(2)}, u32[]{:S(2)}) collective-permute-start(bf16[1024,128]{1,0:T(8,128)(2,1)S(1)} %collective-permute-done.4), channel_id=1, source_target_pairs={{0,4},{1,5},{2,6},{3,7},{4,8},{5,9},{6,10},{7,11},{8,12},{9,13},{1... | collective-permute-start | bytes 786440 | tf_op jit(solution)/shard_map/ppermute | solution.py:33
  32.1 1.9 %collective-permute-start.9 = (bf16[512,128]{1,0:T(8,128)(2,1)S(1)}, bf16[512,128]{1,0:T(8,128)(2,1)S(1)}, u32[]{:S(2)}, u32[]{:S(2)}) collective-permute-start(bf16[512,128]{1,0:T(8,128)(2,1)S(1)} %constant_dynamic-slice_fusion.1), channel_id=1, source_target_pairs={{0,8},{1,9},{2,10},{3,11},{4,12},{5,13},{6,14},{7,15},{8,16},{9,17... | collective-permute-start | bytes 393224 | tf_op jit(solution)/shard_map/ppermute | solution.py:33
  34.0 10.8 %collective-permute-done.9 = bf16[512,128]{1,0:T(8,128)(2,1)S(1)} collective-permute-done((bf16[512,128]{1,0:T(8,128)(2,1)S(1)}, bf16[512,128]{1,0:T(8,128)(2,1)S(1)}, u32[]{:S(2)}, u32[]{:S(2)}) %collective-permute-start.9) | collective-permute-done | bytes 131104 | tf_op jit(solution)/shard_map/ppermute | solution.py:33
  44.9 1.0 slice.41
  45.9 1.0 pad_maximum_fusion.1
  47.0 1.4 %collective-permute-start.12 = (bf16[3584,128]{1,0:T(8,128)(2,1)S(1)}, bf16[3584,128]{1,0:T(8,128)(2,1)S(1)}, u32[]{:S(2)}, u32[]{:S(2)}) collective-permute-start(bf16[3584,128]{1,0:T(8,128)(2,1)S(1)} %pad_maximum_fusion.1), channel_id=1, source_target_pairs={{0,1},{1,2},{2,3},{3,0},{4,5},{5,6},{6,7},{7,4},{8,9},{9,10},{10,1... | collective-permute-start | bytes 2752520 | tf_op jit(solution)/shard_map/ppermute | solution.py:33
  48.4 0.6 collective-permute-start.13
  49.0 1.8 %pad_maximum_fusion.5.refs_12_ = bf16[2048,128]{1,0:T(8,128)(2,1)} fusion(bf16[1024,128]{1,0:T(8,128)(2,1)} %collective-permute-done.10, bf16[1024,128]{1,0:T(8,128)(2,1)S(1)} %collective-permute-done.4), kind=kLoop, calls=%fused_computation.8 | loop fusion | flops 1048576 | bytes 1048576 | tf_op jit(solution)/shard_map/concatenate | solution.py:78
  50.7 0.4 collective-permute-done.13
  51.2 7.0 %collective-permute-done.11.refs_4_ = bf16[2176,128]{1,0:T(8,128)(2,1)} collective-permute-done((bf16[2176,128]{1,0:T(8,128)(2,1)}, bf16[2176,128]{1,0:T(8,128)(2,1)}, u32[]{:S(2)}, u32[]{:S(2)}) %collective-permute-start.11) | collective-permute-done | bytes 557088 | tf_op jit(solution)/shard_map/ppermute | solution.py:33
  58.2 3.5 %collective-permute-done.12.refs_14_ = bf16[3584,128]{1,0:T(8,128)(2,1)S(1)} collective-permute-done((bf16[3584,128]{1,0:T(8,128)(2,1)S(1)}, bf16[3584,128]{1,0:T(8,128)(2,1)S(1)}, u32[]{:S(2)}, u32[]{:S(2)}) %collective-permute-start.12) | collective-permute-done | bytes 917536 | tf_op jit(solution)/shard_map/ppermute | solution.py:33
  61.8 0.3 collective-permute-start.16
  62.1 0.5 collective-permute-start.17
  62.6 0.9 pad_maximum_fusion.3.refs_13_
  63.6 2.0 %collective-permute-done.17.refs_3_ = bf16[2176,128]{1,0:T(8,128)(2,1)S(1)} collective-permute-done((bf16[2176,128]{1,0:T(8,128)(2,1)}, bf16[2176,128]{1,0:T(8,128)(2,1)S(1)}, u32[]{:S(2)}, u32[]{:S(2)}) %collective-permute-start.17) | collective-permute-done | bytes 557088 | tf_op jit(solution)/shard_map/ppermute | solution.py:45
  65.6 6.8 %collective-permute-done.15.refs_6_ = bf16[2176,128]{1,0:T(8,128)(2,1)S(1)} collective-permute-done((bf16[2176,128]{1,0:T(8,128)(2,1)}, bf16[2176,128]{1,0:T(8,128)(2,1)S(1)}, u32[]{:S(2)}, u32[]{:S(2)}) %collective-permute-start.15) | collective-permute-done | bytes 557088 | tf_op jit(solution)/shard_map/ppermute | solution.py:33
  72.4 5.8 %collective-permute-done.16.refs_16_ = bf16[4096,128]{1,0:T(8,128)(2,1)} collective-permute-done((bf16[4096,128]{1,0:T(8,128)(2,1)S(1)}, bf16[4096,128]{1,0:T(8,128)(2,1)}, u32[]{:S(2)}, u32[]{:S(2)}) %collective-permute-start.16) | collective-permute-done | bytes 1048608 | tf_op jit(solution)/shard_map/ppermute | solution.py:33
  78.1 0.5 collective-permute-start.21
  78.7 1.0 slice.43
  80.0 2.4 %collective-permute-done.21.refs_5_ = bf16[2176,128]{1,0:T(8,128)(2,1)} collective-permute-done((bf16[2176,128]{1,0:T(8,128)(2,1)}, bf16[2176,128]{1,0:T(8,128)(2,1)}, u32[]{:S(2)}, u32[]{:S(2)}) %collective-permute-start.21) | collective-permute-done | bytes 557088 | tf_op jit(solution)/shard_map/ppermute | solution.py:45
  82.4 4.2 %collective-permute-done.19.refs_8_ = bf16[1088,128]{1,0:T(8,128)(2,1)S(1)} collective-permute-done((bf16[1088,128]{1,0:T(8,128)(2,1)S(1)}, bf16[1088,128]{1,0:T(8,128)(2,1)S(1)}, u32[]{:S(2)}, u32[]{:S(2)}) %collective-permute-start.19) | collective-permute-done | bytes 278560 | tf_op jit(solution)/shard_map/ppermute | solution.py:33
  86.5 2.3 %collective-permute-done.20.refs_18_ = bf16[1536,128]{1,0:T(8,128)(2,1)S(1)} collective-permute-done((bf16[1536,128]{1,0:T(8,128)(2,1)S(1)}, bf16[1536,128]{1,0:T(8,128)(2,1)S(1)}, u32[]{:S(2)}, u32[]{:S(2)}) %collective-permute-start.20) | collective-permute-done | bytes 393248 | tf_op jit(solution)/shard_map/ppermute | solution.py:33
  88.9 0.5 collective-permute-start.24
  89.4 1.6 %collective-permute-done.24.refs_9_ = bf16[1088,128]{1,0:T(8,128)(2,1)S(1)} collective-permute-done((bf16[1088,128]{1,0:T(8,128)(2,1)S(1)}, bf16[1088,128]{1,0:T(8,128)(2,1)S(1)}, u32[]{:S(2)}, u32[]{:S(2)}) %collective-permute-start.24) | collective-permute-done | bytes 278560 | tf_op jit(solution)/shard_map/ppermute | solution.py:45
  91.1 0.7 copy-done.15
  91.8 20.6 %shard_map.83 = f32[3,64,128]{2,1,0:T(8,128)} custom-call(s32[1156]{0:T(1024)} %concatenate.39.meta, bf16[2176,128]{1,0:T(8,128)(2,1)} %copy-done.2, bf16[3072,128]{1,0:T(8,128)(2,1)} %copy-done.1, bf16[2176,128]{1,0:T(8,128)(2,1)} %collective-permute-done.7.refs_2_, bf16[2176,128]{1,0:T(8,128)(2,1)} %copy-done.11, ...), custom_call_target="tpu_custom_call" | custom-call | tf_op jit(solution)/shard_map/pallas_call | solution.py:321
  112.6 5.3 %collective-permute-done.26 = f32[3,64,128]{2,1,0:T(8,128)S(1)} collective-permute-done((f32[3,64,128]{2,1,0:T(8,128)}, f32[3,64,128]{2,1,0:T(8,128)S(1)}, u32[]{:S(2)}, u32[]{:S(2)}) %collective-permute-start.26) | collective-permute-done | bytes 98336 | tf_op jit(solution)/shard_map/ppermute | solution.py:342
  117.9 1.5 %add.119 = f32[3,64,128]{2,1,0:T(8,128)} add(f32[3,64,128]{2,1,0:T(8,128)} %shard_map.83, f32[3,64,128]{2,1,0:T(8,128)S(1)} %collective-permute-done.26) | non-fusion elementwise | flops 24576 | bytes 294912 | tf_op jit(solution)/shard_map/add | solution.py:342
  (77 shorter events, 1.3 us)
Async XLA Ops:
  0.0 8.3 %copy-start = (bf16[48,128,128]{2,1,0:T(8,128)(2,1)S(1)}, bf16[48,128,128]{2,1,0:T(8,128)(2,1)}, u32[]{:S(2)}) copy-start(bf16[48,128,128]{2,1,0:T(8,128)(2,1)} %param.10) | copy-start | bytes 4718596
  0.9 2.3 %copy-start.16 = (s32[48,12]{1,0:T(8,128)}, s32[48,12]{1,0:T(8,128)S(1)}, u32[]{:S(2)}) copy-start(s32[48,12]{1,0:T(8,128)S(1)} %copy.14.here) | copy-start | bytes 6916
  0.9 2.3 %collective-permute-start = (s32[48,12]{1,0:T(8,128)S(1)}, s32[48,12]{1,0:T(8,128)S(1)}, u32[]{:S(2)}, u32[]{:S(2)}) collective-permute-start(s32[48,12]{1,0:T(8,128)S(1)} %copy.14.here), channel_id=1, source_target_pairs={{0,32},{32,0},{64,96},{96,64},{128,160},{160,128},{192,224},{224,1... | collective-permute-start | bytes 6920 | tf_op jit(solution)/shard_map/ppermute | solution.py:45
  3.2 0.6 copy-start.17
  6.4 17.4 %copy-start.5 = (bf16[1024,128]{1,0:T(8,128)(2,1)S(1)}, bf16[1024,128]{1,0:T(8,128)(2,1)}, u32[]{:S(2)}) copy-start(bf16[1024,128]{1,0:T(8,128)(2,1)} %get-tuple-element.35) | copy-start | bytes 786436
  6.4 13.1 %collective-permute-start.1 = (bf16[1024,128]{1,0:T(8,128)(2,1)}, bf16[1024,128]{1,0:T(8,128)(2,1)S(1)}, u32[]{:S(2)}, u32[]{:S(2)}) collective-permute-start(bf16[1024,128]{1,0:T(8,128)(2,1)} %get-tuple-element.35), channel_id=1, source_target_pairs={{0,4},{1,5},{2,6},{3,7},{4,8},{5,9},{6,10},{7,11},{8,12},{9,13},{1... | collective-permute-start | bytes 786440 | tf_op jit(solution)/shard_map/ppermute | solution.py:33
  10.2 9.3 %collective-permute-start.2 = (bf16[544,128]{1,0:T(8,128)(2,1)}, bf16[544,128]{1,0:T(8,128)(2,1)S(1)}, u32[]{:S(2)}, u32[]{:S(2)}) collective-permute-start(bf16[544,128]{1,0:T(8,128)(2,1)} %get-tuple-element.36), channel_id=1, source_target_pairs={{0,1},{1,2},{2,3},{3,0},{4,5},{5,6},{6,7},{7,4},{8,9},{9,10},{10,1... | collective-permute-start | bytes 417800 | tf_op jit(solution)/shard_map/ppermute | solution.py:33
  12.8 6.7 %collective-permute-start.3 = (bf16[272,128]{1,0:T(8,128)(2,1)S(1)}, bf16[272,128]{1,0:T(8,128)(2,1)S(1)}, u32[]{:S(2)}, u32[]{:S(2)}) collective-permute-start(bf16[272,128]{1,0:T(8,128)(2,1)S(1)} %constant_dynamic-slice_fusion.2), channel_id=1, source_target_pairs={{0,2},{1,3},{2,0},{3,1},{4,6},{5,7},{6,4},{7,5},{8,10},{9,11},{10,... | collective-permute-start | bytes 208904 | tf_op jit(solution)/shard_map/ppermute | solution.py:33
  19.5 4.3 %copy-start.9 = (bf16[544,128]{1,0:T(8,128)(2,1)}, bf16[544,128]{1,0:T(8,128)(2,1)S(1)}, u32[]{:S(2)}) copy-start(bf16[544,128]{1,0:T(8,128)(2,1)S(1)} %collective-permute-done.2) | copy-start | bytes 417796
  19.5 6.4 %collective-permute-start.4 = (bf16[1024,128]{1,0:T(8,128)(2,1)S(1)}, bf16[1024,128]{1,0:T(8,128)(2,1)S(1)}, u32[]{:S(2)}, u32[]{:S(2)}) collective-permute-start(bf16[1024,128]{1,0:T(8,128)(2,1)S(1)} %collective-permute-done.1), channel_id=1, source_target_pairs={{0,4},{1,5},{2,6},{3,7},{4,8},{5,9},{6,10},{7,11},{8,12},{9,13},{1... | collective-permute-start | bytes 786440 | tf_op jit(solution)/shard_map/ppermute | solution.py:33
  21.6 4.4 %collective-permute-start.5 = (bf16[1840,128]{1,0:T(8,128)(2,1)S(1)}, bf16[1840,128]{1,0:T(8,128)(2,1)S(1)}, u32[]{:S(2)}, u32[]{:S(2)}) collective-permute-start(bf16[1840,128]{1,0:T(8,128)(2,1)S(1)} %pad_maximum_fusion.6), channel_id=1, source_target_pairs={{0,32},{32,0},{64,96},{96,64},{128,160},{160,128},{192,224},{224,1... | collective-permute-start | bytes 1413128 | tf_op jit(solution)/shard_map/ppermute | solution.py:45
  23.9 3.0 %copy-start.10 = (bf16[544,128]{1,0:T(8,128)(2,1)S(1)}, bf16[544,128]{1,0:T(8,128)(2,1)}, u32[]{:S(2)}) copy-start(bf16[544,128]{1,0:T(8,128)(2,1)} %copy-done.9) | copy-start | bytes 417796
  23.9 3.0 %copy-start.13 = (bf16[544,128]{1,0:T(8,128)(2,1)S(1)}, bf16[544,128]{1,0:T(8,128)(2,1)}, u32[]{:S(2)}) copy-start(bf16[544,128]{1,0:T(8,128)(2,1)} %get-tuple-element.36) | copy-start | bytes 417796
  26.1 20.8 %copy-start.1 = (bf16[3072,128]{1,0:T(8,128)(2,1)}, bf16[3072,128]{1,0:T(8,128)(2,1)S(1)}, u32[]{:S(2)}) copy-start(bf16[3072,128]{1,0:T(8,128)(2,1)S(1)} %pad_maximum_fusion.2.refs_1_) | copy-start | bytes 2359300
  26.2 18.8 %collective-permute-start.8 = (bf16[3072,128]{1,0:T(8,128)(2,1)S(1)}, bf16[3072,128]{1,0:T(8,128)(2,1)}, u32[]{:S(2)}, u32[]{:S(2)}) collective-permute-start(bf16[3072,128]{1,0:T(8,128)(2,1)S(1)} %pad_maximum_fusion.2.refs_1_), channel_id=1, source_target_pairs={{0,1},{1,2},{2,3},{3,0},{4,5},{5,6},{6,7},{7,4},{8,9},{9,10},{10,1... | collective-permute-start | bytes 2359304 | tf_op jit(solution)/shard_map/ppermute | solution.py:33
  27.0 21.4 %copy-start.2 = (bf16[2176,128]{1,0:T(8,128)(2,1)}, bf16[2176,128]{1,0:T(8,128)(2,1)S(1)}, u32[]{:S(2)}) copy-start(bf16[2176,128]{1,0:T(8,128)(2,1)S(1)} %pad_maximum_fusion.4.refs_0_) | copy-start | bytes 1671172
  27.0 17.9 %collective-permute-start.7 = (bf16[2176,128]{1,0:T(8,128)(2,1)S(1)}, bf16[2176,128]{1,0:T(8,128)(2,1)}, u32[]{:S(2)}, u32[]{:S(2)}) collective-permute-start(bf16[2176,128]{1,0:T(8,128)(2,1)S(1)} %pad_maximum_fusion.4.refs_0_), channel_id=1, source_target_pairs={{0,4},{1,5},{2,6},{3,7},{4,8},{5,9},{6,10},{7,11},{8,12},{9,13},{1... | collective-permute-start | bytes 1671176 | tf_op jit(solution)/shard_map/ppermute | solution.py:33
  29.6 15.3 %collective-permute-start.10 = (bf16[1024,128]{1,0:T(8,128)(2,1)S(1)}, bf16[1024,128]{1,0:T(8,128)(2,1)}, u32[]{:S(2)}, u32[]{:S(2)}) collective-permute-start(bf16[1024,128]{1,0:T(8,128)(2,1)S(1)} %collective-permute-done.4), channel_id=1, source_target_pairs={{0,32},{32,0},{64,96},{96,64},{128,160},{160,128},{192,224},{224,1... | collective-permute-start | bytes 786440 | tf_op jit(solution)/shard_map/ppermute | solution.py:45
  29.6 15.3 %collective-permute-start.6 = (bf16[1024,128]{1,0:T(8,128)(2,1)S(1)}, bf16[1024,128]{1,0:T(8,128)(2,1)S(1)}, u32[]{:S(2)}, u32[]{:S(2)}) collective-permute-start(bf16[1024,128]{1,0:T(8,128)(2,1)S(1)} %collective-permute-done.4), channel_id=1, source_target_pairs={{0,4},{1,5},{2,6},{3,7},{4,8},{5,9},{6,10},{7,11},{8,12},{9,13},{1... | collective-permute-start | bytes 786440 | tf_op jit(solution)/shard_map/ppermute | solution.py:33
  32.1 12.8 %collective-permute-start.9 = (bf16[512,128]{1,0:T(8,128)(2,1)S(1)}, bf16[512,128]{1,0:T(8,128)(2,1)S(1)}, u32[]{:S(2)}, u32[]{:S(2)}) collective-permute-start(bf16[512,128]{1,0:T(8,128)(2,1)S(1)} %constant_dynamic-slice_fusion.1), channel_id=1, source_target_pairs={{0,8},{1,9},{2,10},{3,11},{4,12},{5,13},{6,14},{7,15},{8,16},{9,17... | collective-permute-start | bytes 393224 | tf_op jit(solution)/shard_map/ppermute | solution.py:33
  47.0 14.7 %collective-permute-start.12 = (bf16[3584,128]{1,0:T(8,128)(2,1)S(1)}, bf16[3584,128]{1,0:T(8,128)(2,1)S(1)}, u32[]{:S(2)}, u32[]{:S(2)}) collective-permute-start(bf16[3584,128]{1,0:T(8,128)(2,1)S(1)} %pad_maximum_fusion.1), channel_id=1, source_target_pairs={{0,1},{1,2},{2,3},{3,0},{4,5},{5,6},{6,7},{7,4},{8,9},{9,10},{10,1... | collective-permute-start | bytes 2752520 | tf_op jit(solution)/shard_map/ppermute | solution.py:33
  48.3 9.9 %collective-permute-start.14 = (bf16[3072,128]{1,0:T(8,128)(2,1)}, bf16[3072,128]{1,0:T(8,128)(2,1)S(1)}, u32[]{:S(2)}, u32[]{:S(2)}) collective-permute-start(bf16[3072,128]{1,0:T(8,128)(2,1)} %collective-permute-done.8.refs_10_), channel_id=1, source_target_pairs={{0,32},{32,0},{64,96},{96,64},{128,160},{160,128},{192,224},{224,1... | collective-permute-start | bytes 2359304 | tf_op jit(solution)/shard_map/ppermute | solution.py:45
  48.3 9.8 %collective-permute-start.11 = (bf16[2176,128]{1,0:T(8,128)(2,1)}, bf16[2176,128]{1,0:T(8,128)(2,1)}, u32[]{:S(2)}, u32[]{:S(2)}) collective-permute-start(bf16[2176,128]{1,0:T(8,128)(2,1)} %collective-permute-done.7.refs_2_), channel_id=1, source_target_pairs={{0,4},{1,5},{2,6},{3,7},{4,8},{5,9},{6,10},{7,11},{8,12},{9,13},{1... | collective-permute-start | bytes 1671176 | tf_op jit(solution)/shard_map/ppermute | solution.py:33
  48.4 2.8 %collective-permute-start.13 = (bf16[1536,128]{1,0:T(8,128)(2,1)S(1)}, bf16[1536,128]{1,0:T(8,128)(2,1)S(1)}, u32[]{:S(2)}, u32[]{:S(2)}) collective-permute-start(bf16[1536,128]{1,0:T(8,128)(2,1)S(1)} %pad_maximum_fusion.7), channel_id=1, source_target_pairs={{0,32},{32,0},{64,96},{96,64},{128,160},{160,128},{192,224},{224,1... | collective-permute-start | bytes 1179656 | tf_op jit(solution)/shard_map/ppermute | solution.py:45
  58.2 3.5 %copy-start.8 = (bf16[3072,128]{1,0:T(8,128)(2,1)}, bf16[3072,128]{1,0:T(8,128)(2,1)S(1)}, u32[]{:S(2)}) copy-start(bf16[3072,128]{1,0:T(8,128)(2,1)S(1)} %collective-permute-done.14.refs_11_) | copy-start | bytes 2359300
  61.6 1.9 %copy-start.3 = (bf16[3584,128]{1,0:T(8,128)(2,1)}, bf16[3584,128]{1,0:T(8,128)(2,1)S(1)}, u32[]{:S(2)}) copy-start(bf16[3584,128]{1,0:T(8,128)(2,1)S(1)} %collective-permute-done.12.refs_14_) | copy-start | bytes 2752516
  61.8 16.4 %collective-permute-start.16 = (bf16[4096,128]{1,0:T(8,128)(2,1)S(1)}, bf16[4096,128]{1,0:T(8,128)(2,1)}, u32[]{:S(2)}, u32[]{:S(2)}) collective-permute-start(bf16[4096,128]{1,0:T(8,128)(2,1)S(1)} %pad_maximum_fusion), channel_id=1, source_target_pairs={{0,1},{1,2},{2,3},{3,0},{4,5},{5,6},{6,7},{7,4},{8,9},{9,10},{10,1... | collective-permute-start | bytes 3145736 | tf_op jit(solution)/shard_map/ppermute | solution.py:33
  62.1 10.3 %collective-permute-start.18 = (bf16[3584,128]{1,0:T(8,128)(2,1)S(1)}, bf16[3584,128]{1,0:T(8,128)(2,1)S(1)}, u32[]{:S(2)}, u32[]{:S(2)}) collective-permute-start(bf16[3584,128]{1,0:T(8,128)(2,1)S(1)} %collective-permute-done.12.refs_14_), channel_id=1, source_target_pairs={{0,32},{32,0},{64,96},{96,64},{128,160},{160,128},{192,224},{224,1... | collective-permute-start | bytes 2752520 | tf_op jit(solution)/shard_map/ppermute | solution.py:45
  62.1 3.5 %collective-permute-start.17 = (bf16[2176,128]{1,0:T(8,128)(2,1)}, bf16[2176,128]{1,0:T(8,128)(2,1)S(1)}, u32[]{:S(2)}, u32[]{:S(2)}) collective-permute-start(bf16[2176,128]{1,0:T(8,128)(2,1)} %collective-permute-done.7.refs_2_), channel_id=1, source_target_pairs={{0,32},{32,0},{64,96},{96,64},{128,160},{160,128},{192,224},{224,1... | collective-permute-start | bytes 1671176 | tf_op jit(solution)/shard_map/ppermute | solution.py:45
  62.6 9.7 %collective-permute-start.15 = (bf16[2176,128]{1,0:T(8,128)(2,1)}, bf16[2176,128]{1,0:T(8,128)(2,1)S(1)}, u32[]{:S(2)}, u32[]{:S(2)}) collective-permute-start(bf16[2176,128]{1,0:T(8,128)(2,1)} %collective-permute-done.11.refs_4_), channel_id=1, source_target_pairs={{0,4},{1,5},{2,6},{3,7},{4,8},{5,9},{6,10},{7,11},{8,12},{9,13},{1... | collective-permute-start | bytes 1671176 | tf_op jit(solution)/shard_map/ppermute | solution.py:33
  65.6 13.0 %copy-start.11 = (bf16[2176,128]{1,0:T(8,128)(2,1)}, bf16[2176,128]{1,0:T(8,128)(2,1)S(1)}, u32[]{:S(2)}) copy-start(bf16[2176,128]{1,0:T(8,128)(2,1)S(1)} %collective-permute-done.17.refs_3_) | copy-start | bytes 1671172
  72.4 19.4 %copy-start.4 = (bf16[2176,128]{1,0:T(8,128)(2,1)}, bf16[2176,128]{1,0:T(8,128)(2,1)S(1)}, u32[]{:S(2)}) copy-start(bf16[2176,128]{1,0:T(8,128)(2,1)S(1)} %collective-permute-done.15.refs_6_) | copy-start | bytes 1671172
  72.4 5.8 %copy-start.7 = (bf16[3584,128]{1,0:T(8,128)(2,1)}, bf16[3584,128]{1,0:T(8,128)(2,1)S(1)}, u32[]{:S(2)}) copy-start(bf16[3584,128]{1,0:T(8,128)(2,1)S(1)} %collective-permute-done.18.refs_15_) | copy-start | bytes 2752516
  78.1 10.7 %collective-permute-start.23 = (bf16[4096,128]{1,0:T(8,128)(2,1)}, bf16[4096,128]{1,0:T(8,128)(2,1)S(1)}, u32[]{:S(2)}, u32[]{:S(2)}) collective-permute-start(bf16[4096,128]{1,0:T(8,128)(2,1)} %collective-permute-done.16.refs_16_), channel_id=1, source_target_pairs={{0,32},{32,0},{64,96},{96,64},{128,160},{160,128},{192,224},{224,1... | collective-permute-start | bytes 3145736 | tf_op jit(solution)/shard_map/ppermute | solution.py:45
  78.1 4.2 %collective-permute-start.21 = (bf16[2176,128]{1,0:T(8,128)(2,1)}, bf16[2176,128]{1,0:T(8,128)(2,1)}, u32[]{:S(2)}, u32[]{:S(2)}) collective-permute-start(bf16[2176,128]{1,0:T(8,128)(2,1)} %collective-permute-done.11.refs_4_), channel_id=1, source_target_pairs={{0,32},{32,0},{64,96},{96,64},{128,160},{160,128},{192,224},{224,1... | collective-permute-start | bytes 1671176 | tf_op jit(solution)/shard_map/ppermute | solution.py:45
  78.6 10.2 %collective-permute-start.22 = (bf16[2176,128]{1,0:T(8,128)(2,1)S(1)}, bf16[2176,128]{1,0:T(8,128)(2,1)}, u32[]{:S(2)}, u32[]{:S(2)}) collective-permute-start(bf16[2176,128]{1,0:T(8,128)(2,1)S(1)} %collective-permute-done.15.refs_6_), channel_id=1, source_target_pairs={{0,32},{32,0},{64,96},{96,64},{128,160},{160,128},{192,224},{224,1... | collective-permute-start | bytes 1671176 | tf_op jit(solution)/shard_map/ppermute | solution.py:45
  79.8 9.1 %collective-permute-start.20 = (bf16[1536,128]{1,0:T(8,128)(2,1)S(1)}, bf16[1536,128]{1,0:T(8,128)(2,1)S(1)}, u32[]{:S(2)}, u32[]{:S(2)}) collective-permute-start(bf16[1536,128]{1,0:T(8,128)(2,1)S(1)} %slice.43), channel_id=1, source_target_pairs={{0,1},{1,2},{2,3},{3,0},{4,5},{5,6},{6,7},{7,4},{8,9},{9,10},{10,1... | collective-permute-start | bytes 1179656 | tf_op jit(solution)/shard_map/ppermute | solution.py:33
  79.9 6.6 %collective-permute-start.19 = (bf16[1088,128]{1,0:T(8,128)(2,1)S(1)}, bf16[1088,128]{1,0:T(8,128)(2,1)S(1)}, u32[]{:S(2)}, u32[]{:S(2)}) collective-permute-start(bf16[1088,128]{1,0:T(8,128)(2,1)S(1)} %constant_dynamic-slice_fusion), channel_id=1, source_target_pairs={{0,4},{1,5},{2,6},{3,7},{4,8},{5,9},{6,10},{7,11},{8,12},{9,13},{1... | collective-permute-start | bytes 835592 | tf_op jit(solution)/shard_map/ppermute | solution.py:33
  86.5 5.3 %copy-start.14 = (bf16[1088,128]{1,0:T(8,128)(2,1)}, bf16[1088,128]{1,0:T(8,128)(2,1)S(1)}, u32[]{:S(2)}) copy-start(bf16[1088,128]{1,0:T(8,128)(2,1)S(1)} %collective-permute-done.19.refs_8_) | copy-start | bytes 835588
  88.8 3.0 %copy-start.12 = (bf16[1536,128]{1,0:T(8,128)(2,1)}, bf16[1536,128]{1,0:T(8,128)(2,1)S(1)}, u32[]{:S(2)}) copy-start(bf16[1536,128]{1,0:T(8,128)(2,1)S(1)} %collective-permute-done.20.refs_18_) | copy-start | bytes 1179652
  88.8 3.0 %copy-start.6 = (bf16[4096,128]{1,0:T(8,128)(2,1)}, bf16[4096,128]{1,0:T(8,128)(2,1)S(1)}, u32[]{:S(2)}) copy-start(bf16[4096,128]{1,0:T(8,128)(2,1)S(1)} %collective-permute-done.23.refs_17_) | copy-start | bytes 3145732
  88.8 2.9 %collective-permute-start.25 = (bf16[1536,128]{1,0:T(8,128)(2,1)S(1)}, bf16[1536,128]{1,0:T(8,128)(2,1)}, u32[]{:S(2)}, u32[]{:S(2)}) collective-permute-start(bf16[1536,128]{1,0:T(8,128)(2,1)S(1)} %collective-permute-done.20.refs_18_), channel_id=1, source_target_pairs={{0,32},{32,0},{64,96},{96,64},{128,160},{160,128},{192,224},{224,1... | collective-permute-start | bytes 1179656 | tf_op jit(solution)/shard_map/ppermute | solution.py:45
  88.9 2.1 %collective-permute-start.24 = (bf16[1088,128]{1,0:T(8,128)(2,1)S(1)}, bf16[1088,128]{1,0:T(8,128)(2,1)S(1)}, u32[]{:S(2)}, u32[]{:S(2)}) collective-permute-start(bf16[1088,128]{1,0:T(8,128)(2,1)S(1)} %collective-permute-done.19.refs_8_), channel_id=1, source_target_pairs={{0,32},{32,0},{64,96},{96,64},{128,160},{160,128},{192,224},{224,1... | collective-permute-start | bytes 835592 | tf_op jit(solution)/shard_map/ppermute | solution.py:45
  91.1 0.7 copy-start.15
  112.5 5.5 %collective-permute-start.26 = (f32[3,64,128]{2,1,0:T(8,128)}, f32[3,64,128]{2,1,0:T(8,128)S(1)}, u32[]{:S(2)}, u32[]{:S(2)}) collective-permute-start(f32[3,64,128]{2,1,0:T(8,128)} %shard_map.83), channel_id=1, source_target_pairs={{224,0},{0,32},{32,64},{64,96},{96,128},{128,160},{160,192},{192,2... | collective-permute-start | bytes 294920 | tf_op jit(solution)/shard_map/ppermute | solution.py:342

commit v4 on v3

--- a/solution.py
+++ b/solution.py
@@ -18,7 +18,7 @@
 NC = 32
 TILES = 3
 VMEM_LIMIT = 60 * 2**20
-AHEAD = 2
+AHEAD = 4
 F32, BF16 = jnp.float32, jnp.bfloat16
 
 

time: 120 us -> 120 us (level)
  no operation moved by 1% of the time
where the time goes in v4:
time: 120 us; the launch traced here: 119 us
  waiting for transfers between devices  57.2 us (48%)
  Pallas kernels  23.3 us (19%)
  starting transfers between devices  21.9 us (18%)
  local copies, waits for them, and re-layouts  9.63 us (8%)
  other arithmetic  7.2 us (6%)
    ppermute x14, waiting for transfers between devices, hop(): return lax.ppermute(v, ('pair', 'sec'), route)  45.4 us
    pallas_call x1, Pallas kernels, per_device(): pl.pallas_call(functools.partial(tiles_kernel, [couple_spec(couple) for c...  20.7 us
    ppermute x14, starting transfers between devices, hop(): return lax.ppermute(v, ('pair', 'sec'), route)  18.1 us
    ppermute x12, waiting for transfers between devices, swap(): lax.ppermute(v, 'pair', [(i, i ^ 1) for i in range(lax.axis_size('pair'))])  6.46 us
    ppermute x1, waiting for transfers between devices, per_device(): return tiles + lax.ppermute(tiles, 'pair', ring)  5.34 us
    ppermute x12, starting transfers between devices, swap(): lax.ppermute(v, 'pair', [(i, i ^ 1) for i in range(lax.axis_size('pair'))])  3.62 us
    pallas_call x1, Pallas kernels, per_device(): pl.pallas_call(prepare_kernel, out_shape=(jax.ShapeDtypeStruct((N1 + NC,...  2.6 us
  transfers between devices with their start and end apart: 27, of which 14 were waited for; matrix products, arithmetic and copies ran while one was open for 9% of the time, Pallas kernels for 0%

profile of v4, /device:TPU:32, one launch (start us, length us, event | category | flops | bytes accessed | tf_op | source)
XLA Modules:
  0.0 119.5 jit_solution(7484496628919833788)
XLA Ops:
  0.0 0.9 copy.14.here
  1.0 0.7 compare_select_fusion
  1.8 0.7 dynamic-slice_bitcast_fusion
  2.5 0.7 add_convert_fusion.refs_21_
  3.2 0.6 copy-done.17
  3.8 2.6 %shard_map.82 = (bf16[544,128]{1,0:T(8,128)(2,1)}, bf16[1024,128]{1,0:T(8,128)(2,1)}) custom-call(s32[12]{0:T(128)} %rows.1, bf16[12,128,128]{2,1,0:T(8,128)(2,1)} %psi.1, s32[48,12]{1,0:T(8,128)} %copy-done.16, s32[48,12]{1,0:T(8,128)} %copy-done.17), custom_call_target="tpu_custom_call" | custom-call | tf_op jit(solution)/shard_map/pallas_call | solution.py:297
  6.4 1.9 %collective-permute-start.1 = (bf16[1024,128]{1,0:T(8,128)(2,1)}, bf16[1024,128]{1,0:T(8,128)(2,1)S(1)}, u32[]{:S(2)}, u32[]{:S(2)}) collective-permute-start(bf16[1024,128]{1,0:T(8,128)(2,1)} %get-tuple-element.35), channel_id=1, source_target_pairs={{0,4},{1,5},{2,6},{3,7},{4,8},{5,9},{6,10},{7,11},{8,12},{9,13},{1... | collective-permute-start | bytes 786440 | tf_op jit(solution)/shard_map/ppermute | solution.py:33
  8.3 1.2 %gather_fusion = bf16[3,128,128]{2,1,0:T(8,128)(2,1)} fusion(bf16[48,128,128]{2,1,0:T(8,128)(2,1)S(1)} %copy-done, s32[1024]{0:T(1024)S(1)} %pad_clamp_fusion), kind=kCustom, calls=%fused_computation | custom fusion | bytes 196620 | tf_op jit(solution)/shard_map/gather | solution.py:316
  9.5 0.7 dynamic-slice_reduce_fusion
  10.2 1.7 %collective-permute-start.2 = (bf16[544,128]{1,0:T(8,128)(2,1)}, bf16[544,128]{1,0:T(8,128)(2,1)S(1)}, u32[]{:S(2)}, u32[]{:S(2)}) collective-permute-start(bf16[544,128]{1,0:T(8,128)(2,1)} %get-tuple-element.36), channel_id=1, source_target_pairs={{0,1},{1,2},{2,3},{3,0},{4,5},{5,6},{6,7},{7,4},{8,9},{9,10},{10,1... | collective-permute-start | bytes 417800 | tf_op jit(solution)/shard_map/ppermute | solution.py:33
  11.9 0.9 constant_dynamic-slice_fusion.2
  12.8 2.9 %collective-permute-start.3 = (bf16[272,128]{1,0:T(8,128)(2,1)S(1)}, bf16[272,128]{1,0:T(8,128)(2,1)S(1)}, u32[]{:S(2)}, u32[]{:S(2)}) collective-permute-start(bf16[272,128]{1,0:T(8,128)(2,1)S(1)} %constant_dynamic-slice_fusion.2), channel_id=1, source_target_pairs={{0,2},{1,3},{2,0},{3,1},{4,6},{5,7},{6,4},{7,5},{8,10},{9,11},{10,... | collective-permute-start | bytes 208904 | tf_op jit(solution)/shard_map/ppermute | solution.py:33
  15.9 0.7 concatenate.39.meta
  16.5 3.0 %collective-permute-done.3 = bf16[272,128]{1,0:T(8,128)(2,1)S(1)} collective-permute-done((bf16[272,128]{1,0:T(8,128)(2,1)S(1)}, bf16[272,128]{1,0:T(8,128)(2,1)S(1)}, u32[]{:S(2)}, u32[]{:S(2)}) %collective-permute-start.3) | collective-permute-done | bytes 69664 | tf_op jit(solution)/shard_map/ppermute | solution.py:33
  19.5 2.0 %collective-permute-start.4 = (bf16[1024,128]{1,0:T(8,128)(2,1)S(1)}, bf16[1024,128]{1,0:T(8,128)(2,1)S(1)}, u32[]{:S(2)}, u32[]{:S(2)}) collective-permute-start(bf16[1024,128]{1,0:T(8,128)(2,1)S(1)} %collective-permute-done.1), channel_id=1, source_target_pairs={{0,4},{1,5},{2,6},{3,7},{4,8},{5,9},{6,10},{7,11},{8,12},{9,13},{1... | collective-permute-start | bytes 786440 | tf_op jit(solution)/shard_map/ppermute | solution.py:33
  21.6 1.2 %collective-permute-start.5 = (bf16[1840,128]{1,0:T(8,128)(2,1)S(1)}, bf16[1840,128]{1,0:T(8,128)(2,1)S(1)}, u32[]{:S(2)}, u32[]{:S(2)}) collective-permute-start(bf16[1840,128]{1,0:T(8,128)(2,1)S(1)} %pad_maximum_fusion.6), channel_id=1, source_target_pairs={{0,32},{32,0},{64,96},{96,64},{128,160},{160,128},{192,224},{224,1... | collective-permute-start | bytes 1413128 | tf_op jit(solution)/shard_map/ppermute | solution.py:45
  22.8 1.0 fusion.8
  23.9 2.1 %collective-permute-done.4 = bf16[1024,128]{1,0:T(8,128)(2,1)S(1)} collective-permute-done((bf16[1024,128]{1,0:T(8,128)(2,1)S(1)}, bf16[1024,128]{1,0:T(8,128)(2,1)S(1)}, u32[]{:S(2)}, u32[]{:S(2)}) %collective-permute-start.4) | collective-permute-done | bytes 262176 | tf_op jit(solution)/shard_map/ppermute | solution.py:33
  26.2 0.8 collective-permute-start.8
  27.0 2.6 %collective-permute-start.7 = (bf16[2176,128]{1,0:T(8,128)(2,1)S(1)}, bf16[2176,128]{1,0:T(8,128)(2,1)}, u32[]{:S(2)}, u32[]{:S(2)}) collective-permute-start(bf16[2176,128]{1,0:T(8,128)(2,1)S(1)} %pad_maximum_fusion.4.refs_0_), channel_id=1, source_target_pairs={{0,4},{1,5},{2,6},{3,7},{4,8},{5,9},{6,10},{7,11},{8,12},{9,13},{1... | collective-permute-start | bytes 1671176 | tf_op jit(solution)/shard_map/ppermute | solution.py:33
  29.6 2.5 %collective-permute-start.6 = (bf16[1024,128]{1,0:T(8,128)(2,1)S(1)}, bf16[1024,128]{1,0:T(8,128)(2,1)S(1)}, u32[]{:S(2)}, u32[]{:S(2)}) collective-permute-start(bf16[1024,128]{1,0:T(8,128)(2,1)S(1)} %collective-permute-done.4), channel_id=1, source_target_pairs={{0,4},{1,5},{2,6},{3,7},{4,8},{5,9},{6,10},{7,11},{8,12},{9,13},{1... | collective-permute-start | bytes 786440 | tf_op jit(solution)/shard_map/ppermute | solution.py:33
  32.1 1.9 %collective-permute-start.9 = (bf16[512,128]{1,0:T(8,128)(2,1)S(1)}, bf16[512,128]{1,0:T(8,128)(2,1)S(1)}, u32[]{:S(2)}, u32[]{:S(2)}) collective-permute-start(bf16[512,128]{1,0:T(8,128)(2,1)S(1)} %constant_dynamic-slice_fusion.1), channel_id=1, source_target_pairs={{0,8},{1,9},{2,10},{3,11},{4,12},{5,13},{6,14},{7,15},{8,16},{9,17... | collective-permute-start | bytes 393224 | tf_op jit(solution)/shard_map/ppermute | solution.py:33
  34.0 10.8 %collective-permute-done.9 = bf16[512,128]{1,0:T(8,128)(2,1)S(1)} collective-permute-done((bf16[512,128]{1,0:T(8,128)(2,1)S(1)}, bf16[512,128]{1,0:T(8,128)(2,1)S(1)}, u32[]{:S(2)}, u32[]{:S(2)}) %collective-permute-start.9) | collective-permute-done | bytes 131104 | tf_op jit(solution)/shard_map/ppermute | solution.py:33
  44.9 1.0 slice.41
  45.9 1.0 pad_maximum_fusion.1
  47.0 1.4 %collective-permute-start.12 = (bf16[3584,128]{1,0:T(8,128)(2,1)S(1)}, bf16[3584,128]{1,0:T(8,128)(2,1)S(1)}, u32[]{:S(2)}, u32[]{:S(2)}) collective-permute-start(bf16[3584,128]{1,0:T(8,128)(2,1)S(1)} %pad_maximum_fusion.1), channel_id=1, source_target_pairs={{0,1},{1,2},{2,3},{3,0},{4,5},{5,6},{6,7},{7,4},{8,9},{9,10},{10,1... | collective-permute-start | bytes 2752520 | tf_op jit(solution)/shard_map/ppermute | solution.py:33
  48.4 0.6 collective-permute-start.13
  49.0 1.8 %pad_maximum_fusion.5.refs_12_ = bf16[2048,128]{1,0:T(8,128)(2,1)} fusion(bf16[1024,128]{1,0:T(8,128)(2,1)} %collective-permute-done.10, bf16[1024,128]{1,0:T(8,128)(2,1)S(1)} %collective-permute-done.4), kind=kLoop, calls=%fused_computation.8 | loop fusion | flops 1048576 | bytes 1048576 | tf_op jit(solution)/shard_map/concatenate | solution.py:78
  50.7 0.4 collective-permute-done.13
  51.2 7.0 %collective-permute-done.11.refs_4_ = bf16[2176,128]{1,0:T(8,128)(2,1)} collective-permute-done((bf16[2176,128]{1,0:T(8,128)(2,1)}, bf16[2176,128]{1,0:T(8,128)(2,1)}, u32[]{:S(2)}, u32[]{:S(2)}) %collective-permute-start.11) | collective-permute-done | bytes 557088 | tf_op jit(solution)/shard_map/ppermute | solution.py:33
  58.2 3.5 %collective-permute-done.12.refs_14_ = bf16[3584,128]{1,0:T(8,128)(2,1)S(1)} collective-permute-done((bf16[3584,128]{1,0:T(8,128)(2,1)S(1)}, bf16[3584,128]{1,0:T(8,128)(2,1)S(1)}, u32[]{:S(2)}, u32[]{:S(2)}) %collective-permute-start.12) | collective-permute-done | bytes 917536 | tf_op jit(solution)/shard_map/ppermute | solution.py:33
  61.8 0.3 collective-permute-start.16
  62.1 0.5 collective-permute-start.17
  62.6 0.9 pad_maximum_fusion.3.refs_13_
  63.6 2.0 %collective-permute-done.17.refs_3_ = bf16[2176,128]{1,0:T(8,128)(2,1)S(1)} collective-permute-done((bf16[2176,128]{1,0:T(8,128)(2,1)}, bf16[2176,128]{1,0:T(8,128)(2,1)S(1)}, u32[]{:S(2)}, u32[]{:S(2)}) %collective-permute-start.17) | collective-permute-done | bytes 557088 | tf_op jit(solution)/shard_map/ppermute | solution.py:45
  65.6 6.8 %collective-permute-done.15.refs_6_ = bf16[2176,128]{1,0:T(8,128)(2,1)S(1)} collective-permute-done((bf16[2176,128]{1,0:T(8,128)(2,1)}, bf16[2176,128]{1,0:T(8,128)(2,1)S(1)}, u32[]{:S(2)}, u32[]{:S(2)}) %collective-permute-start.15) | collective-permute-done | bytes 557088 | tf_op jit(solution)/shard_map/ppermute | solution.py:33
  72.4 5.8 %collective-permute-done.16.refs_16_ = bf16[4096,128]{1,0:T(8,128)(2,1)} collective-permute-done((bf16[4096,128]{1,0:T(8,128)(2,1)S(1)}, bf16[4096,128]{1,0:T(8,128)(2,1)}, u32[]{:S(2)}, u32[]{:S(2)}) %collective-permute-start.16) | collective-permute-done | bytes 1048608 | tf_op jit(solution)/shard_map/ppermute | solution.py:33
  78.1 0.5 collective-permute-start.21
  78.7 1.0 slice.43
  80.0 2.4 %collective-permute-done.21.refs_5_ = bf16[2176,128]{1,0:T(8,128)(2,1)} collective-permute-done((bf16[2176,128]{1,0:T(8,128)(2,1)}, bf16[2176,128]{1,0:T(8,128)(2,1)}, u32[]{:S(2)}, u32[]{:S(2)}) %collective-permute-start.21) | collective-permute-done | bytes 557088 | tf_op jit(solution)/shard_map/ppermute | solution.py:45
  82.4 4.2 %collective-permute-done.19.refs_8_ = bf16[1088,128]{1,0:T(8,128)(2,1)S(1)} collective-permute-done((bf16[1088,128]{1,0:T(8,128)(2,1)S(1)}, bf16[1088,128]{1,0:T(8,128)(2,1)S(1)}, u32[]{:S(2)}, u32[]{:S(2)}) %collective-permute-start.19) | collective-permute-done | bytes 278560 | tf_op jit(solution)/shard_map/ppermute | solution.py:33
  86.5 2.3 %collective-permute-done.20.refs_18_ = bf16[1536,128]{1,0:T(8,128)(2,1)S(1)} collective-permute-done((bf16[1536,128]{1,0:T(8,128)(2,1)S(1)}, bf16[1536,128]{1,0:T(8,128)(2,1)S(1)}, u32[]{:S(2)}, u32[]{:S(2)}) %collective-permute-start.20) | collective-permute-done | bytes 393248 | tf_op jit(solution)/shard_map/ppermute | solution.py:33
  88.9 0.5 collective-permute-start.24
  89.4 1.6 %collective-permute-done.24.refs_9_ = bf16[1088,128]{1,0:T(8,128)(2,1)S(1)} collective-permute-done((bf16[1088,128]{1,0:T(8,128)(2,1)S(1)}, bf16[1088,128]{1,0:T(8,128)(2,1)S(1)}, u32[]{:S(2)}, u32[]{:S(2)}) %collective-permute-start.24) | collective-permute-done | bytes 278560 | tf_op jit(solution)/shard_map/ppermute | solution.py:45
  91.1 0.7 copy-done.15
  91.8 20.7 %shard_map.83 = f32[3,64,128]{2,1,0:T(8,128)} custom-call(s32[1156]{0:T(1024)} %concatenate.39.meta, bf16[2176,128]{1,0:T(8,128)(2,1)} %copy-done.2, bf16[3072,128]{1,0:T(8,128)(2,1)} %copy-done.1, bf16[2176,128]{1,0:T(8,128)(2,1)} %collective-permute-done.7.refs_2_, bf16[2176,128]{1,0:T(8,128)(2,1)} %copy-done.11, ...), custom_call_target="tpu_custom_call" | custom-call | tf_op jit(solution)/shard_map/pallas_call | solution.py:321
  112.6 5.3 %collective-permute-done.26 = f32[3,64,128]{2,1,0:T(8,128)S(1)} collective-permute-done((f32[3,64,128]{2,1,0:T(8,128)}, f32[3,64,128]{2,1,0:T(8,128)S(1)}, u32[]{:S(2)}, u32[]{:S(2)}) %collective-permute-start.26) | collective-permute-done | bytes 98336 | tf_op jit(solution)/shard_map/ppermute | solution.py:342
  117.9 1.5 %add.119 = f32[3,64,128]{2,1,0:T(8,128)} add(f32[3,64,128]{2,1,0:T(8,128)} %shard_map.83, f32[3,64,128]{2,1,0:T(8,128)S(1)} %collective-permute-done.26) | non-fusion elementwise | flops 24576 | bytes 294912 | tf_op jit(solution)/shard_map/add | solution.py:342
  (77 shorter events, 1.3 us)
Async XLA Ops:
  0.0 8.3 %copy-start = (bf16[48,128,128]{2,1,0:T(8,128)(2,1)S(1)}, bf16[48,128,128]{2,1,0:T(8,128)(2,1)}, u32[]{:S(2)}) copy-start(bf16[48,128,128]{2,1,0:T(8,128)(2,1)} %param.10) | copy-start | bytes 4718596
  0.9 2.3 %copy-start.16 = (s32[48,12]{1,0:T(8,128)}, s32[48,12]{1,0:T(8,128)S(1)}, u32[]{:S(2)}) copy-start(s32[48,12]{1,0:T(8,128)S(1)} %copy.14.here) | copy-start | bytes 6916
  0.9 2.3 %collective-permute-start = (s32[48,12]{1,0:T(8,128)S(1)}, s32[48,12]{1,0:T(8,128)S(1)}, u32[]{:S(2)}, u32[]{:S(2)}) collective-permute-start(s32[48,12]{1,0:T(8,128)S(1)} %copy.14.here), channel_id=1, source_target_pairs={{0,32},{32,0},{64,96},{96,64},{128,160},{160,128},{192,224},{224,1... | collective-permute-start | bytes 6920 | tf_op jit(solution)/shard_map/ppermute | solution.py:45
  3.2 0.6 copy-start.17
  6.4 17.4 %copy-start.5 = (bf16[1024,128]{1,0:T(8,128)(2,1)S(1)}, bf16[1024,128]{1,0:T(8,128)(2,1)}, u32[]{:S(2)}) copy-start(bf16[1024,128]{1,0:T(8,128)(2,1)} %get-tuple-element.35) | copy-start | bytes 786436
  6.4 13.1 %collective-permute-start.1 = (bf16[1024,128]{1,0:T(8,128)(2,1)}, bf16[1024,128]{1,0:T(8,128)(2,1)S(1)}, u32[]{:S(2)}, u32[]{:S(2)}) collective-permute-start(bf16[1024,128]{1,0:T(8,128)(2,1)} %get-tuple-element.35), channel_id=1, source_target_pairs={{0,4},{1,5},{2,6},{3,7},{4,8},{5,9},{6,10},{7,11},{8,12},{9,13},{1... | collective-permute-start | bytes 786440 | tf_op jit(solution)/shard_map/ppermute | solution.py:33
  10.2 9.3 %collective-permute-start.2 = (bf16[544,128]{1,0:T(8,128)(2,1)}, bf16[544,128]{1,0:T(8,128)(2,1)S(1)}, u32[]{:S(2)}, u32[]{:S(2)}) collective-permute-start(bf16[544,128]{1,0:T(8,128)(2,1)} %get-tuple-element.36), channel_id=1, source_target_pairs={{0,1},{1,2},{2,3},{3,0},{4,5},{5,6},{6,7},{7,4},{8,9},{9,10},{10,1... | collective-permute-start | bytes 417800 | tf_op jit(solution)/shard_map/ppermute | solution.py:33
  12.8 6.7 %collective-permute-start.3 = (bf16[272,128]{1,0:T(8,128)(2,1)S(1)}, bf16[272,128]{1,0:T(8,128)(2,1)S(1)}, u32[]{:S(2)}, u32[]{:S(2)}) collective-permute-start(bf16[272,128]{1,0:T(8,128)(2,1)S(1)} %constant_dynamic-slice_fusion.2), channel_id=1, source_target_pairs={{0,2},{1,3},{2,0},{3,1},{4,6},{5,7},{6,4},{7,5},{8,10},{9,11},{10,... | collective-permute-start | bytes 208904 | tf_op jit(solution)/shard_map/ppermute | solution.py:33
  19.5 4.3 %copy-start.9 = (bf16[544,128]{1,0:T(8,128)(2,1)}, bf16[544,128]{1,0:T(8,128)(2,1)S(1)}, u32[]{:S(2)}) copy-start(bf16[544,128]{1,0:T(8,128)(2,1)S(1)} %collective-permute-done.2) | copy-start | bytes 417796
  19.5 6.4 %collective-permute-start.4 = (bf16[1024,128]{1,0:T(8,128)(2,1)S(1)}, bf16[1024,128]{1,0:T(8,128)(2,1)S(1)}, u32[]{:S(2)}, u32[]{:S(2)}) collective-permute-start(bf16[1024,128]{1,0:T(8,128)(2,1)S(1)} %collective-permute-done.1), channel_id=1, source_target_pairs={{0,4},{1,5},{2,6},{3,7},{4,8},{5,9},{6,10},{7,11},{8,12},{9,13},{1... | collective-permute-start | bytes 786440 | tf_op jit(solution)/shard_map/ppermute | solution.py:33
  21.6 4.4 %collective-permute-start.5 = (bf16[1840,128]{1,0:T(8,128)(2,1)S(1)}, bf16[1840,128]{1,0:T(8,128)(2,1)S(1)}, u32[]{:S(2)}, u32[]{:S(2)}) collective-permute-start(bf16[1840,128]{1,0:T(8,128)(2,1)S(1)} %pad_maximum_fusion.6), channel_id=1, source_target_pairs={{0,32},{32,0},{64,96},{96,64},{128,160},{160,128},{192,224},{224,1... | collective-permute-start | bytes 1413128 | tf_op jit(solution)/shard_map/ppermute | solution.py:45
  23.9 3.0 %copy-start.10 = (bf16[544,128]{1,0:T(8,128)(2,1)S(1)}, bf16[544,128]{1,0:T(8,128)(2,1)}, u32[]{:S(2)}) copy-start(bf16[544,128]{1,0:T(8,128)(2,1)} %copy-done.9) | copy-start | bytes 417796
  23.9 3.0 %copy-start.13 = (bf16[544,128]{1,0:T(8,128)(2,1)S(1)}, bf16[544,128]{1,0:T(8,128)(2,1)}, u32[]{:S(2)}) copy-start(bf16[544,128]{1,0:T(8,128)(2,1)} %get-tuple-element.36) | copy-start | bytes 417796
  26.1 20.8 %copy-start.1 = (bf16[3072,128]{1,0:T(8,128)(2,1)}, bf16[3072,128]{1,0:T(8,128)(2,1)S(1)}, u32[]{:S(2)}) copy-start(bf16[3072,128]{1,0:T(8,128)(2,1)S(1)} %pad_maximum_fusion.2.refs_1_) | copy-start | bytes 2359300
  26.2 18.8 %collective-permute-start.8 = (bf16[3072,128]{1,0:T(8,128)(2,1)S(1)}, bf16[3072,128]{1,0:T(8,128)(2,1)}, u32[]{:S(2)}, u32[]{:S(2)}) collective-permute-start(bf16[3072,128]{1,0:T(8,128)(2,1)S(1)} %pad_maximum_fusion.2.refs_1_), channel_id=1, source_target_pairs={{0,1},{1,2},{2,3},{3,0},{4,5},{5,6},{6,7},{7,4},{8,9},{9,10},{10,1... | collective-permute-start | bytes 2359304 | tf_op jit(solution)/shard_map/ppermute | solution.py:33
  27.0 21.4 %copy-start.2 = (bf16[2176,128]{1,0:T(8,128)(2,1)}, bf16[2176,128]{1,0:T(8,128)(2,1)S(1)}, u32[]{:S(2)}) copy-start(bf16[2176,128]{1,0:T(8,128)(2,1)S(1)} %pad_maximum_fusion.4.refs_0_) | copy-start | bytes 1671172
  27.0 17.9 %collective-permute-start.7 = (bf16[2176,128]{1,0:T(8,128)(2,1)S(1)}, bf16[2176,128]{1,0:T(8,128)(2,1)}, u32[]{:S(2)}, u32[]{:S(2)}) collective-permute-start(bf16[2176,128]{1,0:T(8,128)(2,1)S(1)} %pad_maximum_fusion.4.refs_0_), channel_id=1, source_target_pairs={{0,4},{1,5},{2,6},{3,7},{4,8},{5,9},{6,10},{7,11},{8,12},{9,13},{1... | collective-permute-start | bytes 1671176 | tf_op jit(solution)/shard_map/ppermute | solution.py:33
  29.6 15.3 %collective-permute-start.10 = (bf16[1024,128]{1,0:T(8,128)(2,1)S(1)}, bf16[1024,128]{1,0:T(8,128)(2,1)}, u32[]{:S(2)}, u32[]{:S(2)}) collective-permute-start(bf16[1024,128]{1,0:T(8,128)(2,1)S(1)} %collective-permute-done.4), channel_id=1, source_target_pairs={{0,32},{32,0},{64,96},{96,64},{128,160},{160,128},{192,224},{224,1... | collective-permute-start | bytes 786440 | tf_op jit(solution)/shard_map/ppermute | solution.py:45
  29.6 15.3 %collective-permute-start.6 = (bf16[1024,128]{1,0:T(8,128)(2,1)S(1)}, bf16[1024,128]{1,0:T(8,128)(2,1)S(1)}, u32[]{:S(2)}, u32[]{:S(2)}) collective-permute-start(bf16[1024,128]{1,0:T(8,128)(2,1)S(1)} %collective-permute-done.4), channel_id=1, source_target_pairs={{0,4},{1,5},{2,6},{3,7},{4,8},{5,9},{6,10},{7,11},{8,12},{9,13},{1... | collective-permute-start | bytes 786440 | tf_op jit(solution)/shard_map/ppermute | solution.py:33
  32.1 12.8 %collective-permute-start.9 = (bf16[512,128]{1,0:T(8,128)(2,1)S(1)}, bf16[512,128]{1,0:T(8,128)(2,1)S(1)}, u32[]{:S(2)}, u32[]{:S(2)}) collective-permute-start(bf16[512,128]{1,0:T(8,128)(2,1)S(1)} %constant_dynamic-slice_fusion.1), channel_id=1, source_target_pairs={{0,8},{1,9},{2,10},{3,11},{4,12},{5,13},{6,14},{7,15},{8,16},{9,17... | collective-permute-start | bytes 393224 | tf_op jit(solution)/shard_map/ppermute | solution.py:33
  47.0 14.7 %collective-permute-start.12 = (bf16[3584,128]{1,0:T(8,128)(2,1)S(1)}, bf16[3584,128]{1,0:T(8,128)(2,1)S(1)}, u32[]{:S(2)}, u32[]{:S(2)}) collective-permute-start(bf16[3584,128]{1,0:T(8,128)(2,1)S(1)} %pad_maximum_fusion.1), channel_id=1, source_target_pairs={{0,1},{1,2},{2,3},{3,0},{4,5},{5,6},{6,7},{7,4},{8,9},{9,10},{10,1... | collective-permute-start | bytes 2752520 | tf_op jit(solution)/shard_map/ppermute | solution.py:33
  48.3 9.9 %collective-permute-start.14 = (bf16[3072,128]{1,0:T(8,128)(2,1)}, bf16[3072,128]{1,0:T(8,128)(2,1)S(1)}, u32[]{:S(2)}, u32[]{:S(2)}) collective-permute-start(bf16[3072,128]{1,0:T(8,128)(2,1)} %collective-permute-done.8.refs_10_), channel_id=1, source_target_pairs={{0,32},{32,0},{64,96},{96,64},{128,160},{160,128},{192,224},{224,1... | collective-permute-start | bytes 2359304 | tf_op jit(solution)/shard_map/ppermute | solution.py:45
  48.3 9.8 %collective-permute-start.11 = (bf16[2176,128]{1,0:T(8,128)(2,1)}, bf16[2176,128]{1,0:T(8,128)(2,1)}, u32[]{:S(2)}, u32[]{:S(2)}) collective-permute-start(bf16[2176,128]{1,0:T(8,128)(2,1)} %collective-permute-done.7.refs_2_), channel_id=1, source_target_pairs={{0,4},{1,5},{2,6},{3,7},{4,8},{5,9},{6,10},{7,11},{8,12},{9,13},{1... | collective-permute-start | bytes 1671176 | tf_op jit(solution)/shard_map/ppermute | solution.py:33
  48.4 2.8 %collective-permute-start.13 = (bf16[1536,128]{1,0:T(8,128)(2,1)S(1)}, bf16[1536,128]{1,0:T(8,128)(2,1)S(1)}, u32[]{:S(2)}, u32[]{:S(2)}) collective-permute-start(bf16[1536,128]{1,0:T(8,128)(2,1)S(1)} %pad_maximum_fusion.7), channel_id=1, source_target_pairs={{0,32},{32,0},{64,96},{96,64},{128,160},{160,128},{192,224},{224,1... | collective-permute-start | bytes 1179656 | tf_op jit(solution)/shard_map/ppermute | solution.py:45
  58.2 3.5 %copy-start.8 = (bf16[3072,128]{1,0:T(8,128)(2,1)}, bf16[3072,128]{1,0:T(8,128)(2,1)S(1)}, u32[]{:S(2)}) copy-start(bf16[3072,128]{1,0:T(8,128)(2,1)S(1)} %collective-permute-done.14.refs_11_) | copy-start | bytes 2359300
  61.6 1.9 %copy-start.3 = (bf16[3584,128]{1,0:T(8,128)(2,1)}, bf16[3584,128]{1,0:T(8,128)(2,1)S(1)}, u32[]{:S(2)}) copy-start(bf16[3584,128]{1,0:T(8,128)(2,1)S(1)} %collective-permute-done.12.refs_14_) | copy-start | bytes 2752516
  61.8 16.4 %collective-permute-start.16 = (bf16[4096,128]{1,0:T(8,128)(2,1)S(1)}, bf16[4096,128]{1,0:T(8,128)(2,1)}, u32[]{:S(2)}, u32[]{:S(2)}) collective-permute-start(bf16[4096,128]{1,0:T(8,128)(2,1)S(1)} %pad_maximum_fusion), channel_id=1, source_target_pairs={{0,1},{1,2},{2,3},{3,0},{4,5},{5,6},{6,7},{7,4},{8,9},{9,10},{10,1... | collective-permute-start | bytes 3145736 | tf_op jit(solution)/shard_map/ppermute | solution.py:33
  62.1 10.3 %collective-permute-start.18 = (bf16[3584,128]{1,0:T(8,128)(2,1)S(1)}, bf16[3584,128]{1,0:T(8,128)(2,1)S(1)}, u32[]{:S(2)}, u32[]{:S(2)}) collective-permute-start(bf16[3584,128]{1,0:T(8,128)(2,1)S(1)} %collective-permute-done.12.refs_14_), channel_id=1, source_target_pairs={{0,32},{32,0},{64,96},{96,64},{128,160},{160,128},{192,224},{224,1... | collective-permute-start | bytes 2752520 | tf_op jit(solution)/shard_map/ppermute | solution.py:45
  62.1 3.5 %collective-permute-start.17 = (bf16[2176,128]{1,0:T(8,128)(2,1)}, bf16[2176,128]{1,0:T(8,128)(2,1)S(1)}, u32[]{:S(2)}, u32[]{:S(2)}) collective-permute-start(bf16[2176,128]{1,0:T(8,128)(2,1)} %collective-permute-done.7.refs_2_), channel_id=1, source_target_pairs={{0,32},{32,0},{64,96},{96,64},{128,160},{160,128},{192,224},{224,1... | collective-permute-start | bytes 1671176 | tf_op jit(solution)/shard_map/ppermute | solution.py:45
  62.6 9.7 %collective-permute-start.15 = (bf16[2176,128]{1,0:T(8,128)(2,1)}, bf16[2176,128]{1,0:T(8,128)(2,1)S(1)}, u32[]{:S(2)}, u32[]{:S(2)}) collective-permute-start(bf16[2176,128]{1,0:T(8,128)(2,1)} %collective-permute-done.11.refs_4_), channel_id=1, source_target_pairs={{0,4},{1,5},{2,6},{3,7},{4,8},{5,9},{6,10},{7,11},{8,12},{9,13},{1... | collective-permute-start | bytes 1671176 | tf_op jit(solution)/shard_map/ppermute | solution.py:33
  65.6 13.0 %copy-start.11 = (bf16[2176,128]{1,0:T(8,128)(2,1)}, bf16[2176,128]{1,0:T(8,128)(2,1)S(1)}, u32[]{:S(2)}) copy-start(bf16[2176,128]{1,0:T(8,128)(2,1)S(1)} %collective-permute-done.17.refs_3_) | copy-start | bytes 1671172
  72.4 19.4 %copy-start.4 = (bf16[2176,128]{1,0:T(8,128)(2,1)}, bf16[2176,128]{1,0:T(8,128)(2,1)S(1)}, u32[]{:S(2)}) copy-start(bf16[2176,128]{1,0:T(8,128)(2,1)S(1)} %collective-permute-done.15.refs_6_) | copy-start | bytes 1671172
  72.4 5.8 %copy-start.7 = (bf16[3584,128]{1,0:T(8,128)(2,1)}, bf16[3584,128]{1,0:T(8,128)(2,1)S(1)}, u32[]{:S(2)}) copy-start(bf16[3584,128]{1,0:T(8,128)(2,1)S(1)} %collective-permute-done.18.refs_15_) | copy-start | bytes 2752516
  78.1 10.7 %collective-permute-start.23 = (bf16[4096,128]{1,0:T(8,128)(2,1)}, bf16[4096,128]{1,0:T(8,128)(2,1)S(1)}, u32[]{:S(2)}, u32[]{:S(2)}) collective-permute-start(bf16[4096,128]{1,0:T(8,128)(2,1)} %collective-permute-done.16.refs_16_), channel_id=1, source_target_pairs={{0,32},{32,0},{64,96},{96,64},{128,160},{160,128},{192,224},{224,1... | collective-permute-start | bytes 3145736 | tf_op jit(solution)/shard_map/ppermute | solution.py:45
  78.1 4.2 %collective-permute-start.21 = (bf16[2176,128]{1,0:T(8,128)(2,1)}, bf16[2176,128]{1,0:T(8,128)(2,1)}, u32[]{:S(2)}, u32[]{:S(2)}) collective-permute-start(bf16[2176,128]{1,0:T(8,128)(2,1)} %collective-permute-done.11.refs_4_), channel_id=1, source_target_pairs={{0,32},{32,0},{64,96},{96,64},{128,160},{160,128},{192,224},{224,1... | collective-permute-start | bytes 1671176 | tf_op jit(solution)/shard_map/ppermute | solution.py:45
  78.6 10.2 %collective-permute-start.22 = (bf16[2176,128]{1,0:T(8,128)(2,1)S(1)}, bf16[2176,128]{1,0:T(8,128)(2,1)}, u32[]{:S(2)}, u32[]{:S(2)}) collective-permute-start(bf16[2176,128]{1,0:T(8,128)(2,1)S(1)} %collective-permute-done.15.refs_6_), channel_id=1, source_target_pairs={{0,32},{32,0},{64,96},{96,64},{128,160},{160,128},{192,224},{224,1... | collective-permute-start | bytes 1671176 | tf_op jit(solution)/shard_map/ppermute | solution.py:45
  79.8 9.1 %collective-permute-start.20 = (bf16[1536,128]{1,0:T(8,128)(2,1)S(1)}, bf16[1536,128]{1,0:T(8,128)(2,1)S(1)}, u32[]{:S(2)}, u32[]{:S(2)}) collective-permute-start(bf16[1536,128]{1,0:T(8,128)(2,1)S(1)} %slice.43), channel_id=1, source_target_pairs={{0,1},{1,2},{2,3},{3,0},{4,5},{5,6},{6,7},{7,4},{8,9},{9,10},{10,1... | collective-permute-start | bytes 1179656 | tf_op jit(solution)/shard_map/ppermute | solution.py:33
  79.9 6.6 %collective-permute-start.19 = (bf16[1088,128]{1,0:T(8,128)(2,1)S(1)}, bf16[1088,128]{1,0:T(8,128)(2,1)S(1)}, u32[]{:S(2)}, u32[]{:S(2)}) collective-permute-start(bf16[1088,128]{1,0:T(8,128)(2,1)S(1)} %constant_dynamic-slice_fusion), channel_id=1, source_target_pairs={{0,4},{1,5},{2,6},{3,7},{4,8},{5,9},{6,10},{7,11},{8,12},{9,13},{1... | collective-permute-start | bytes 835592 | tf_op jit(solution)/shard_map/ppermute | solution.py:33
  86.5 5.3 %copy-start.14 = (bf16[1088,128]{1,0:T(8,128)(2,1)}, bf16[1088,128]{1,0:T(8,128)(2,1)S(1)}, u32[]{:S(2)}) copy-start(bf16[1088,128]{1,0:T(8,128)(2,1)S(1)} %collective-permute-done.19.refs_8_) | copy-start | bytes 835588
  88.8 3.0 %copy-start.12 = (bf16[1536,128]{1,0:T(8,128)(2,1)}, bf16[1536,128]{1,0:T(8,128)(2,1)S(1)}, u32[]{:S(2)}) copy-start(bf16[1536,128]{1,0:T(8,128)(2,1)S(1)} %collective-permute-done.20.refs_18_) | copy-start | bytes 1179652
  88.8 3.0 %copy-start.6 = (bf16[4096,128]{1,0:T(8,128)(2,1)}, bf16[4096,128]{1,0:T(8,128)(2,1)S(1)}, u32[]{:S(2)}) copy-start(bf16[4096,128]{1,0:T(8,128)(2,1)S(1)} %collective-permute-done.23.refs_17_) | copy-start | bytes 3145732
  88.8 2.9 %collective-permute-start.25 = (bf16[1536,128]{1,0:T(8,128)(2,1)S(1)}, bf16[1536,128]{1,0:T(8,128)(2,1)}, u32[]{:S(2)}, u32[]{:S(2)}) collective-permute-start(bf16[1536,128]{1,0:T(8,128)(2,1)S(1)} %collective-permute-done.20.refs_18_), channel_id=1, source_target_pairs={{0,32},{32,0},{64,96},{96,64},{128,160},{160,128},{192,224},{224,1... | collective-permute-start | bytes 1179656 | tf_op jit(solution)/shard_map/ppermute | solution.py:45
  88.9 2.1 %collective-permute-start.24 = (bf16[1088,128]{1,0:T(8,128)(2,1)S(1)}, bf16[1088,128]{1,0:T(8,128)(2,1)S(1)}, u32[]{:S(2)}, u32[]{:S(2)}) collective-permute-start(bf16[1088,128]{1,0:T(8,128)(2,1)S(1)} %collective-permute-done.19.refs_8_), channel_id=1, source_target_pairs={{0,32},{32,0},{64,96},{96,64},{128,160},{160,128},{192,224},{224,1... | collective-permute-start | bytes 835592 | tf_op jit(solution)/shard_map/ppermute | solution.py:45
  91.1 0.7 copy-start.15
  112.5 5.5 %collective-permute-start.26 = (f32[3,64,128]{2,1,0:T(8,128)}, f32[3,64,128]{2,1,0:T(8,128)S(1)}, u32[]{:S(2)}, u32[]{:S(2)}) collective-permute-start(f32[3,64,128]{2,1,0:T(8,128)} %shard_map.83), channel_id=1, source_target_pairs={{224,0},{0,32},{32,64},{64,96},{96,128},{128,160},{160,192},{192,2... | collective-permute-start | bytes 294920 | tf_op jit(solution)/shard_map/ppermute | solution.py:342
